TPU v7x, 128 devices: a whole 4x4x4 slice. The times are simulated.
128 devices in a mesh: row: 16 (over x, z), col: 8 (over y, core).
Axes of the slice: x: 4, y: 4, z: 4, core: 2. Of those that a mesh axis runs over, the one named last changes fastest.
Arguments:
- partials: float32 [8, 8, 16, 1024, 128], P('col', None, 'row'), may hold values from -5 to 5
- panel: float32 [8, 16, 1024, 2, 1024], P(None, 'row', None, None, 'col'), may hold values from -0.1875 to 0.1875
- inverse: float32 [2, 1024, 1024], P(None, 'col'), as said below
- rhs_blocks: float32 [2, 1024, 128], replicated, may hold values from -6 to 6
Outputs:
- new_partials: float32 [8, 8, 16, 1024, 128], P('col', None, 'row')
- solved: float32 [2, 1024, 128], P(None, 'col')
Inputs may be any that keep to these rules, and one draw needn't show every extreme that they name: `inverse`: each of the two blocks is lower triangular with a positive diagonal.
All inputs are finite; a program needn't handle non-finite values.
Results may differ from a plain program's by a relative error of at most 0.0001.
Values sent between devices are 32-bit elements; how exact they have to be, the bound alone decides.
No kernel may reach another device: no remote copies, remote signals or barrier semaphores. Data moves between devices by JAX's collectives and lax.ppermute only.
A program may use at most 128 MiB of HBM per device.

v0:
```python
import jax
import jax.numpy as jnp
from jax import lax
from jax.sharding import PartitionSpec as P


def from_root(value, axis, source):
    kept = jnp.where(lax.axis_index(axis) == source, value, 0).astype(value.dtype)
    return lax.psum(kept, axis)


def spread(block, root):
    return from_root(block, "row", root)


def solve_block(inverse_rows, right, summed):
    return jnp.dot(
        inverse_rows,
        right - summed,
        precision=lax.Precision.HIGHEST,
        preferred_element_type=jnp.float32,
    )


def per_device(partials, panel, inverse, rhs_blocks):
    row_id = lax.axis_index("row")
    nrow = lax.axis_size("row")
    held = partials[0, :, 0]
    tiles = panel[:, 0]
    count = held.shape[0]
    order = jnp.arange(count, dtype=jnp.int32) * nrow + row_id
    outcome = []
    for k in range(2):
        summed = lax.psum(held[0], "col")
        block = spread(solve_block(inverse[k], rhs_blocks[k], summed), k)
        update = jnp.einsum(
            "lnj,jq->lnq",
            tiles[:, :, k, :],
            block,
            precision=lax.Precision.HIGHEST,
            preferred_element_type=jnp.float32,
        )
        held = held + jnp.where((order > k)[:, None, None], update, jnp.float32(0.0))
        outcome.append(block)
    return (held[None, :, None], jnp.stack(outcome))


def solution(mesh):
    return jax.shard_map(
        per_device,
        mesh=mesh,
        in_specs=(
            P("col", None, "row", None, None),
            P(None, "row", None, None, "col"),
            P(None, "col", None),
            P(),
        ),
        out_specs=(P("col", None, "row", None, None), P(None, "col", None)),
        check_vma=False,
    )
```

profile of v0, /device:TPU:1, one launch (start us, length us, event | category | flops | bytes accessed | tf_op | source)
XLA Modules:
  0.0 333.6 jit_solution(9860619450769688140)
XLA Ops:
  7.2 0.0 all-reduce.5.cloned.1.call-start
  7.2 1.9 slice_bitcast_fusion.9
  9.1 0.0 all-reduce.5.cloned.1.call-update
  9.1 0.0 all-reduce.7.cloned.1.call-start
  9.2 5.3 %copy.6 = f32[1,8,1,1024,128]{3,4,1,2,0:T(8,128)} copy(f32[1,8,1,1024,128]{4,3,2,1,0:T(8,128)} %param.4) | data formatting | bytes 8388608 | tf_op args[0]
  14.5 0.0 copy-start.1
  14.5 0.0 copy-start.2
  14.5 7.7 %copy.13 = f32[8,1,1024,2,128]{4,2,0,3,1:T(8,128)} copy(f32[8,1,1024,2,128]{4,3,2,1,0:T(2,128)} %param.5) | data formatting | bytes 16777216 | tf_op args[1]
  22.2 50.1 %all-reduce.5.cloned.1.call-done = f32[1024,128]{1,0:T(8,128)} async-done(((f32[1024,128]{1,0:T(8,128)}), f32[1024,128]{1,0:T(8,128)}) %all-reduce.5.cloned.1.call-update) | async-done | bytes 524304 | tf_op jit(solution)/shard_map/psum | solution.py:34
  72.3 0.0 copy-done.1
  72.3 0.0 copy-done.2
  72.3 2.7 fusion.4
  75.0 0.0 all-reduce.7.cloned.1.call-update
  75.0 0.0 all-reduce.9.cloned.1.call-start
  75.1 82.0 %all-reduce.7.cloned.1.call-done = f32[128,128]{0,1:T(8,128)} async-done(((f32[128,128]{0,1:T(8,128)}), f32[128,128]{0,1:T(8,128)}) %all-reduce.7.cloned.1.call-update) | async-done | bytes 65552 | tf_op jit(solution)/shard_map/psum | solution.py:9
  157.0 7.4 %bitcast_add_fusion.1 = f32[8,1024,128]{1,2,0:T(8,128)S(1)} fusion(f32[1,8,1,1024,128]{3,4,1,2,0:T(8,128)} %copy.6, f32[8,1024,2,128]{3,1,0,2:T(8,128)} %bitcast.51, pred[8]{0:T(512)(128)(4,1)S(1)} %fusion.13, f32[128,128]{0,1:T(8,128)} %all-reduce.7.cloned.1.call-done), kind=kOutput, calls=%fused_computation.7 | convolution fusion | flops 1612709888 | bytes 12648456 | tf_op jit(solution)/shard_map/lnj,jq->lnq/dot_general | solution.py:36
  164.4 0.0 copy-start
  164.5 2.0 copy-done
  166.5 0.9 slice_bitcast_fusion.8
  167.3 0.0 all-reduce.9.cloned.1.call-update
  167.3 0.0 all-reduce.11.cloned.1.call-start
  167.4 0.0 slice-done
  167.4 0.2 copy.11
  167.6 59.4 %all-reduce.9.cloned.1.call-done = f32[1024,128]{0,1:T(8,128)} async-done(((f32[1024,128]{0,1:T(8,128)}), f32[1024,128]{0,1:T(8,128)}) %all-reduce.9.cloned.1.call-update) | async-done | bytes 524304 | tf_op jit(solution)/shard_map/psum | solution.py:34
  227.0 2.3 fusion.3
  229.3 0.0 all-reduce.11.cloned.1.call-update
  229.3 82.3 %all-reduce.11.cloned.1.call-done = f32[128,128]{0,1:T(8,128)} async-done(((f32[128,128]{0,1:T(8,128)}), f32[128,128]{0,1:T(8,128)}) %all-reduce.11.cloned.1.call-update) | async-done | bytes 65552 | tf_op jit(solution)/shard_map/psum | solution.py:9
  311.6 9.3 %fusion.2 = f32[1,8,1,1024,128]{3,4,1,2,0:T(8,128)} fusion(f32[8,1024,128]{1,2,0:T(8,128)} %copy-done, f32[8,1024,2,128]{3,1,0,2:T(8,128)} %bitcast.52, pred[8]{0:T(512)(128)(4,1)S(1)} %fusion.12, f32[128,128]{0,1:T(8,128)} %all-reduce.11.cloned.1.call-done), kind=kOutput, calls=%fused_computation.6 | convolution fusion | flops 1612709888 | bytes 12648456 | tf_op jit(solution)/shard_map/lnj,jq->lnq/dot_general | solution.py:36
  320.9 5.3 %copy.9 = f32[1,8,1,1024,128]{4,3,2,1,0:T(8,128)} copy(f32[1,8,1,1024,128]{3,4,1,2,0:T(8,128)} %fusion.2) | data formatting | bytes 8388608
  326.3 0.0 copy-done.3
  326.3 0.0 copy-done.4
  326.3 0.8 copy.10
  (6 shorter events, 0.0 us)
Async XLA Ops:
  7.2 65.1 %all-reduce.5.cloned.1.call-start = ((), (), s32[]{:S(2)}) async-start(), calls=%async_computation | async-start | bytes 1048576 | tf_op jit(solution)/shard_map/psum | solution.py:34
  9.1 147.9 %all-reduce.7.cloned.1.call-start = ((), (), s32[]{:S(2)}) async-start(), calls=%async_computation.1 | async-start | bytes 131072 | tf_op jit(solution)/shard_map/psum | solution.py:9
  14.5 57.8 %copy-start.1 = (f32[2,1024,128]{2,1,0:T(8,128)S(1)}, f32[2,1024,128]{2,1,0:T(8,128)}, u32[]{:S(2)}) copy-start(f32[2,1024,128]{2,1,0:T(8,128)} %param.7) | copy-start | bytes 3145732
  14.5 57.8 %copy-start.2 = (f32[2,128,1024]{2,1,0:T(8,128)S(1)}, f32[2,128,1024]{2,1,0:T(8,128)}, u32[]{:S(2)}) copy-start(f32[2,128,1024]{2,1,0:T(8,128)} %param.6) | copy-start | bytes 3145732
  75.0 152.0 %all-reduce.9.cloned.1.call-start = ((), (), s32[]{:S(2)}) async-start(), calls=%async_computation.2 | async-start | bytes 1048576 | tf_op jit(solution)/shard_map/psum | solution.py:34
  157.0 10.4 %slice-start = ((f32[2,1024,128]{2,1,0:T(8,128)}), f32[1,1024,128]{2,1,0:T(8,128)S(1)}, s32[]{:S(2)}) async-start(f32[2,1024,128]{2,1,0:T(8,128)} %param.7), calls=%async_computation.4 | async-start | bytes 1048576 | tf_op jit(solution)/shard_map/slice | solution.py:35
  164.4 2.0 copy-start
  167.3 144.3 %all-reduce.11.cloned.1.call-start = ((), (), s32[]{:S(2)}) async-start(), calls=%async_computation.3 | async-start | bytes 131072 | tf_op jit(solution)/shard_map/psum | solution.py:9
  320.9 5.3 %copy-start.3 = (f32[128,128]{0,1:T(8,128)S(1)}, f32[128,128]{0,1:T(8,128)}, u32[]{:S(2)}) copy-start(f32[128,128]{0,1:T(8,128)} %all-reduce.7.cloned.1.call-done) | copy-start | bytes 196612
  320.9 5.3 %copy-start.4 = (f32[128,128]{0,1:T(8,128)S(1)}, f32[128,128]{0,1:T(8,128)}, u32[]{:S(2)}) copy-start(f32[128,128]{0,1:T(8,128)} %all-reduce.11.cloned.1.call-done) | copy-start | bytes 196612
Sparse Core Ops, SparseCore 0:
  10.3 61.9 all-reduce.4
  76.4 80.5 all-reduce.6
  167.5 59.5 all-reduce.8
  231.0 80.5 all-reduce.10
where the time goes:
time: 335 us; the launch traced here: 334 us
  waiting for transfers between devices  274 us (82%)
  local copies, waits for them, and re-layouts  24.1 us (7%)
  matrix products  21.6 us (6%)
  between operations  13.8 us (4%)
    psum x2, waiting for transfers between devices, from_root(): return lax.psum(kept, axis)  164 us
    psum x2, waiting for transfers between devices, per_device(): summed = lax.psum(held[0], 'col')  110 us
    unnamed x15, local copies, waits for them, and re-layouts  21.3 us
    dot_general x2, matrix products, per_device(): jnp.einsum('lnj,jq->lnq', tiles[:, :, k, :], block, precision=lax.Precisi...  16.7 us
  transfers between devices with their start and end apart: 4, of which 4 were waited for; matrix products, arithmetic and copies ran while one was open for 4% of the time, Pallas kernels for 0%

commit v1 on v0

v1 whole, which is shorter than its diff:
```python
import functools

import jax
import jax.numpy as jnp
from jax import lax
from jax.experimental import pallas as pl
from jax.experimental.pallas import tpu as pltpu
from jax.sharding import PartitionSpec as P

F32 = jnp.float32
BF16 = jnp.bfloat16
NY = 4
NZ = 4
NX = 4
W = 128
NB = 1024
VMEM = pl.BlockSpec(memory_space=pltpu.VMEM)
ANY = pl.BlockSpec(memory_space=pl.ANY)


def params(mib=32):
    return pltpu.CompilerParams(vmem_limit_bytes=mib * 2**20)


def in_vmem(x):
    return pltpu.with_memory_space_constraint(x, pltpu.VMEM)


def vm(shape, dtype=F32):
    return pltpu.VMEM(shape, dtype)


def split(x):
    hi = x.astype(BF16)
    return hi, (x - hi.astype(F32)).astype(BF16)


def dot(a, b):
    return jnp.dot(a, b, preferred_element_type=F32)


def dot3(a, b):
    ah, al = split(a)
    bh, bl = split(b)
    n = b.shape[1]
    both = dot(ah, jnp.concatenate([bh, bl], axis=1))
    return both[:, :n] + (both[:, n:] + dot(al, bh))


def position():
    col = lax.axis_index("col")
    return col // 2, col % 2


def pick_kernel(p_ref, send_ref, keep_ref, sem):
    _, h = position()
    one = pltpu.make_async_copy(p_ref.at[0, :, 1 - h], send_ref, sem.at[0])
    two = pltpu.make_async_copy(p_ref.at[0, :, h], keep_ref, sem.at[1])
    one.start()
    two.start()
    one.wait()
    two.wait()


def pick(partials):
    half = vm((NY, W, W))
    return pl.pallas_call(
        pick_kernel,
        out_shape=(half, half),
        in_specs=[ANY],
        out_specs=(VMEM, VMEM),
        scratch_shapes=[pltpu.SemaphoreType.DMA((2,))],
        compiler_params=params(),
        name="pick",
    )(partials.reshape(8, NY, 2, W, W))


def fan_kernel(keep_ref, got_ref, *outs):
    y, _ = position()
    for s in range(NY):
        at = (y + s) % NY
        outs[s][...] = keep_ref[at] + got_ref[at]


def fan(keep, got):
    return pl.pallas_call(
        fan_kernel,
        out_shape=tuple(vm((W, W)) for _ in range(NY)),
        in_specs=[VMEM, VMEM],
        out_specs=(VMEM,) * NY,
        compiler_params=params(),
        name="fan",
    )(in_vmem(keep), in_vmem(got))


def right_kernel(k, rhs_ref, a, b, c, d, out_ref):
    y, h = position()
    at = pl.multiple_of((2 * y + h) * W, W)
    out_ref[...] = rhs_ref[k, pl.ds(at, W), :] - ((a[...] + b[...]) + (c[...] + d[...]))


def right(k, rhs, pieces):
    return pl.pallas_call(
        functools.partial(right_kernel, k),
        out_shape=vm((W, W)),
        in_specs=[VMEM] * 5,
        out_specs=VMEM,
        compiler_params=params(),
        name="right",
    )(in_vmem(rhs), *[in_vmem(p) for p in pieces])


def lay_kernel(a, b, c, d, out_ref):
    y, _ = position()
    for s, piece in enumerate((a, b, c, d)):
        out_ref[(y + NY - s) % NY] = piece[...]


def lay(pieces):
    return pl.pallas_call(
        lay_kernel,
        out_shape=vm((NY, W, W)),
        in_specs=[VMEM] * NY,
        out_specs=VMEM,
        compiler_params=params(),
        name="lay",
    )(*[in_vmem(p) for p in pieces])


def whole(mine_ref, other_ref, all_ref):
    _, h = position()
    for at in range(NY):
        all_ref[at, h] = mine_ref[at]
        all_ref[at, 1 - h] = other_ref[at]
    return all_ref[...].reshape(NB, W)


def first_kernel(inv_ref, mine_ref, other_ref, ph_ref, pl_ref, part_ref, solved_ref, send_ref, keep_ref, all_ref):
    _, h = position()
    block = dot3(inv_ref[0], whole(mine_ref, other_ref, all_ref))
    solved_ref[...] = block
    bh, bl = split(block)
    both = jnp.concatenate([bh, bl], axis=1)
    for at in range(NY):
        for parity, out_ref in ((1 - h, send_ref), (h, keep_ref)):
            rows = pl.ds(pl.multiple_of((2 * at + parity) * W, W), W)
            prod = dot(ph_ref[0, rows, :W], both)
            out_ref[at] = part_ref[0, rows, :] + (
                prod[:, :W] + (prod[:, W:] + dot(pl_ref[0, rows, :W], bh))
            )


def first(inverse, mine, other, p_hi, p_lo, partials):
    half = vm((NY, W, W))
    return pl.pallas_call(
        first_kernel,
        out_shape=(vm((W, W)), half, half),
        in_specs=[VMEM] * 6,
        out_specs=(VMEM,) * 3,
        scratch_shapes=[pltpu.VMEM((NY, 2, W, W), F32)],
        compiler_params=params(),
        name="first",
    )(*[in_vmem(v) for v in (inverse, mine, other, p_hi, p_lo, partials)])


def second_kernel(inv_ref, mine_ref, other_ref, y0_ref, out_ref, all_ref):
    out_ref[0] = y0_ref[...]
    out_ref[1] = dot3(inv_ref[1], whole(mine_ref, other_ref, all_ref))


def second(inverse, mine, other, y0):
    return pl.pallas_call(
        second_kernel,
        out_shape=vm((2, W, W)),
        in_specs=[VMEM] * 4,
        out_specs=VMEM,
        scratch_shapes=[pltpu.VMEM((NY, 2, W, W), F32)],
        compiler_params=params(),
        name="second",
    )(*[in_vmem(v) for v in (inverse, mine, other, y0)])


def parts_kernel(panel_ref, hi_ref, lo_ref):
    rows = hi_ref.shape[1]
    for k in range(2):
        hi, lo = split(panel_ref[0, pl.ds(k, rows, stride=2), :])
        hi_ref[0, :, k * W : (k + 1) * W] = hi
        lo_ref[0, :, k * W : (k + 1) * W] = lo


def parts(panel):
    out = jax.ShapeDtypeStruct((8, NB, 2 * W), BF16)
    spec = pl.BlockSpec((1, NB, 2 * W), lambda i: (i, 0, 0))
    return pl.pallas_call(
        parts_kernel,
        out_shape=(out, out),
        grid=(8,),
        in_specs=[pl.BlockSpec((1, 2 * NB, W), lambda i: (i, 0, 0))],
        out_specs=(spec, spec),
        compiler_params=params(),
        cost_estimate=pl.CostEstimate(flops=10**7, bytes_accessed=16 * 2**20, transcendentals=0),
        name="parts",
    )(panel.reshape(8, 2 * NB, W))


STEP = 256


def update_kernel(y_ref, ph_ref, pl_ref, part_ref, out_ref, solved_ref, buf, both_ref, sem):
    row = lax.axis_index("row")
    x = row // NZ
    block = jnp.where(x == 0, y_ref[0], y_ref[1] + y_ref[2] + y_ref[3])
    solved_ref[...] = block

    def weights(slot, keep0, keep1):
        y0 = jnp.where(keep0, block[0], 0.0)
        y1 = jnp.where(keep1, block[1], 0.0)
        h, l = split(jnp.concatenate([y0, y1], axis=0))
        both_ref[slot] = jnp.concatenate([h, l], axis=1)

    weights(0, row > 0, row > 1)
    weights(1, row >= 0, row >= 0)
    per = NB // STEP

    def copy(i):
        l, j = i // per, i % per
        rows = pl.ds(pl.multiple_of(j * STEP, STEP), STEP)
        return pltpu.make_async_copy(buf.at[l, rows, :], out_ref.at[l, rows, :], sem.at[i])

    def body(i, _):
        l, j = i // per, i % per
        rows = pl.ds(pl.multiple_of(j * STEP, STEP), STEP)
        w = both_ref[jnp.minimum(l, 1)]
        prod = dot(ph_ref[l, rows, :], w)
        low = dot(pl_ref[l, rows, :], w[:, :W])
        buf[l, rows, :] = part_ref[l, rows, :] + (prod[:, :W] + (prod[:, W:] + low))
        copy(i).start()
        return 0

    lax.fori_loop(0, 8 * per, body, 0)

    def done(i, _):
        copy(i).wait()
        return 0

    lax.fori_loop(0, 8 * per, done, 0)


def update(y, p_hi, p_lo, partials):
    return pl.pallas_call(
        update_kernel,
        out_shape=(jax.ShapeDtypeStruct((8, NB, W), F32), jax.ShapeDtypeStruct((2, W, W), F32)),
        in_specs=[VMEM] * 4,
        out_specs=(ANY, VMEM),
        scratch_shapes=[
            pltpu.VMEM((8, NB, W), F32),
            pltpu.VMEM((2, 2 * W, 2 * W), BF16),
            pltpu.SemaphoreType.DMA((8 * NB // STEP,)),
        ],
        compiler_params=params(),
        name="update",
    )(y, *[in_vmem(v) for v in (p_hi, p_lo, partials)])


def swap(x):
    return lax.ppermute(x, "col", [(i, i ^ 1) for i in range(8)])


def along_y(x, s):
    return lax.ppermute(x, "col", [(i, (i + 2 * s) % 8) for i in range(8)])


def to_next_row(x, s):
    pairs = [(c, 8 + (c + 2 * s) % 8) for c in range(8)]
    return lax.ppermute(x, ("row", "col"), pairs)


def gather(pieces):
    mine = lay(pieces)
    return mine, swap(mine)


def per_device(partials, panel, inverse, rhs):
    partials = partials.reshape(8, NB, W)
    send, keep = pick(partials)
    own, *others = fan(keep, swap(send))
    w0 = right(0, rhs, [own] + [along_y(v, s) for s, v in zip((1, 2, 3), others)])
    p_hi, p_lo = parts(panel)
    mine, other = gather([to_next_row(w0, s) for s in range(4)])
    y0, send, keep = first(inverse, mine, other, p_hi, p_lo, partials)
    own, *others = fan(keep, swap(send))
    w1 = right(1, rhs, [own] + [along_y(v, s) for s, v in zip((1, 2, 3), others)])
    mine, other = gather([w1] + [along_y(w1, s) for s in (1, 2, 3)])
    y = second(inverse, mine, other, y0)
    row = lax.axis_index("row")
    got = [lax.ppermute(y, "row", [(1, z)]) for z in (0, 2, 3)]
    y = jnp.where(row == 1, y, got[0] + got[1] + got[2])
    got = [lax.ppermute(y, "row", [(z, z + NZ * s) for z in range(NZ)]) for s in (1, 2, 3)]
    new, solved = update(jnp.stack([y] + got), p_hi, p_lo, partials)
    return new[None, :, None], solved


def solution(mesh):
    return jax.shard_map(
        per_device,
        mesh=mesh,
        in_specs=(
            P("col", None, "row", None, None),
            P(None, "row", None, None, "col"),
            P(None, "col", None),
            P(),
        ),
        out_specs=(P("col", None, "row", None, None), P(None, "col", None)),
        check_vma=False,
    )
```

time: 335 us -> 90.1 us (0.27)
  waiting for transfers between devices: 274 us -> 26.8 us
  starting transfers between devices: 0.16 us -> 34.2 us
  matrix products: 21.6 us -> 0 us
  between operations: 13.8 us -> 0.89 us
  Pallas kernels: 0 us -> 12.1 us
  local copies, waits for them, and re-layouts: 24.1 us -> 14.7 us
    psum x4 -> x0, waiting for transfers between devices: 274 us -> none  [the longest x2 164 us: from_root(): return lax.psum(kept, axis)]
    ppermute x0 -> x23, starting transfers between devices: none -> 34.2 us  [the longest x9 11.8 us: along_y(): return lax.ppermute(x, 'col', [(i, (i + 2 * s) % 8) for i in range(8)])]
    ppermute x0 -> x23, waiting for transfers between devices: none -> 26.8 us  [the longest x9 9.92 us: along_y(): return lax.ppermute(x, 'col', [(i, (i + 2 * s) % 8) for i in range(8)])]
    dot_general x4 -> x0, matrix products: 21.6 us -> none  [the longest x2 16.7 us: per_device(): jnp.einsum('lnj,jq->lnq', tiles[:, :, k, :], block, precision=lax.Precisi...]
    pallas_call x0 -> x11, Pallas kernels: none -> 12.1 us  [the longest x1 8.95 us: update(): pl.pallas_call(update_kernel, out_shape=(jax.ShapeDtypeStruct((8, NB, W),...]
    unnamed x15 -> x20, local copies, waits for them, and re-layouts: 21.3 us -> 14.7 us
  transfers between devices with their start and end apart: 4 -> 23, of which waited for: 4 -> 15; matrix products, arithmetic and copies ran while one was open for 4% -> 0% of each run, Pallas kernels for 0% -> 2%
where the time goes in v1:
time: 90.1 us; the launch traced here: 88.9 us
  starting transfers between devices  34.2 us (38%)
  waiting for transfers between devices  26.8 us (30%)
  local copies, waits for them, and re-layouts  14.7 us (16%)
  Pallas kernels  12.1 us (13%)
    unnamed x20, local copies, waits for them, and re-layouts  14.7 us
    ppermute x9, starting transfers between devices, along_y(): return lax.ppermute(x, 'col', [(i, (i + 2 * s) % 8) for i in range(8)])  11.8 us
    ppermute x9, waiting for transfers between devices, along_y(): return lax.ppermute(x, 'col', [(i, (i + 2 * s) % 8) for i in range(8)])  9.92 us
    ppermute x4, starting transfers between devices, to_next_row(): return lax.ppermute(x, ('row', 'col'), pairs)  9.12 us
    pallas_call x1, Pallas kernels, update(): pl.pallas_call(update_kernel, out_shape=(jax.ShapeDtypeStruct((8, NB, W),...  8.95 us
    ppermute x3, waiting for transfers between devices, per_device(): got = [lax.ppermute(y, 'row', [(1, z)]) for z in (0, 2, 3)]  7.26 us
    ppermute x4, starting transfers between devices, swap(): return lax.ppermute(x, 'col', [(i, i ^ 1) for i in range(8)])  6.81 us
    ppermute x3, waiting for transfers between devices, per_device(): lax.ppermute(y, 'row', [(z, z + NZ * s) for z in range(NZ)])  3.94 us
  transfers between devices with their start and end apart: 23, of which 15 were waited for; matrix products, arithmetic and copies ran while one was open for 0% of the time, Pallas kernels for 2%

profile of v1, /device:TPU:1, one launch (start us, length us, event | category | flops | bytes accessed | tf_op | source)
XLA Modules:
  0.0 88.9 jit_solution(50494059564823260)
XLA Ops:
  0.6 2.2 %copy-done = f32[1,8,1,1024,128]{4,3,2,1,0:T(8,128)S(1)} copy-done((f32[1,8,1,1024,128]{4,3,2,1,0:T(8,128)S(1)}, f32[1,8,1,1024,128]{4,3,2,1,0:T(8,128)}, u32[]{:S(2)}) %copy-start) | copy-done | bytes 4194328
  2.9 1.5 %collective-permute-start = (f32[4,128,128]{2,1,0:T(8,128)S(1)}, f32[4,128,128]{2,1,0:T(8,128)S(1)}, u32[]{:S(2)}, u32[]{:S(2)}) collective-permute-start(f32[4,128,128]{2,1,0:T(8,128)S(1)} %get-tuple-element.20), channel_id=1, source_target_pairs={{0,1},{1,0},{2,3},{3,2},{4,5},{5,4},{6,7},{7,6},{8,9},{9,8},{10,11... | collective-permute-start | bytes 786440 | tf_op jit(solution)/shard_map/ppermute | solution.py:266
  4.4 1.2 %collective-permute-done.got_ref = f32[4,128,128]{2,1,0:T(8,128)S(1)} collective-permute-done((f32[4,128,128]{2,1,0:T(8,128)S(1)}, f32[4,128,128]{2,1,0:T(8,128)S(1)}, u32[]{:S(2)}, u32[]{:S(2)}) %collective-permute-start) | collective-permute-done | bytes 262176 | tf_op jit(solution)/shard_map/ppermute | solution.py:266
  5.6 1.4 %collective-permute-start.1 = (f32[128,128]{1,0:T(8,128)S(1)}, f32[128,128]{1,0:T(8,128)S(1)}, u32[]{:S(2)}, u32[]{:S(2)}) collective-permute-start(f32[128,128]{1,0:T(8,128)S(1)} %get-tuple-element.22), channel_id=1, source_target_pairs={{0,2},{1,3},{2,4},{3,5},{4,6},{5,7},{6,0},{7,1},{8,10},{9,11},{10,... | collective-permute-start | bytes 196616 | tf_op jit(solution)/shard_map/ppermute | solution.py:270
  7.0 2.6 %collective-permute-start.2 = (f32[128,128]{1,0:T(8,128)S(1)}, f32[128,128]{1,0:T(8,128)S(1)}, u32[]{:S(2)}, u32[]{:S(2)}) collective-permute-start(f32[128,128]{1,0:T(8,128)S(1)} %get-tuple-element.23), channel_id=1, source_target_pairs={{0,4},{1,5},{2,6},{3,7},{4,0},{5,1},{6,2},{7,3},{8,12},{9,13},{10,... | collective-permute-start | bytes 196616 | tf_op jit(solution)/shard_map/ppermute | solution.py:270
  10.7 1.9 %collective-permute-done.2.c = f32[128,128]{1,0:T(8,128)S(1)} collective-permute-done((f32[128,128]{1,0:T(8,128)S(1)}, f32[128,128]{1,0:T(8,128)S(1)}, u32[]{:S(2)}, u32[]{:S(2)}) %collective-permute-start.2) | collective-permute-done | bytes 65568 | tf_op jit(solution)/shard_map/ppermute | solution.py:270
  13.1 5.2 %collective-permute-start.7 = (f32[128,128]{1,0:T(8,128)S(1)}, f32[128,128]{1,0:T(8,128)S(1)}, u32[]{:S(2)}, u32[]{:S(2)}) collective-permute-start(f32[128,128]{1,0:T(8,128)S(1)} %right.2), channel_id=1, source_target_pairs={{0,14},{1,15},{2,8},{3,9},{4,10},{5,11},{6,12},{7,13}} | collective-permute-start | bytes 196616 | tf_op jit(solution)/shard_map/ppermute | solution.py:275
  18.3 1.3 %collective-permute-start.6 = (f32[128,128]{1,0:T(8,128)S(1)}, f32[128,128]{1,0:T(8,128)S(1)}, u32[]{:S(2)}, u32[]{:S(2)}) collective-permute-start(f32[128,128]{1,0:T(8,128)S(1)} %right.2), channel_id=1, source_target_pairs={{0,12},{1,13},{2,14},{3,15},{4,8},{5,9},{6,10},{7,11}} | collective-permute-start | bytes 196616 | tf_op jit(solution)/shard_map/ppermute | solution.py:275
  19.6 1.3 %collective-permute-start.5 = (f32[128,128]{1,0:T(8,128)S(1)}, f32[128,128]{1,0:T(8,128)S(1)}, u32[]{:S(2)}, u32[]{:S(2)}) collective-permute-start(f32[128,128]{1,0:T(8,128)S(1)} %right.2), channel_id=1, source_target_pairs={{0,10},{1,11},{2,12},{3,13},{4,14},{5,15},{6,8},{7,9}} | collective-permute-start | bytes 196616 | tf_op jit(solution)/shard_map/ppermute | solution.py:275
  20.9 1.3 %collective-permute-start.4 = (f32[128,128]{1,0:T(8,128)S(1)}, f32[128,128]{1,0:T(8,128)S(1)}, u32[]{:S(2)}, u32[]{:S(2)}) collective-permute-start(f32[128,128]{1,0:T(8,128)S(1)} %right.2), channel_id=1, source_target_pairs={{0,8},{1,9},{2,10},{3,11},{4,12},{5,13},{6,14},{7,15}} | collective-permute-start | bytes 196616 | tf_op jit(solution)/shard_map/ppermute | solution.py:275
  22.3 1.9 %collective-permute-done.4.a = f32[128,128]{1,0:T(8,128)S(1)} collective-permute-done((f32[128,128]{1,0:T(8,128)S(1)}, f32[128,128]{1,0:T(8,128)S(1)}, u32[]{:S(2)}, u32[]{:S(2)}) %collective-permute-start.4) | collective-permute-done | bytes 65568 | tf_op jit(solution)/shard_map/ppermute | solution.py:275
  24.2 2.4 %collective-permute-start.8 = (f32[4,128,128]{2,1,0:T(8,128)S(1)}, f32[4,128,128]{2,1,0:T(8,128)S(1)}, u32[]{:S(2)}, u32[]{:S(2)}) collective-permute-start(f32[4,128,128]{2,1,0:T(8,128)S(1)} %lay.2.mine_ref), channel_id=1, source_target_pairs={{0,1},{1,0},{2,3},{3,2},{4,5},{5,4},{6,7},{7,6},{8,9},{9,8},{10,11... | collective-permute-start | bytes 786440 | tf_op jit(solution)/shard_map/ppermute | solution.py:266
  26.6 3.4 %copy-done.7 = f32[8,1,1024,2,128]{4,3,2,1,0:T(2,128)S(1)} copy-done((f32[8,1,1024,2,128]{4,3,2,1,0:T(2,128)S(1)}, f32[8,1,1024,2,128]{4,3,2,1,0:T(2,128)}, u32[]{:S(2)}) %copy-start.7) | copy-done | bytes 8388632
  30.0 1.9 %parts.1 = (bf16[8,1024,256]{2,1,0:T(8,128)(2,1)S(1)}, bf16[8,1024,256]{2,1,0:T(8,128)(2,1)S(1)}) custom-call(f32[8,2048,128]{2,1,0:T(8,128)S(1)} %bitcast.13), custom_call_target="tpu_custom_call" | custom-call | flops 10000000 | bytes 16777216 | tf_op jit(solution)/shard_map/parts/pallas_call | solution.py:194
  33.9 1.3 %copy-done.5 = bf16[8,1024,256]{2,1,0:T(8,128)(2,1)} copy-done((bf16[8,1024,256]{2,1,0:T(8,128)(2,1)}, bf16[8,1024,256]{2,1,0:T(8,128)(2,1)S(1)}, u32[]{:S(2)}) %copy-start.5) | copy-done | bytes 4194328
  35.3 1.5 %collective-permute-done.9.got_ref = f32[4,128,128]{2,1,0:T(8,128)S(1)} collective-permute-done((f32[4,128,128]{2,1,0:T(8,128)S(1)}, f32[4,128,128]{2,1,0:T(8,128)S(1)}, u32[]{:S(2)}, u32[]{:S(2)}) %collective-permute-start.9) | collective-permute-done | bytes 262176 | tf_op jit(solution)/shard_map/ppermute | solution.py:266
  37.5 2.0 %collective-permute-start.11 = (f32[128,128]{1,0:T(8,128)S(1)}, f32[128,128]{1,0:T(8,128)S(1)}, u32[]{:S(2)}, u32[]{:S(2)}) collective-permute-start(f32[128,128]{1,0:T(8,128)S(1)} %get-tuple-element.31), channel_id=1, source_target_pairs={{0,4},{1,5},{2,6},{3,7},{4,0},{5,1},{6,2},{7,3},{8,12},{9,13},{10,... | collective-permute-start | bytes 196616 | tf_op jit(solution)/shard_map/ppermute | solution.py:270
  40.3 1.3 %collective-permute-done.10.b = f32[128,128]{1,0:T(8,128)S(1)} collective-permute-done((f32[128,128]{1,0:T(8,128)S(1)}, f32[128,128]{1,0:T(8,128)S(1)}, u32[]{:S(2)}, u32[]{:S(2)}) %collective-permute-start.10) | collective-permute-done | bytes 65568 | tf_op jit(solution)/shard_map/ppermute | solution.py:270
  41.7 1.4 %collective-permute-done.11.c = f32[128,128]{1,0:T(8,128)S(1)} collective-permute-done((f32[128,128]{1,0:T(8,128)S(1)}, f32[128,128]{1,0:T(8,128)S(1)}, u32[]{:S(2)}, u32[]{:S(2)}) %collective-permute-start.11) | collective-permute-done | bytes 65568 | tf_op jit(solution)/shard_map/ppermute | solution.py:270
  43.6 2.4 %collective-permute-start.15 = (f32[128,128]{1,0:T(8,128)S(1)}, f32[128,128]{1,0:T(8,128)S(1)}, u32[]{:S(2)}, u32[]{:S(2)}) collective-permute-start(f32[128,128]{1,0:T(8,128)S(1)} %right.3.a), channel_id=1, source_target_pairs={{0,6},{1,7},{2,0},{3,1},{4,2},{5,3},{6,4},{7,5},{8,14},{9,15},{10,... | collective-permute-start | bytes 196616 | tf_op jit(solution)/shard_map/ppermute | solution.py:270
  47.4 3.3 %collective-permute-done.14.c = f32[128,128]{1,0:T(8,128)S(1)} collective-permute-done((f32[128,128]{1,0:T(8,128)S(1)}, f32[128,128]{1,0:T(8,128)S(1)}, u32[]{:S(2)}, u32[]{:S(2)}) %collective-permute-start.14) | collective-permute-done | bytes 65568 | tf_op jit(solution)/shard_map/ppermute | solution.py:270
  51.1 2.9 %collective-permute-start.16 = (f32[4,128,128]{2,1,0:T(8,128)S(1)}, f32[4,128,128]{2,1,0:T(8,128)S(1)}, u32[]{:S(2)}, u32[]{:S(2)}) collective-permute-start(f32[4,128,128]{2,1,0:T(8,128)S(1)} %lay.3.mine_ref), channel_id=1, source_target_pairs={{0,1},{1,0},{2,3},{3,2},{4,5},{5,4},{6,7},{7,6},{8,9},{9,8},{10,11... | collective-permute-start | bytes 786440 | tf_op jit(solution)/shard_map/ppermute | solution.py:266
  56.8 1.3 %collective-permute-start.17 = (f32[2,128,128]{2,1,0:T(8,128)S(1)}, f32[2,128,128]{2,1,0:T(8,128)S(1)}, u32[]{:S(2)}, u32[]{:S(2)}) collective-permute-start(f32[2,128,128]{2,1,0:T(8,128)S(1)} %second.1), channel_id=1, source_target_pairs={{8,0},{9,1},{10,2},{11,3},{12,4},{13,5},{14,6},{15,7}} | collective-permute-start | bytes 393224 | tf_op jit(solution)/shard_map/ppermute | solution.py:296
  58.2 7.3 %collective-permute-done.17 = f32[2,128,128]{2,1,0:T(8,128)S(1)} collective-permute-done((f32[2,128,128]{2,1,0:T(8,128)S(1)}, f32[2,128,128]{2,1,0:T(8,128)S(1)}, u32[]{:S(2)}, u32[]{:S(2)}) %collective-permute-start.17) | collective-permute-done | bytes 131104 | tf_op jit(solution)/shard_map/ppermute | solution.py:296
  65.5 1.3 %collective-permute-start.22 = (f32[2,128,128]{2,1,0:T(8,128)S(1)}, f32[2,128,128]{2,1,0:T(8,128)S(1)}, u32[]{:S(2)}, u32[]{:S(2)}) collective-permute-start(f32[2,128,128]{2,1,0:T(8,128)S(1)} %add_select_fusion), channel_id=1, source_target_pairs={{0,96},{8,104},{16,112},{24,120},{1,97},{9,105},{17,113},{25,121},... | collective-permute-start | bytes 393224 | tf_op jit(solution)/shard_map/ppermute | solution.py:298
  66.8 1.3 %collective-permute-start.21 = (f32[2,128,128]{2,1,0:T(8,128)S(1)}, f32[2,128,128]{2,1,0:T(8,128)S(1)}, u32[]{:S(2)}, u32[]{:S(2)}) collective-permute-start(f32[2,128,128]{2,1,0:T(8,128)S(1)} %add_select_fusion), channel_id=1, source_target_pairs={{0,64},{8,72},{16,80},{24,88},{1,65},{9,73},{17,81},{25,89},{2,66}... | collective-permute-start | bytes 393224 | tf_op jit(solution)/shard_map/ppermute | solution.py:298
  68.1 1.3 %collective-permute-start.20 = (f32[2,128,128]{2,1,0:T(8,128)S(1)}, f32[2,128,128]{2,1,0:T(8,128)S(1)}, u32[]{:S(2)}, u32[]{:S(2)}) collective-permute-start(f32[2,128,128]{2,1,0:T(8,128)S(1)} %add_select_fusion), channel_id=1, source_target_pairs={{0,32},{8,40},{16,48},{24,56},{1,33},{9,41},{17,49},{25,57},{2,34}... | collective-permute-start | bytes 393224 | tf_op jit(solution)/shard_map/ppermute | solution.py:298
  70.5 2.8 %collective-permute-done.20 = f32[2,128,128]{2,1,0:T(8,128)S(1)} collective-permute-done((f32[2,128,128]{2,1,0:T(8,128)S(1)}, f32[2,128,128]{2,1,0:T(8,128)S(1)}, u32[]{:S(2)}, u32[]{:S(2)}) %collective-permute-start.20) | collective-permute-done | bytes 131104 | tf_op jit(solution)/shard_map/ppermute | solution.py:298
  73.4 2.2 %copy-done.2 = f32[1,8,1,1024,128]{4,3,2,1,0:T(8,128)S(1)} copy-done((f32[1,8,1,1024,128]{4,3,2,1,0:T(8,128)S(1)}, f32[1,8,1,1024,128]{4,3,2,1,0:T(8,128)}, u32[]{:S(2)}) %copy-start.2) | copy-done | bytes 4194328
  75.6 2.2 %copy-done.4 = bf16[8,1024,256]{2,1,0:T(8,128)(2,1)S(1)} copy-done((bf16[8,1024,256]{2,1,0:T(8,128)(2,1)S(1)}, bf16[8,1024,256]{2,1,0:T(8,128)(2,1)}, u32[]{:S(2)}) %copy-start.4) | copy-done | bytes 4194328
  77.7 2.2 %copy-done.6 = bf16[8,1024,256]{2,1,0:T(8,128)(2,1)S(1)} copy-done((bf16[8,1024,256]{2,1,0:T(8,128)(2,1)S(1)}, bf16[8,1024,256]{2,1,0:T(8,128)(2,1)}, u32[]{:S(2)}) %copy-start.6) | copy-done | bytes 4194328
  79.9 8.9 %update.1 = (f32[8,1024,128]{2,1,0:T(8,128)}, f32[2,128,128]{2,1,0:T(8,128)}) custom-call(f32[4,2,128,128]{3,2,1,0:T(8,128)S(1)} %pad_maximum_fusion.y_ref, bf16[8,1024,256]{2,1,0:T(8,128)(2,1)S(1)} %copy-done.4, bf16[8,1024,256]{2,1,0:T(8,128)(2,1)S(1)} %copy-done.6, f32[8,1024,128]{2,1,0:T(8,128)S(1)} %bitcast.12), custom_call_target="tpu_custom_call" | custom-call | tf_op jit(solution)/shard_map/update/pallas_call | solution.py:250
  (47 shorter events, 11.5 us)
Async XLA Ops:
  0.6 2.2 %copy-start = (f32[1,8,1,1024,128]{4,3,2,1,0:T(8,128)S(1)}, f32[1,8,1,1024,128]{4,3,2,1,0:T(8,128)}, u32[]{:S(2)}) copy-start(f32[1,8,1,1024,128]{4,3,2,1,0:T(8,128)} %param.4) | copy-start | bytes 12582916
  2.8 10.2 %copy-start.9 = (f32[2,1024,128]{2,1,0:T(8,128)S(1)}, f32[2,1024,128]{2,1,0:T(8,128)}, u32[]{:S(2)}) copy-start(f32[2,1024,128]{2,1,0:T(8,128)} %rhs_ref.3) | copy-start | bytes 3145732
  2.9 2.7 %collective-permute-start = (f32[4,128,128]{2,1,0:T(8,128)S(1)}, f32[4,128,128]{2,1,0:T(8,128)S(1)}, u32[]{:S(2)}, u32[]{:S(2)}) collective-permute-start(f32[4,128,128]{2,1,0:T(8,128)S(1)} %get-tuple-element.20), channel_id=1, source_target_pairs={{0,1},{1,0},{2,3},{3,2},{4,5},{5,4},{6,7},{7,6},{8,9},{9,8},{10,11... | collective-permute-start | bytes 786440 | tf_op jit(solution)/shard_map/ppermute | solution.py:266
  5.6 5.1 %collective-permute-start.1 = (f32[128,128]{1,0:T(8,128)S(1)}, f32[128,128]{1,0:T(8,128)S(1)}, u32[]{:S(2)}, u32[]{:S(2)}) collective-permute-start(f32[128,128]{1,0:T(8,128)S(1)} %get-tuple-element.22), channel_id=1, source_target_pairs={{0,2},{1,3},{2,4},{3,5},{4,6},{5,7},{6,0},{7,1},{8,10},{9,11},{10,... | collective-permute-start | bytes 196616 | tf_op jit(solution)/shard_map/ppermute | solution.py:270
  7.0 5.6 %collective-permute-start.2 = (f32[128,128]{1,0:T(8,128)S(1)}, f32[128,128]{1,0:T(8,128)S(1)}, u32[]{:S(2)}, u32[]{:S(2)}) collective-permute-start(f32[128,128]{1,0:T(8,128)S(1)} %get-tuple-element.23), channel_id=1, source_target_pairs={{0,4},{1,5},{2,6},{3,7},{4,0},{5,1},{6,2},{7,3},{8,12},{9,13},{10,... | collective-permute-start | bytes 196616 | tf_op jit(solution)/shard_map/ppermute | solution.py:270
  9.7 3.4 %collective-permute-start.3 = (f32[128,128]{1,0:T(8,128)S(1)}, f32[128,128]{1,0:T(8,128)S(1)}, u32[]{:S(2)}, u32[]{:S(2)}) collective-permute-start(f32[128,128]{1,0:T(8,128)S(1)} %get-tuple-element.24), channel_id=1, source_target_pairs={{0,6},{1,7},{2,0},{3,1},{4,2},{5,3},{6,4},{7,5},{8,14},{9,15},{10,... | collective-permute-start | bytes 196616 | tf_op jit(solution)/shard_map/ppermute | solution.py:270
  13.1 9.2 %collective-permute-start.7 = (f32[128,128]{1,0:T(8,128)S(1)}, f32[128,128]{1,0:T(8,128)S(1)}, u32[]{:S(2)}, u32[]{:S(2)}) collective-permute-start(f32[128,128]{1,0:T(8,128)S(1)} %right.2), channel_id=1, source_target_pairs={{0,14},{1,15},{2,8},{3,9},{4,10},{5,11},{6,12},{7,13}} | collective-permute-start | bytes 196616 | tf_op jit(solution)/shard_map/ppermute | solution.py:275
  18.3 3.9 %collective-permute-start.6 = (f32[128,128]{1,0:T(8,128)S(1)}, f32[128,128]{1,0:T(8,128)S(1)}, u32[]{:S(2)}, u32[]{:S(2)}) collective-permute-start(f32[128,128]{1,0:T(8,128)S(1)} %right.2), channel_id=1, source_target_pairs={{0,12},{1,13},{2,14},{3,15},{4,8},{5,9},{6,10},{7,11}} | collective-permute-start | bytes 196616 | tf_op jit(solution)/shard_map/ppermute | solution.py:275
  19.6 2.6 %collective-permute-start.5 = (f32[128,128]{1,0:T(8,128)S(1)}, f32[128,128]{1,0:T(8,128)S(1)}, u32[]{:S(2)}, u32[]{:S(2)}) collective-permute-start(f32[128,128]{1,0:T(8,128)S(1)} %right.2), channel_id=1, source_target_pairs={{0,10},{1,11},{2,12},{3,13},{4,14},{5,15},{6,8},{7,9}} | collective-permute-start | bytes 196616 | tf_op jit(solution)/shard_map/ppermute | solution.py:275
  20.9 3.2 %collective-permute-start.4 = (f32[128,128]{1,0:T(8,128)S(1)}, f32[128,128]{1,0:T(8,128)S(1)}, u32[]{:S(2)}, u32[]{:S(2)}) collective-permute-start(f32[128,128]{1,0:T(8,128)S(1)} %right.2), channel_id=1, source_target_pairs={{0,8},{1,9},{2,10},{3,11},{4,12},{5,13},{6,14},{7,15}} | collective-permute-start | bytes 196616 | tf_op jit(solution)/shard_map/ppermute | solution.py:275
  24.2 7.8 %collective-permute-start.8 = (f32[4,128,128]{2,1,0:T(8,128)S(1)}, f32[4,128,128]{2,1,0:T(8,128)S(1)}, u32[]{:S(2)}, u32[]{:S(2)}) collective-permute-start(f32[4,128,128]{2,1,0:T(8,128)S(1)} %lay.2.mine_ref), channel_id=1, source_target_pairs={{0,1},{1,0},{2,3},{3,2},{4,5},{5,4},{6,7},{7,6},{8,9},{9,8},{10,11... | collective-permute-start | bytes 786440 | tf_op jit(solution)/shard_map/ppermute | solution.py:266
  26.6 3.4 %copy-start.7 = (f32[8,1,1024,2,128]{4,3,2,1,0:T(2,128)S(1)}, f32[8,1,1024,2,128]{4,3,2,1,0:T(2,128)}, u32[]{:S(2)}) copy-start(f32[8,1,1024,2,128]{4,3,2,1,0:T(2,128)} %param.5) | copy-start | bytes 25165828
  30.0 2.2 %copy-start.1 = (f32[1,8,1,1024,128]{4,3,2,1,0:T(8,128)S(1)}, f32[1,8,1,1024,128]{4,3,2,1,0:T(8,128)}, u32[]{:S(2)}) copy-start(f32[1,8,1,1024,128]{4,3,2,1,0:T(8,128)} %param.4) | copy-start | bytes 12582916
  30.0 2.5 %copy-start.8 = (f32[2,128,1024]{2,1,0:T(8,128)S(1)}, f32[2,128,1024]{2,1,0:T(8,128)}, u32[]{:S(2)}) copy-start(f32[2,128,1024]{2,1,0:T(8,128)} %inv_ref.3) | copy-start | bytes 3145732
  31.9 3.3 %copy-start.5 = (bf16[8,1024,256]{2,1,0:T(8,128)(2,1)}, bf16[8,1024,256]{2,1,0:T(8,128)(2,1)S(1)}, u32[]{:S(2)}) copy-start(bf16[8,1024,256]{2,1,0:T(8,128)(2,1)S(1)} %get-tuple-element.26.pl_ref) | copy-start | bytes 12582916
  35.3 1.5 %collective-permute-start.9 = (f32[4,128,128]{2,1,0:T(8,128)S(1)}, f32[4,128,128]{2,1,0:T(8,128)S(1)}, u32[]{:S(2)}, u32[]{:S(2)}) collective-permute-start(f32[4,128,128]{2,1,0:T(8,128)S(1)} %get-tuple-element.28), channel_id=1, source_target_pairs={{0,1},{1,0},{2,3},{3,2},{4,5},{5,4},{6,7},{7,6},{8,9},{9,8},{10,11... | collective-permute-start | bytes 786440 | tf_op jit(solution)/shard_map/ppermute | solution.py:266
  36.8 4.8 %collective-permute-start.10 = (f32[128,128]{1,0:T(8,128)S(1)}, f32[128,128]{1,0:T(8,128)S(1)}, u32[]{:S(2)}, u32[]{:S(2)}) collective-permute-start(f32[128,128]{1,0:T(8,128)S(1)} %get-tuple-element.30), channel_id=1, source_target_pairs={{0,2},{1,3},{2,4},{3,5},{4,6},{5,7},{6,0},{7,1},{8,10},{9,11},{10,... | collective-permute-start | bytes 196616 | tf_op jit(solution)/shard_map/ppermute | solution.py:270
  37.5 5.6 %collective-permute-start.11 = (f32[128,128]{1,0:T(8,128)S(1)}, f32[128,128]{1,0:T(8,128)S(1)}, u32[]{:S(2)}, u32[]{:S(2)}) collective-permute-start(f32[128,128]{1,0:T(8,128)S(1)} %get-tuple-element.31), channel_id=1, source_target_pairs={{0,4},{1,5},{2,6},{3,7},{4,0},{5,1},{6,2},{7,3},{8,12},{9,13},{10,... | collective-permute-start | bytes 196616 | tf_op jit(solution)/shard_map/ppermute | solution.py:270
  39.5 4.0 %collective-permute-start.12 = (f32[128,128]{1,0:T(8,128)S(1)}, f32[128,128]{1,0:T(8,128)S(1)}, u32[]{:S(2)}, u32[]{:S(2)}) collective-permute-start(f32[128,128]{1,0:T(8,128)S(1)} %get-tuple-element.32), channel_id=1, source_target_pairs={{0,6},{1,7},{2,0},{3,1},{4,2},{5,3},{6,4},{7,5},{8,14},{9,15},{10,... | collective-permute-start | bytes 196616 | tf_op jit(solution)/shard_map/ppermute | solution.py:270
  43.6 3.9 %collective-permute-start.15 = (f32[128,128]{1,0:T(8,128)S(1)}, f32[128,128]{1,0:T(8,128)S(1)}, u32[]{:S(2)}, u32[]{:S(2)}) collective-permute-start(f32[128,128]{1,0:T(8,128)S(1)} %right.3.a), channel_id=1, source_target_pairs={{0,6},{1,7},{2,0},{3,1},{4,2},{5,3},{6,4},{7,5},{8,14},{9,15},{10,... | collective-permute-start | bytes 196616 | tf_op jit(solution)/shard_map/ppermute | solution.py:270
  46.0 4.7 %collective-permute-start.14 = (f32[128,128]{1,0:T(8,128)S(1)}, f32[128,128]{1,0:T(8,128)S(1)}, u32[]{:S(2)}, u32[]{:S(2)}) collective-permute-start(f32[128,128]{1,0:T(8,128)S(1)} %right.3.a), channel_id=1, source_target_pairs={{0,4},{1,5},{2,6},{3,7},{4,0},{5,1},{6,2},{7,3},{8,12},{9,13},{10,... | collective-permute-start | bytes 196616 | tf_op jit(solution)/shard_map/ppermute | solution.py:270
  46.0 5.0 %collective-permute-start.13 = (f32[128,128]{1,0:T(8,128)S(1)}, f32[128,128]{1,0:T(8,128)S(1)}, u32[]{:S(2)}, u32[]{:S(2)}) collective-permute-start(f32[128,128]{1,0:T(8,128)S(1)} %right.3.a), channel_id=1, source_target_pairs={{0,2},{1,3},{2,4},{3,5},{4,6},{5,7},{6,0},{7,1},{8,10},{9,11},{10,... | collective-permute-start | bytes 196616 | tf_op jit(solution)/shard_map/ppermute | solution.py:270
  51.1 4.0 %collective-permute-start.16 = (f32[4,128,128]{2,1,0:T(8,128)S(1)}, f32[4,128,128]{2,1,0:T(8,128)S(1)}, u32[]{:S(2)}, u32[]{:S(2)}) collective-permute-start(f32[4,128,128]{2,1,0:T(8,128)S(1)} %lay.3.mine_ref), channel_id=1, source_target_pairs={{0,1},{1,0},{2,3},{3,2},{4,5},{5,4},{6,7},{7,6},{8,9},{9,8},{10,11... | collective-permute-start | bytes 786440 | tf_op jit(solution)/shard_map/ppermute | solution.py:266
  55.5 2.7 %collective-permute-start.19 = (f32[2,128,128]{2,1,0:T(8,128)S(1)}, f32[2,128,128]{2,1,0:T(8,128)S(1)}, u32[]{:S(2)}, u32[]{:S(2)}) collective-permute-start(f32[2,128,128]{2,1,0:T(8,128)S(1)} %second.1), channel_id=1, source_target_pairs={{8,24},{9,25},{10,26},{11,27},{12,28},{13,29},{14,30},{15,31}} | collective-permute-start | bytes 393224 | tf_op jit(solution)/shard_map/ppermute | solution.py:296
  56.2 2.0 %collective-permute-start.18 = (f32[2,128,128]{2,1,0:T(8,128)S(1)}, f32[2,128,128]{2,1,0:T(8,128)S(1)}, u32[]{:S(2)}, u32[]{:S(2)}) collective-permute-start(f32[2,128,128]{2,1,0:T(8,128)S(1)} %second.1), channel_id=1, source_target_pairs={{8,16},{9,17},{10,18},{11,19},{12,20},{13,21},{14,22},{15,23}} | collective-permute-start | bytes 393224 | tf_op jit(solution)/shard_map/ppermute | solution.py:296
  56.8 8.6 %collective-permute-start.17 = (f32[2,128,128]{2,1,0:T(8,128)S(1)}, f32[2,128,128]{2,1,0:T(8,128)S(1)}, u32[]{:S(2)}, u32[]{:S(2)}) collective-permute-start(f32[2,128,128]{2,1,0:T(8,128)S(1)} %second.1), channel_id=1, source_target_pairs={{8,0},{9,1},{10,2},{11,3},{12,4},{13,5},{14,6},{15,7}} | collective-permute-start | bytes 393224 | tf_op jit(solution)/shard_map/ppermute | solution.py:296
  65.5 3.9 %collective-permute-start.22 = (f32[2,128,128]{2,1,0:T(8,128)S(1)}, f32[2,128,128]{2,1,0:T(8,128)S(1)}, u32[]{:S(2)}, u32[]{:S(2)}) collective-permute-start(f32[2,128,128]{2,1,0:T(8,128)S(1)} %add_select_fusion), channel_id=1, source_target_pairs={{0,96},{8,104},{16,112},{24,120},{1,97},{9,105},{17,113},{25,121},... | collective-permute-start | bytes 393224 | tf_op jit(solution)/shard_map/ppermute | solution.py:298
  66.8 3.8 %collective-permute-start.21 = (f32[2,128,128]{2,1,0:T(8,128)S(1)}, f32[2,128,128]{2,1,0:T(8,128)S(1)}, u32[]{:S(2)}, u32[]{:S(2)}) collective-permute-start(f32[2,128,128]{2,1,0:T(8,128)S(1)} %add_select_fusion), channel_id=1, source_target_pairs={{0,64},{8,72},{16,80},{24,88},{1,65},{9,73},{17,81},{25,89},{2,66}... | collective-permute-start | bytes 393224 | tf_op jit(solution)/shard_map/ppermute | solution.py:298
  68.1 5.3 %collective-permute-start.20 = (f32[2,128,128]{2,1,0:T(8,128)S(1)}, f32[2,128,128]{2,1,0:T(8,128)S(1)}, u32[]{:S(2)}, u32[]{:S(2)}) collective-permute-start(f32[2,128,128]{2,1,0:T(8,128)S(1)} %add_select_fusion), channel_id=1, source_target_pairs={{0,32},{8,40},{16,48},{24,56},{1,33},{9,41},{17,49},{25,57},{2,34}... | collective-permute-start | bytes 393224 | tf_op jit(solution)/shard_map/ppermute | solution.py:298
  73.4 2.2 %copy-start.2 = (f32[1,8,1,1024,128]{4,3,2,1,0:T(8,128)S(1)}, f32[1,8,1,1024,128]{4,3,2,1,0:T(8,128)}, u32[]{:S(2)}) copy-start(f32[1,8,1,1024,128]{4,3,2,1,0:T(8,128)} %param.4) | copy-start | bytes 12582916
  75.6 2.2 %copy-start.4 = (bf16[8,1024,256]{2,1,0:T(8,128)(2,1)S(1)}, bf16[8,1024,256]{2,1,0:T(8,128)(2,1)}, u32[]{:S(2)}) copy-start(bf16[8,1024,256]{2,1,0:T(8,128)(2,1)} %copy-done.3) | copy-start | bytes 12582916
  77.7 2.2 %copy-start.6 = (bf16[8,1024,256]{2,1,0:T(8,128)(2,1)S(1)}, bf16[8,1024,256]{2,1,0:T(8,128)(2,1)}, u32[]{:S(2)}) copy-start(bf16[8,1024,256]{2,1,0:T(8,128)(2,1)} %copy-done.5) | copy-start | bytes 12582916
  (1 other events, 2.0 us)

commit v2 on v0

v2 whole, which is shorter than its diff:
```python
import functools

import jax
import jax.numpy as jnp
from jax import lax
from jax.experimental import pallas as pl
from jax.experimental.pallas import tpu as pltpu
from jax.sharding import PartitionSpec as P

F32 = jnp.float32
BF16 = jnp.bfloat16
NZ = 4
W = 128
NB = 1024
HALF = NB // 2
VMEM = pl.BlockSpec(memory_space=pltpu.VMEM)
ANY = pl.BlockSpec(memory_space=pl.ANY)


def in_vmem(x):
    return pltpu.with_memory_space_constraint(x, pltpu.VMEM)


def in_hbm(x):
    return pltpu.with_memory_space_constraint(x, pltpu.HBM)


def vm(shape, dtype=F32):
    return pltpu.VMEM(shape, dtype)


def call(kernel, name, out, hbm=(), vmem=(), deps=(), scratch=(), mib=4, out_specs=None):
    return pl.pallas_call(
        kernel,
        out_shape=out,
        in_specs=[ANY] * len(hbm) + [VMEM] * len(vmem) + [ANY] * len(deps),
        out_specs=out_specs or (VMEM,) * len(out),
        scratch_shapes=scratch,
        compiler_params=pltpu.CompilerParams(vmem_limit_bytes=mib * 2**20),
        name=name,
    )(*[in_hbm(v) for v in hbm], *[in_vmem(v) for v in vmem], *deps)


def split(x):
    hi = x.astype(BF16)
    return hi, (x - hi.astype(F32)).astype(BF16)


def dot(a, b):
    return jnp.dot(a, b, preferred_element_type=F32)


def pair_of(b):
    bh, bl = split(b)
    return jnp.concatenate([bh, bl], axis=1)


def dot3(a, both):
    ah, al = split(a)
    prod = dot(ah, both)
    return prod[:, :W] + (prod[:, W:] + dot(al, both[:, :W]))


def core():
    return lax.rem(lax.axis_index("col"), 2)


def half(h):
    return pl.ds(pl.multiple_of(h * HALF, HALF), HALF)


def pick_kernel(p_ref, send_ref, keep_ref, sem):
    h = core()
    one = pltpu.make_async_copy(p_ref.at[0, half(1 - h), :], send_ref, sem.at[0])
    two = pltpu.make_async_copy(p_ref.at[0, half(h), :], keep_ref, sem.at[1])
    one.start()
    two.start()
    one.wait()
    two.wait()


def pick(partials):
    out = vm((HALF, W))
    return call(pick_kernel, "pick", (out, out), hbm=(partials,), scratch=[pltpu.SemaphoreType.DMA((2,))])


def prep_kernel(panel_ref, inv_ref, rhs_ref, dep_ref, ts_ref, tk_ref, is_ref, ik_ref, r_ref, buf, sem):
    h = core()
    copies = []
    for i, (at, inv_out) in enumerate(((1 - h, is_ref), (h, ik_ref))):
        rows = pl.ds(pl.multiple_of(at * NB, NB), NB)
        copies.append(pltpu.make_async_copy(panel_ref.at[0, rows, :], buf.at[i], sem.at[2 * i]))
        copies.append(pltpu.make_async_copy(inv_ref.at[:, :, half(at)], inv_out, sem.at[2 * i + 1]))
    copies.append(pltpu.make_async_copy(rhs_ref.at[:, half(h), :], r_ref, sem.at[4]))
    for c in copies:
        c.start()
    for c in copies:
        c.wait()
    ts_ref[...] = buf[0, pl.ds(0, HALF, stride=2), :]
    tk_ref[...] = buf[1, pl.ds(0, HALF, stride=2), :]


def prep(panel, inverse, rhs, dep):
    return call(
        prep_kernel,
        "prep",
        (vm((HALF, W)), vm((HALF, W)), vm((2, W, HALF)), vm((2, W, HALF)), vm((2, HALF, W))),
        hbm=(panel, inverse, rhs),
        deps=(dep,),
        scratch=[pltpu.VMEM((2, NB, W), F32), pltpu.SemaphoreType.DMA((5,))],
    )


def add_kernel(a_ref, b_ref, out_ref):
    out_ref[...] = a_ref[...] + b_ref[...]


def add(a, b):
    return call(add_kernel, "add", (vm(a.shape),), vmem=(a, b))[0]


def join_kernel(keep_ref, got_ref, out_ref):
    h = core()
    out_ref[h] = keep_ref[...]
    out_ref[1 - h] = got_ref[...]


def join(keep, got):
    return call(join_kernel, "join", (vm((2, HALF, W)),), vmem=(keep, got))[0]


def first_kernel(rhs_ref, a, b, c, d, ik_ref, ig_ref, z_ref, s_ref):
    h = core()
    total = (a[...] + b[...]) + (c[...] + d[...])
    s_ref[...] = total
    both = pair_of(rhs_ref[0] - total)
    z_ref[h] = dot3(ik_ref[0], both)
    z_ref[1 - h] = dot3(ig_ref[0], both)


def first(rhs, sums, ik, ig):
    return call(first_kernel, "first", (vm((2, W, W)), vm((HALF, W))), vmem=(rhs, *sums, ik, ig))


def fold_kernel(z_ref, got_ref, tile_ref, y_ref, u_ref):
    block = z_ref[...] + got_ref[...]
    y_ref[...] = block
    u_ref[...] = dot3(tile_ref[0], pair_of(block[0])) + dot3(tile_ref[1], pair_of(block[1]))


def fold(z, got, tile):
    return call(fold_kernel, "fold", (vm((2, W, W)), vm((HALF, W))), vmem=(z, got, tile))


def second_kernel(rhs_ref, a, b, c, d, s_ref, ik_ref, ig_ref, dep_ref, send_ref, keep_ref):
    total = ((a[...] + b[...]) + (c[...] + d[...])) + s_ref[...]
    both = pair_of(rhs_ref[1] - total)
    keep_ref[...] = dot3(ik_ref[1], both)
    send_ref[...] = dot3(ig_ref[1], both)


def second(rhs, sums, s, ik, ig, dep):
    return call(
        second_kernel, "second", (vm((W, W)), vm((W, W))), vmem=(rhs, *sums, s, ik, ig), deps=(dep,)
    )


def stack_kernel(y_ref, keep_ref, got_ref, out_ref):
    out_ref[0] = y_ref[core()]
    out_ref[1] = keep_ref[...] + got_ref[...]


def stack(y0, keep, got):
    return call(stack_kernel, "stack", (vm((2, W, W)),), vmem=(y0, keep, got))[0]


def choose_kernel(a, b, c, d, out_ref):
    z = lax.rem(lax.axis_index("row"), NZ)
    for m, got in enumerate((a, b, c, d)):

        @pl.when(z == m)
        def _():
            out_ref[...] = got[...]


def choose(got):
    return call(choose_kernel, "choose", (vm((2, W, W)),), vmem=got)[0]


def parts_kernel(panel_ref, p_ref, dep_ref, hi_ref, lo_ref, part_ref, buf, sem):
    bring = pltpu.make_async_copy(p_ref, part_ref, sem.at[8])
    copies = [pltpu.make_async_copy(panel_ref.at[l], buf.at[l], sem.at[l]) for l in range(8)]
    for c in copies:
        c.start()
    bring.start()
    for l in range(8):
        copies[l].wait()
        for k in range(2):
            hi, lo = split(buf[l, pl.ds(k, NB, stride=2), :])
            hi_ref[l, :, k * W : (k + 1) * W] = hi
            lo_ref[l, :, k * W : (k + 1) * W] = lo
    bring.wait()


def parts(panel, partials, dep):
    out = vm((8, NB, 2 * W), BF16)
    return call(
        parts_kernel,
        "parts",
        (out, out, vm((8, NB, W))),
        hbm=(panel, partials),
        deps=(dep,),
        scratch=[pltpu.VMEM((8, 2 * NB, W), F32), pltpu.SemaphoreType.DMA((9,))],
        mib=12,
    )


STEP = 512


def update_kernel(a, b, c, d, ph_ref, pl_ref, part_ref, out_ref, solved_ref, buf, sem):
    row = lax.axis_index("row")
    x = row // NZ
    for m, got in enumerate((a, b, c, d)):

        @pl.when(x == m)
        def _():
            solved_ref[...] = got[...]

    y0 = solved_ref[0]
    y1 = solved_ref[1]
    per = NB // STEP
    head = jnp.concatenate([jnp.where(row > 0, y0, 0.0), jnp.where(row > 1, y1, 0.0)], axis=0)
    rest = jnp.concatenate([y0, y1], axis=0)

    def copy(l, j):
        rows = pl.ds(pl.multiple_of(j * STEP, STEP), STEP)
        return pltpu.make_async_copy(buf.at[l, rows, :], out_ref.at[l, rows, :], sem.at[l * per + j])

    def piece(l, j, w):
        rows = pl.ds(pl.multiple_of(j * STEP, STEP), STEP)
        prod = dot(ph_ref[l, rows, :], w)
        low = dot(pl_ref[l, rows, :], w[:, :W])
        buf[l, rows, :] = part_ref[l, rows, :] + (prod[:, :W] + (prod[:, W:] + low))
        copy(l, j).start()

    w = pair_of(head)
    for j in range(per):
        piece(0, j, w)
    w = pair_of(rest)

    def body(l, _):
        for j in range(per):
            piece(l, j, w)
        return 0

    lax.fori_loop(1, 8, body, 0)

    def done(l, _):
        for j in range(per):
            copy(l, j).wait()
        return 0

    lax.fori_loop(0, 8, done, 0)


def update(got, p_hi, p_lo, partials):
    return call(
        update_kernel,
        "update",
        (jax.ShapeDtypeStruct((8, NB, W), F32), jax.ShapeDtypeStruct((2, W, W), F32)),
        vmem=(*got, p_hi, p_lo, partials),
        out_specs=(ANY, VMEM),
        scratch=[pltpu.VMEM((8, NB, W), F32), pltpu.SemaphoreType.DMA((8 * NB // STEP,))],
        mib=10,
    )


def exchange(x, row_mask, col_mask):
    pairs = [(r * 8 + c, (r ^ row_mask) * 8 + (c ^ col_mask)) for r in range(16) for c in range(8)]
    return lax.ppermute(x, ("row", "col"), pairs)


def swap(x):
    return exchange(x, 0, 1)


def chips(x):
    return [x] + [exchange(x, 0, 2 * m) for m in (2, 1, 3)]


def per_device(partials, panel, inverse, rhs):
    partials = partials.reshape(8, NB, W)
    panel = panel.reshape(8, 2 * NB, W)
    send, keep = pick(partials)
    got = swap(send)
    tile_send, tile_keep, inv_send, inv_keep, rhs = prep(panel, inverse, rhs, send)
    inv_got = swap(inv_send)
    tile = exchange(join(tile_keep, swap(tile_send)), 1, 0)
    z, total = first(rhs, chips(add(keep, got)), inv_keep, inv_got)
    total = exchange(total, 1, 0)
    y0, u = fold(z, swap(z), tile)
    p_hi, p_lo, held = parts(panel, partials, u)
    send, keep = second(rhs, chips(u), total, inv_keep, inv_got, p_hi)
    y = stack(y0, keep, swap(send))
    y = choose([exchange(y, m, 1) for m in range(4)])
    new, solved = update([exchange(y, NZ * m, 1) for m in range(4)], p_hi, p_lo, held)
    return new[None, :, None], solved


def solution(mesh):
    return jax.shard_map(
        per_device,
        mesh=mesh,
        in_specs=(
            P("col", None, "row", None, None),
            P(None, "row", None, None, "col"),
            P(None, "col", None),
            P(),
        ),
        out_specs=(P("col", None, "row", None, None), P(None, "col", None)),
        check_vma=False,
    )
```

time: 335 us -> 70.6 us (0.21)
  waiting for transfers between devices: 274 us -> 32.5 us
  local copies, waits for them, and re-layouts: 24.1 us -> 0 us
  starting transfers between devices: 0.16 us -> 23.5 us
  matrix products: 21.6 us -> 0 us
  Pallas kernels: 0 us -> 13.7 us
  between operations: 13.8 us -> 0.72 us
    psum x4 -> x0, waiting for transfers between devices: 274 us -> none  [the longest x2 164 us: from_root(): return lax.psum(kept, axis)]
    ppermute x0 -> x21, waiting for transfers between devices: none -> 32.5 us  [exchange(): return lax.ppermute(x, ('row', 'col'), pairs)]
    ppermute x0 -> x21, starting transfers between devices: none -> 23.5 us  [exchange(): return lax.ppermute(x, ('row', 'col'), pairs)]
    dot_general x4 -> x0, matrix products: 21.6 us -> none  [the longest x2 16.7 us: per_device(): jnp.einsum('lnj,jq->lnq', tiles[:, :, k, :], block, precision=lax.Precisi...]
    unnamed x15 -> x0, local copies, waits for them, and re-layouts: 21.3 us -> none
    pallas_call x0 -> x11, Pallas kernels: none -> 13.7 us  [call(): pl.pallas_call(kernel, out_shape=out, in_specs=[ANY] * len(hbm) + [VMEM]...]
  transfers between devices with their start and end apart: 4 -> 21, of which waited for: 4 -> 15; matrix products, arithmetic and copies ran while one was open for 4% -> 0% of each run, Pallas kernels for 0% -> 8%
where the time goes in v2:
time: 70.6 us; the launch traced here: 70.4 us
  waiting for transfers between devices  32.5 us (46%)
  starting transfers between devices  23.5 us (33%)
  Pallas kernels  13.7 us (19%)
  between operations  0.72 us (1%)
    ppermute x21, waiting for transfers between devices, exchange(): return lax.ppermute(x, ('row', 'col'), pairs)  32.5 us
    ppermute x21, starting transfers between devices, exchange(): return lax.ppermute(x, ('row', 'col'), pairs)  23.5 us
    pallas_call x11, Pallas kernels, call(): pl.pallas_call(kernel, out_shape=out, in_specs=[ANY] * len(hbm) + [VMEM]...  13.7 us
  transfers between devices with their start and end apart: 21, of which 15 were waited for; matrix products, arithmetic and copies ran while one was open for 0% of the time, Pallas kernels for 8%

profile of v2, /device:TPU:1, one launch (start us, length us, event | category | flops | bytes accessed | tf_op | source)
XLA Modules:
  0.0 70.4 jit_solution(6886948578556714883)
XLA Ops:
  0.6 1.1 %pick.1 = (f32[512,128]{1,0:T(8,128)S(1)}, f32[512,128]{1,0:T(8,128)S(1)}) custom-call(f32[8,1024,128]{2,1,0:T(8,128)} %bitcast.7), custom_call_target="tpu_custom_call" | custom-call | tf_op jit(solution)/shard_map/pick/pallas_call | solution.py:33
  1.7 1.8 %prep.1 = (f32[512,128]{1,0:T(8,128)S(1)}, f32[512,128]{1,0:T(8,128)S(1)}, f32[2,128,512]{2,1,0:T(8,128)S(1)}, f32[2,128,512]{2,1,0:T(8,128)S(1)}, f32[2,512,128]{2,1,0:T(8,128)S(1)}) custom-call(f32[8,2048,128]{2,1,0:T(8,128)} %bitcast.5, f32[2,128,1024]{2,1,0:T(8,128)} %inv_ref.1, f32[2,1024,128]{2,1,0:T(8,128)} %rhs_ref.1, ...), custom_call_target="tpu_custom_call" | custom-call | tf_op jit(solution)/shard_map/prep/pallas_call | solution.py:33
  3.5 1.5 %collective-permute-start.6 = (f32[512,128]{1,0:T(8,128)S(1)}, f32[512,128]{1,0:T(8,128)S(1)}, u32[]{:S(2)}, u32[]{:S(2)}) collective-permute-start(f32[512,128]{1,0:T(8,128)S(1)} %get-tuple-element.27), channel_id=1, source_target_pairs={{0,1},{1,0},{2,3},{3,2},{4,5},{5,4},{6,7},{7,6},{8,9},{9,8},{10,11... | collective-permute-start | bytes 786440 | tf_op jit(solution)/shard_map/ppermute | solution.py:281
  5.1 0.4 collective-permute-start.4
  5.5 0.7 collective-permute-done.6.got_ref
  6.2 1.8 %collective-permute-start.7 = (f32[2,512,128]{2,1,0:T(8,128)S(1)}, f32[2,512,128]{2,1,0:T(8,128)S(1)}, u32[]{:S(2)}, u32[]{:S(2)}) collective-permute-start(f32[2,512,128]{2,1,0:T(8,128)S(1)} %join.1), channel_id=1, source_target_pairs={{0,8},{1,9},{2,10},{3,11},{4,12},{5,13},{6,14},{7,15},{8,0},{9,1},... | collective-permute-start | bytes 1572872 | tf_op jit(solution)/shard_map/ppermute | solution.py:281
  8.0 2.8 %collective-permute-start.3 = (f32[512,128]{1,0:T(8,128)S(1)}, f32[512,128]{1,0:T(8,128)S(1)}, u32[]{:S(2)}, u32[]{:S(2)}) collective-permute-start(f32[512,128]{1,0:T(8,128)S(1)} %add.1.a), channel_id=1, source_target_pairs={{0,6},{1,7},{2,4},{3,5},{4,2},{5,3},{6,0},{7,1},{8,14},{9,15},{10,... | collective-permute-start | bytes 786440 | tf_op jit(solution)/shard_map/ppermute | solution.py:281
  10.8 1.3 %collective-permute-start.1 = (f32[512,128]{1,0:T(8,128)S(1)}, f32[512,128]{1,0:T(8,128)S(1)}, u32[]{:S(2)}, u32[]{:S(2)}) collective-permute-start(f32[512,128]{1,0:T(8,128)S(1)} %add.1.a), channel_id=1, source_target_pairs={{0,4},{1,5},{2,6},{3,7},{4,0},{5,1},{6,2},{7,3},{8,12},{9,13},{10,... | collective-permute-start | bytes 786440 | tf_op jit(solution)/shard_map/ppermute | solution.py:281
  12.1 4.5 %collective-permute-done.3.d = f32[512,128]{1,0:T(8,128)S(1)} collective-permute-done((f32[512,128]{1,0:T(8,128)S(1)}, f32[512,128]{1,0:T(8,128)S(1)}, u32[]{:S(2)}, u32[]{:S(2)}) %collective-permute-start.3) | collective-permute-done | bytes 262176 | tf_op jit(solution)/shard_map/ppermute | solution.py:281
  16.6 1.1 %collective-permute-done.2.c = f32[512,128]{1,0:T(8,128)S(1)} collective-permute-done((f32[512,128]{1,0:T(8,128)S(1)}, f32[512,128]{1,0:T(8,128)S(1)}, u32[]{:S(2)}, u32[]{:S(2)}) %collective-permute-start.2) | collective-permute-done | bytes 262176 | tf_op jit(solution)/shard_map/ppermute | solution.py:281
  17.7 5.6 %collective-permute-done.1.b = f32[512,128]{1,0:T(8,128)S(1)} collective-permute-done((f32[512,128]{1,0:T(8,128)S(1)}, f32[512,128]{1,0:T(8,128)S(1)}, u32[]{:S(2)}, u32[]{:S(2)}) %collective-permute-start.1) | collective-permute-done | bytes 262176 | tf_op jit(solution)/shard_map/ppermute | solution.py:281
  23.6 1.8 %collective-permute-start.5 = (f32[2,128,128]{2,1,0:T(8,128)S(1)}, f32[2,128,128]{2,1,0:T(8,128)S(1)}, u32[]{:S(2)}, u32[]{:S(2)}) collective-permute-start(f32[2,128,128]{2,1,0:T(8,128)S(1)} %get-tuple-element.25.z_ref), channel_id=1, source_target_pairs={{0,1},{1,0},{2,3},{3,2},{4,5},{5,4},{6,7},{7,6},{8,9},{9,8},{10,11... | collective-permute-start | bytes 393224 | tf_op jit(solution)/shard_map/ppermute | solution.py:281
  25.6 0.7 %collective-permute-done.5.got_ref = f32[2,128,128]{2,1,0:T(8,128)S(1)} collective-permute-done((f32[2,128,128]{2,1,0:T(8,128)S(1)}, f32[2,128,128]{2,1,0:T(8,128)S(1)}, u32[]{:S(2)}, u32[]{:S(2)}) %collective-permute-start.5) | collective-permute-done | bytes 131104 | tf_op jit(solution)/shard_map/ppermute | solution.py:281
  26.4 0.4 fold.1
  26.7 2.7 %collective-permute-start.10 = (f32[512,128]{1,0:T(8,128)S(1)}, f32[512,128]{1,0:T(8,128)S(1)}, u32[]{:S(2)}, u32[]{:S(2)}) collective-permute-start(f32[512,128]{1,0:T(8,128)S(1)} %get-tuple-element.29.dep_ref.a), channel_id=1, source_target_pairs={{0,6},{1,7},{2,4},{3,5},{4,2},{5,3},{6,0},{7,1},{8,14},{9,15},{10,... | collective-permute-start | bytes 786440 | tf_op jit(solution)/shard_map/ppermute | solution.py:281
  29.4 1.3 %collective-permute-start.8 = (f32[512,128]{1,0:T(8,128)S(1)}, f32[512,128]{1,0:T(8,128)S(1)}, u32[]{:S(2)}, u32[]{:S(2)}) collective-permute-start(f32[512,128]{1,0:T(8,128)S(1)} %get-tuple-element.29.dep_ref.a), channel_id=1, source_target_pairs={{0,4},{1,5},{2,6},{3,7},{4,0},{5,1},{6,2},{7,3},{8,12},{9,13},{10,... | collective-permute-start | bytes 786440 | tf_op jit(solution)/shard_map/ppermute | solution.py:281
  30.7 4.8 %parts.1 = (bf16[8,1024,256]{2,1,0:T(8,128)(2,1)S(1)}, bf16[8,1024,256]{2,1,0:T(8,128)(2,1)S(1)}, f32[8,1024,128]{2,1,0:T(8,128)S(1)}) custom-call(f32[8,2048,128]{2,1,0:T(8,128)} %bitcast.6, f32[8,1024,128]{2,1,0:T(8,128)} %bitcast.8, f32[512,128]{1,0:T(8,128)S(1)} %get-tuple-element.29.dep_ref.a), custom_call_target="tpu_custom_call" | custom-call | tf_op jit(solution)/shard_map/parts/pallas_call | solution.py:33
  35.6 1.1 %collective-permute-done.9.c = f32[512,128]{1,0:T(8,128)S(1)} collective-permute-done((f32[512,128]{1,0:T(8,128)S(1)}, f32[512,128]{1,0:T(8,128)S(1)}, u32[]{:S(2)}, u32[]{:S(2)}) %collective-permute-start.9) | collective-permute-done | bytes 262176 | tf_op jit(solution)/shard_map/ppermute | solution.py:281
  36.6 5.4 %collective-permute-done.8.b = f32[512,128]{1,0:T(8,128)S(1)} collective-permute-done((f32[512,128]{1,0:T(8,128)S(1)}, f32[512,128]{1,0:T(8,128)S(1)}, u32[]{:S(2)}, u32[]{:S(2)}) %collective-permute-start.8) | collective-permute-done | bytes 262176 | tf_op jit(solution)/shard_map/ppermute | solution.py:281
  42.4 1.6 %collective-permute-start.12 = (f32[128,128]{1,0:T(8,128)S(1)}, f32[128,128]{1,0:T(8,128)S(1)}, u32[]{:S(2)}, u32[]{:S(2)}) collective-permute-start(f32[128,128]{1,0:T(8,128)S(1)} %get-tuple-element.33), channel_id=1, source_target_pairs={{0,1},{1,0},{2,3},{3,2},{4,5},{5,4},{6,7},{7,6},{8,9},{9,8},{10,11... | collective-permute-start | bytes 196616 | tf_op jit(solution)/shard_map/ppermute | solution.py:281
  43.9 0.9 %collective-permute-done.12.got_ref = f32[128,128]{1,0:T(8,128)S(1)} collective-permute-done((f32[128,128]{1,0:T(8,128)S(1)}, f32[128,128]{1,0:T(8,128)S(1)}, u32[]{:S(2)}, u32[]{:S(2)}) %collective-permute-start.12) | collective-permute-done | bytes 65568 | tf_op jit(solution)/shard_map/ppermute | solution.py:281
  44.9 2.9 %collective-permute-start.16 = (f32[2,128,128]{2,1,0:T(8,128)S(1)}, f32[2,128,128]{2,1,0:T(8,128)S(1)}, u32[]{:S(2)}, u32[]{:S(2)}) collective-permute-start(f32[2,128,128]{2,1,0:T(8,128)S(1)} %stack.1), channel_id=1, source_target_pairs={{0,25},{1,24},{2,27},{3,26},{4,29},{5,28},{6,31},{7,30},{8,17},{9,... | collective-permute-start | bytes 393224 | tf_op jit(solution)/shard_map/ppermute | solution.py:281
  47.8 0.8 %collective-permute-start.15 = (f32[2,128,128]{2,1,0:T(8,128)S(1)}, f32[2,128,128]{2,1,0:T(8,128)S(1)}, u32[]{:S(2)}, u32[]{:S(2)}) collective-permute-start(f32[2,128,128]{2,1,0:T(8,128)S(1)} %stack.1), channel_id=1, source_target_pairs={{0,17},{1,16},{2,19},{3,18},{4,21},{5,20},{6,23},{7,22},{8,25},{9,... | collective-permute-start | bytes 393224 | tf_op jit(solution)/shard_map/ppermute | solution.py:281
  48.9 4.7 %collective-permute-done.16.d = f32[2,128,128]{2,1,0:T(8,128)S(1)} collective-permute-done((f32[2,128,128]{2,1,0:T(8,128)S(1)}, f32[2,128,128]{2,1,0:T(8,128)S(1)}, u32[]{:S(2)}, u32[]{:S(2)}) %collective-permute-start.16) | collective-permute-done | bytes 131104 | tf_op jit(solution)/shard_map/ppermute | solution.py:281
  53.6 1.4 %collective-permute-done.15.c = f32[2,128,128]{2,1,0:T(8,128)S(1)} collective-permute-done((f32[2,128,128]{2,1,0:T(8,128)S(1)}, f32[2,128,128]{2,1,0:T(8,128)S(1)}, u32[]{:S(2)}, u32[]{:S(2)}) %collective-permute-start.15) | collective-permute-done | bytes 131104 | tf_op jit(solution)/shard_map/ppermute | solution.py:281
  55.1 2.7 %collective-permute-start.20 = (f32[2,128,128]{2,1,0:T(8,128)S(1)}, f32[2,128,128]{2,1,0:T(8,128)S(1)}, u32[]{:S(2)}, u32[]{:S(2)}) collective-permute-start(f32[2,128,128]{2,1,0:T(8,128)S(1)} %choose.1), channel_id=1, source_target_pairs={{0,97},{1,96},{2,99},{3,98},{4,101},{5,100},{6,103},{7,102},{8,105... | collective-permute-start | bytes 393224 | tf_op jit(solution)/shard_map/ppermute | solution.py:281
  57.8 0.7 collective-permute-start.19
  58.5 0.4 collective-permute-start.18
  59.1 4.2 %collective-permute-done.20.d = f32[2,128,128]{2,1,0:T(8,128)S(1)} collective-permute-done((f32[2,128,128]{2,1,0:T(8,128)S(1)}, f32[2,128,128]{2,1,0:T(8,128)S(1)}, u32[]{:S(2)}, u32[]{:S(2)}) %collective-permute-start.20) | collective-permute-done | bytes 131104 | tf_op jit(solution)/shard_map/ppermute | solution.py:281
  63.4 1.6 %collective-permute-done.19.c = f32[2,128,128]{2,1,0:T(8,128)S(1)} collective-permute-done((f32[2,128,128]{2,1,0:T(8,128)S(1)}, f32[2,128,128]{2,1,0:T(8,128)S(1)}, u32[]{:S(2)}, u32[]{:S(2)}) %collective-permute-start.19) | collective-permute-done | bytes 131104 | tf_op jit(solution)/shard_map/ppermute | solution.py:281
  65.0 0.3 collective-permute-done.18.b
  65.4 5.1 %update.1 = (f32[8,1024,128]{2,1,0:T(8,128)}, f32[2,128,128]{2,1,0:T(8,128)}) custom-call(f32[2,128,128]{2,1,0:T(8,128)S(1)} %collective-permute-done.17.a, f32[2,128,128]{2,1,0:T(8,128)S(1)} %collective-permute-done.18.b, f32[2,128,128]{2,1,0:T(8,128)S(1)} %collective-permute-done.19.c, f32[2,128,128]{2,1,0:T(8,128)S(1)} %collective-permute-done.20.d, ...), custom_call_target="tpu_custom_call" | custom-call | tf_op jit(solution)/shard_map/update/pallas_call | solution.py:33
  (21 shorter events, 1.8 us)
Async XLA Ops:
  3.5 2.7 %collective-permute-start.6 = (f32[512,128]{1,0:T(8,128)S(1)}, f32[512,128]{1,0:T(8,128)S(1)}, u32[]{:S(2)}, u32[]{:S(2)}) collective-permute-start(f32[512,128]{1,0:T(8,128)S(1)} %get-tuple-element.27), channel_id=1, source_target_pairs={{0,1},{1,0},{2,3},{3,2},{4,5},{5,4},{6,7},{7,6},{8,9},{9,8},{10,11... | collective-permute-start | bytes 786440 | tf_op jit(solution)/shard_map/ppermute | solution.py:281
  5.0 3.0 %collective-permute-start = (f32[512,128]{1,0:T(8,128)S(1)}, f32[512,128]{1,0:T(8,128)S(1)}, u32[]{:S(2)}, u32[]{:S(2)}) collective-permute-start(f32[512,128]{1,0:T(8,128)S(1)} %get-tuple-element.20.dep_ref), channel_id=1, source_target_pairs={{0,1},{1,0},{2,3},{3,2},{4,5},{5,4},{6,7},{7,6},{8,9},{9,8},{10,11... | collective-permute-start | bytes 786440 | tf_op jit(solution)/shard_map/ppermute | solution.py:281
  5.1 18.2 %collective-permute-start.4 = (f32[2,128,512]{2,1,0:T(8,128)S(1)}, f32[2,128,512]{2,1,0:T(8,128)S(1)}, u32[]{:S(2)}, u32[]{:S(2)}) collective-permute-start(f32[2,128,512]{2,1,0:T(8,128)S(1)} %get-tuple-element.24), channel_id=1, source_target_pairs={{0,1},{1,0},{2,3},{3,2},{4,5},{5,4},{6,7},{7,6},{8,9},{9,8},{10,11... | collective-permute-start | bytes 1572872 | tf_op jit(solution)/shard_map/ppermute | solution.py:281
  6.2 20.2 %collective-permute-start.7 = (f32[2,512,128]{2,1,0:T(8,128)S(1)}, f32[2,512,128]{2,1,0:T(8,128)S(1)}, u32[]{:S(2)}, u32[]{:S(2)}) collective-permute-start(f32[2,512,128]{2,1,0:T(8,128)S(1)} %join.1), channel_id=1, source_target_pairs={{0,8},{1,9},{2,10},{3,11},{4,12},{5,13},{6,14},{7,15},{8,0},{9,1},... | collective-permute-start | bytes 1572872 | tf_op jit(solution)/shard_map/ppermute | solution.py:281
  8.0 8.6 %collective-permute-start.3 = (f32[512,128]{1,0:T(8,128)S(1)}, f32[512,128]{1,0:T(8,128)S(1)}, u32[]{:S(2)}, u32[]{:S(2)}) collective-permute-start(f32[512,128]{1,0:T(8,128)S(1)} %add.1.a), channel_id=1, source_target_pairs={{0,6},{1,7},{2,4},{3,5},{4,2},{5,3},{6,0},{7,1},{8,14},{9,15},{10,... | collective-permute-start | bytes 786440 | tf_op jit(solution)/shard_map/ppermute | solution.py:281
  10.8 6.9 %collective-permute-start.2 = (f32[512,128]{1,0:T(8,128)S(1)}, f32[512,128]{1,0:T(8,128)S(1)}, u32[]{:S(2)}, u32[]{:S(2)}) collective-permute-start(f32[512,128]{1,0:T(8,128)S(1)} %add.1.a), channel_id=1, source_target_pairs={{0,2},{1,3},{2,0},{3,1},{4,6},{5,7},{6,4},{7,5},{8,10},{9,11},{10,... | collective-permute-start | bytes 786440 | tf_op jit(solution)/shard_map/ppermute | solution.py:281
  10.8 12.5 %collective-permute-start.1 = (f32[512,128]{1,0:T(8,128)S(1)}, f32[512,128]{1,0:T(8,128)S(1)}, u32[]{:S(2)}, u32[]{:S(2)}) collective-permute-start(f32[512,128]{1,0:T(8,128)S(1)} %add.1.a), channel_id=1, source_target_pairs={{0,4},{1,5},{2,6},{3,7},{4,0},{5,1},{6,2},{7,3},{8,12},{9,13},{10,... | collective-permute-start | bytes 786440 | tf_op jit(solution)/shard_map/ppermute | solution.py:281
  23.6 2.7 %collective-permute-start.5 = (f32[2,128,128]{2,1,0:T(8,128)S(1)}, f32[2,128,128]{2,1,0:T(8,128)S(1)}, u32[]{:S(2)}, u32[]{:S(2)}) collective-permute-start(f32[2,128,128]{2,1,0:T(8,128)S(1)} %get-tuple-element.25.z_ref), channel_id=1, source_target_pairs={{0,1},{1,0},{2,3},{3,2},{4,5},{5,4},{6,7},{7,6},{8,9},{9,8},{10,11... | collective-permute-start | bytes 393224 | tf_op jit(solution)/shard_map/ppermute | solution.py:281
  25.4 10.1 %collective-permute-start.11 = (f32[512,128]{1,0:T(8,128)S(1)}, f32[512,128]{1,0:T(8,128)S(1)}, u32[]{:S(2)}, u32[]{:S(2)}) collective-permute-start(f32[512,128]{1,0:T(8,128)S(1)} %get-tuple-element.30), channel_id=1, source_target_pairs={{0,8},{1,9},{2,10},{3,11},{4,12},{5,13},{6,14},{7,15},{8,0},{9,1},... | collective-permute-start | bytes 786440 | tf_op jit(solution)/shard_map/ppermute | solution.py:281
  26.7 8.8 %collective-permute-start.10 = (f32[512,128]{1,0:T(8,128)S(1)}, f32[512,128]{1,0:T(8,128)S(1)}, u32[]{:S(2)}, u32[]{:S(2)}) collective-permute-start(f32[512,128]{1,0:T(8,128)S(1)} %get-tuple-element.29.dep_ref.a), channel_id=1, source_target_pairs={{0,6},{1,7},{2,4},{3,5},{4,2},{5,3},{6,0},{7,1},{8,14},{9,15},{10,... | collective-permute-start | bytes 786440 | tf_op jit(solution)/shard_map/ppermute | solution.py:281
  29.4 7.2 %collective-permute-start.9 = (f32[512,128]{1,0:T(8,128)S(1)}, f32[512,128]{1,0:T(8,128)S(1)}, u32[]{:S(2)}, u32[]{:S(2)}) collective-permute-start(f32[512,128]{1,0:T(8,128)S(1)} %get-tuple-element.29.dep_ref.a), channel_id=1, source_target_pairs={{0,2},{1,3},{2,0},{3,1},{4,6},{5,7},{6,4},{7,5},{8,10},{9,11},{10,... | collective-permute-start | bytes 786440 | tf_op jit(solution)/shard_map/ppermute | solution.py:281
  29.4 12.6 %collective-permute-start.8 = (f32[512,128]{1,0:T(8,128)S(1)}, f32[512,128]{1,0:T(8,128)S(1)}, u32[]{:S(2)}, u32[]{:S(2)}) collective-permute-start(f32[512,128]{1,0:T(8,128)S(1)} %get-tuple-element.29.dep_ref.a), channel_id=1, source_target_pairs={{0,4},{1,5},{2,6},{3,7},{4,0},{5,1},{6,2},{7,3},{8,12},{9,13},{10,... | collective-permute-start | bytes 786440 | tf_op jit(solution)/shard_map/ppermute | solution.py:281
  42.4 2.5 %collective-permute-start.12 = (f32[128,128]{1,0:T(8,128)S(1)}, f32[128,128]{1,0:T(8,128)S(1)}, u32[]{:S(2)}, u32[]{:S(2)}) collective-permute-start(f32[128,128]{1,0:T(8,128)S(1)} %get-tuple-element.33), channel_id=1, source_target_pairs={{0,1},{1,0},{2,3},{3,2},{4,5},{5,4},{6,7},{7,6},{8,9},{9,8},{10,11... | collective-permute-start | bytes 196616 | tf_op jit(solution)/shard_map/ppermute | solution.py:281
  44.9 8.7 %collective-permute-start.16 = (f32[2,128,128]{2,1,0:T(8,128)S(1)}, f32[2,128,128]{2,1,0:T(8,128)S(1)}, u32[]{:S(2)}, u32[]{:S(2)}) collective-permute-start(f32[2,128,128]{2,1,0:T(8,128)S(1)} %stack.1), channel_id=1, source_target_pairs={{0,25},{1,24},{2,27},{3,26},{4,29},{5,28},{6,31},{7,30},{8,17},{9,... | collective-permute-start | bytes 393224 | tf_op jit(solution)/shard_map/ppermute | solution.py:281
  47.8 7.2 %collective-permute-start.15 = (f32[2,128,128]{2,1,0:T(8,128)S(1)}, f32[2,128,128]{2,1,0:T(8,128)S(1)}, u32[]{:S(2)}, u32[]{:S(2)}) collective-permute-start(f32[2,128,128]{2,1,0:T(8,128)S(1)} %stack.1), channel_id=1, source_target_pairs={{0,17},{1,16},{2,19},{3,18},{4,21},{5,20},{6,23},{7,22},{8,25},{9,... | collective-permute-start | bytes 393224 | tf_op jit(solution)/shard_map/ppermute | solution.py:281
  48.6 6.5 %collective-permute-start.14 = (f32[2,128,128]{2,1,0:T(8,128)S(1)}, f32[2,128,128]{2,1,0:T(8,128)S(1)}, u32[]{:S(2)}, u32[]{:S(2)}) collective-permute-start(f32[2,128,128]{2,1,0:T(8,128)S(1)} %stack.1), channel_id=1, source_target_pairs={{0,9},{1,8},{2,11},{3,10},{4,13},{5,12},{6,15},{7,14},{8,1},{9,0},... | collective-permute-start | bytes 393224 | tf_op jit(solution)/shard_map/ppermute | solution.py:281
  48.7 6.4 %collective-permute-start.13 = (f32[2,128,128]{2,1,0:T(8,128)S(1)}, f32[2,128,128]{2,1,0:T(8,128)S(1)}, u32[]{:S(2)}, u32[]{:S(2)}) collective-permute-start(f32[2,128,128]{2,1,0:T(8,128)S(1)} %stack.1), channel_id=1, source_target_pairs={{0,1},{1,0},{2,3},{3,2},{4,5},{5,4},{6,7},{7,6},{8,9},{9,8},{10,11... | collective-permute-start | bytes 393224 | tf_op jit(solution)/shard_map/ppermute | solution.py:281
  55.1 8.2 %collective-permute-start.20 = (f32[2,128,128]{2,1,0:T(8,128)S(1)}, f32[2,128,128]{2,1,0:T(8,128)S(1)}, u32[]{:S(2)}, u32[]{:S(2)}) collective-permute-start(f32[2,128,128]{2,1,0:T(8,128)S(1)} %choose.1), channel_id=1, source_target_pairs={{0,97},{1,96},{2,99},{3,98},{4,101},{5,100},{6,103},{7,102},{8,105... | collective-permute-start | bytes 393224 | tf_op jit(solution)/shard_map/ppermute | solution.py:281
  57.8 7.2 %collective-permute-start.19 = (f32[2,128,128]{2,1,0:T(8,128)S(1)}, f32[2,128,128]{2,1,0:T(8,128)S(1)}, u32[]{:S(2)}, u32[]{:S(2)}) collective-permute-start(f32[2,128,128]{2,1,0:T(8,128)S(1)} %choose.1), channel_id=1, source_target_pairs={{0,65},{1,64},{2,67},{3,66},{4,69},{5,68},{6,71},{7,70},{8,73},{9,... | collective-permute-start | bytes 393224 | tf_op jit(solution)/shard_map/ppermute | solution.py:281
  58.5 6.9 %collective-permute-start.18 = (f32[2,128,128]{2,1,0:T(8,128)S(1)}, f32[2,128,128]{2,1,0:T(8,128)S(1)}, u32[]{:S(2)}, u32[]{:S(2)}) collective-permute-start(f32[2,128,128]{2,1,0:T(8,128)S(1)} %choose.1), channel_id=1, source_target_pairs={{0,33},{1,32},{2,35},{3,34},{4,37},{5,36},{6,39},{7,38},{8,41},{9,... | collective-permute-start | bytes 393224 | tf_op jit(solution)/shard_map/ppermute | solution.py:281
  58.8 6.5 %collective-permute-start.17 = (f32[2,128,128]{2,1,0:T(8,128)S(1)}, f32[2,128,128]{2,1,0:T(8,128)S(1)}, u32[]{:S(2)}, u32[]{:S(2)}) collective-permute-start(f32[2,128,128]{2,1,0:T(8,128)S(1)} %choose.1), channel_id=1, source_target_pairs={{0,1},{1,0},{2,3},{3,2},{4,5},{5,4},{6,7},{7,6},{8,9},{9,8},{10,11... | collective-permute-start | bytes 393224 | tf_op jit(solution)/shard_map/ppermute | solution.py:281

commit v3 on v2

v3 whole, which is shorter than its diff:
```python
import functools

import jax
import jax.numpy as jnp
from jax import lax
from jax.experimental import pallas as pl
from jax.experimental.pallas import tpu as pltpu
from jax.sharding import PartitionSpec as P

F32 = jnp.float32
BF16 = jnp.bfloat16
NZ = 4
W = 128
NB = 1024
PACK = NB // 4
VMEM = pl.BlockSpec(memory_space=pltpu.VMEM)
ANY = pl.BlockSpec(memory_space=pl.ANY)


def in_vmem(x):
    return pltpu.with_memory_space_constraint(x, pltpu.VMEM)


def in_hbm(x):
    return pltpu.with_memory_space_constraint(x, pltpu.HBM)


def vm(shape, dtype=F32):
    return pltpu.VMEM(shape, dtype)


PACKED = vm((PACK, W))


def call(kernel, name, out, hbm=(), vmem=(), deps=(), scratch=(), mib=4, out_specs=None, mb=None, aliases={}):
    return pl.pallas_call(
        kernel,
        out_shape=out,
        in_specs=[ANY] * len(hbm) + [VMEM] * len(vmem) + [ANY] * len(deps),
        out_specs=out_specs or (VMEM,) * len(out),
        scratch_shapes=scratch,
        compiler_params=pltpu.CompilerParams(vmem_limit_bytes=mib * 2**20),
        input_output_aliases=aliases,
        cost_estimate=mb and pl.CostEstimate(flops=0, bytes_accessed=mb * 2**20, transcendentals=0),
        name=name,
    )(*[in_hbm(v) for v in hbm], *[in_vmem(v) for v in vmem], *deps)


def split(x):
    hi = x.astype(BF16)
    return hi, (x - hi.astype(F32)).astype(BF16)


def dot(a, b):
    return jnp.dot(a, b, preferred_element_type=F32)


def pair_of(b):
    bh, bl = split(b)
    return jnp.concatenate([bh, bl], axis=1)


def dot3(a, both):
    ah, al = split(a)
    prod = dot(ah, both)
    return prod[:, :W] + (prod[:, W:] + dot(al, both[:, :W]))


def core():
    return lax.rem(lax.axis_index("col"), 2)


def odd_row():
    return lax.rem(lax.axis_index("row"), 2)


def lane_group(shape):
    return lax.broadcasted_iota(jnp.int32, shape, 1) // 32


def pack(src, b):
    out = None
    for g in range(4):
        rows = src[PACK * g : PACK * (g + 1)]
        shift = 32 * ((g - b) % 4)
        rows = pltpu.roll(rows, shift, 1) if shift else rows
        out = rows if out is None else jnp.where(lane_group(rows.shape) == g, rows, out)
    return out


def unpack(p):
    out = []
    for g in range(4):
        m = jnp.where(lane_group(p.shape) == g, p, 0.0)
        m = m + pltpu.roll(m, 32, 1)
        out.append(m + pltpu.roll(m, 64, 1))
    return jnp.concatenate(out, axis=0)


def start_kernel(p_ref, send_ref, keep_ref, p_buf, q_buf, sem):
    h = core()
    one = pltpu.make_async_copy(p_ref.at[0], p_buf, sem.at[0])
    one.start()
    one.wait()
    for b in range(4):
        q_buf[b] = pack(p_buf, b)
    for r in range(2):
        keep_ref[r] = q_buf[2 * r + h]
        send_ref[r] = q_buf[2 * r + 1 - h]


def start(partials):
    return call(
        start_kernel,
        "start",
        (vm((2, PACK, W)), vm((2, PACK, W))),
        hbm=(partials,),
        scratch=[pltpu.VMEM((NB, W), F32), pltpu.VMEM((4, PACK, W), F32), pltpu.SemaphoreType.DMA((1,))],
    )


def tile_kernel(panel_ref, dep_ref, out_ref, buf, sem):
    copy = pltpu.make_async_copy(panel_ref.at[0], buf, sem.at[0])
    copy.start()
    copy.wait()
    out_ref[...] = buf[pl.ds(0, NB, stride=2), :]


def first_tile(panel, dep):
    return call(
        tile_kernel,
        "tile",
        (vm((NB, W)),),
        hbm=(panel,),
        deps=(dep,),
        scratch=[pltpu.VMEM((2 * NB, W), F32), pltpu.SemaphoreType.DMA((1,))],
        mb=8,
    )[0]


def prep_kernel(inv_ref, rhs_ref, dep_ref, inv_out, rhs_out, r_buf, q_buf, sem):
    one = pltpu.make_async_copy(rhs_ref, r_buf, sem.at[0])
    two = pltpu.make_async_copy(inv_ref, inv_out, sem.at[1])
    one.start()
    two.start()
    one.wait()
    b = 2 * odd_row() + core()
    for k in range(2):
        for at in range(4):
            q_buf[at] = pack(r_buf.at[k], at)
        rhs_out[k] = q_buf[b]
    two.wait()


def prep(inverse, rhs, dep):
    return call(
        prep_kernel,
        "prep",
        (vm((2, W, NB)), vm((2, PACK, W))),
        hbm=(inverse, rhs),
        deps=(dep,),
        scratch=[
            pltpu.VMEM((2, NB, W), F32),
            pltpu.VMEM((4, PACK, W), F32),
            pltpu.SemaphoreType.DMA((2,)),
        ],
        mb=8,
    )


def add_kernel(a_ref, b_ref, mine_ref, other_ref):
    r = odd_row()
    mine_ref[...] = a_ref[r] + b_ref[r]
    other_ref[...] = a_ref[1 - r] + b_ref[1 - r]


def add(a, b):
    return call(add_kernel, "add", (PACKED, PACKED), vmem=(a, b))


def order_kernel(mine_ref, got_ref, _, even_ref, odd_ref, same_ref):
    r = odd_row()

    @pl.when(r == 0)
    def _():
        even_ref[...] = mine_ref[...]
        odd_ref[...] = got_ref[...]

    @pl.when(r == 1)
    def _():
        even_ref[...] = got_ref[...]
        odd_ref[...] = mine_ref[...]


def order(mine, got, tile):
    return call(
        order_kernel, "order", (PACKED, PACKED, vm((NB, W))), vmem=(mine, got, tile), aliases={2: 2}
    )


def odd_kernel(own_ref, got_ref, dep0, dep1, dep2, dep3, out_ref):
    r = odd_row()

    @pl.when(r == 1)
    def _():
        out_ref[...] = own_ref[...]

    @pl.when(r == 0)
    def _():
        out_ref[...] = got_ref[...]


def odd_tile(own, got, deps):
    return call(odd_kernel, "odd", (vm((NB, W)),), vmem=(own, got), deps=deps)[0]


def first_kernel(rhs_ref, a, b, c, d, odd_ref, own_ref, got_ref, t_own, t_got, y_ref, u_ref):
    total = (a[...] + b[...]) + (c[...] + d[...])
    both = pair_of(unpack(rhs_ref[0] - total))
    y_own = dot3(own_ref[0], both)
    y_got = dot3(got_ref[0], both)
    y_ref[0] = y_own
    y_ref[1] = y_got
    own, got = pair_of(y_own), pair_of(y_got)
    out = odd_ref[...]
    group = lane_group(out.shape)
    for g in range(4):
        rows = pl.ds(PACK * g, PACK)
        u = dot3(t_own[rows, :], own) + dot3(t_got[rows, :], got)
        out = jnp.where(group == g, out + u, out)
    u_ref[...] = out


def first(rhs, sums, odd, own, got, t_own, t_got):
    return call(
        first_kernel,
        "first",
        (vm((2, W, W)), PACKED),
        vmem=(rhs, *sums, odd, own, got, t_own, t_got),
        mib=8,
    )


def second_kernel(rhs_ref, a, b, c, d, own_ref, got_ref, y_ref, dep_ref, keep_ref, send_ref):
    total = (a[...] + b[...]) + (c[...] + d[...])
    both = pair_of(unpack(rhs_ref[1] - total))
    group = lane_group((W, W))
    keep_ref[...] = jnp.where(group < 2, y_ref[0], dot3(own_ref[1], both))
    send_ref[...] = jnp.where(group < 2, y_ref[1], dot3(got_ref[1], both))


def second(rhs, sums, own, got, y0, dep):
    return call(
        second_kernel,
        "second",
        (vm((W, W)), vm((W, W))),
        vmem=(rhs, *sums, own, got, y0),
        deps=(dep,),
        mib=8,
    )


def merge_kernel(keep_ref, got_ref, out_ref):
    mine = lane_group((W, W)) % 2 == core()
    out_ref[...] = jnp.where(mine, keep_ref[...], got_ref[...])


def merge(keep, got):
    return call(merge_kernel, "merge", (vm((W, W)),), vmem=(keep, got))[0]


def choose_kernel(a, b, c, d, out_ref):
    x = lax.axis_index("row") // NZ
    for m, got in enumerate((a, b, c, d)):

        @pl.when(x == m)
        def _():
            out_ref[...] = got[...]


def choose(got):
    return call(choose_kernel, "choose", (vm((W, W)),), vmem=got)[0]


GROUP = 4


def parts_kernel(group, panel_ref, p_ref, dep_ref, hi_ref, lo_ref, part_ref, buf, sem):
    bring = pltpu.make_async_copy(p_ref.at[pl.ds(group * GROUP, GROUP)], part_ref, sem.at[GROUP])
    copies = [
        pltpu.make_async_copy(panel_ref.at[group * GROUP + l], buf.at[l], sem.at[l]) for l in range(GROUP)
    ]
    for c in copies:
        c.start()
    bring.start()
    for l in range(GROUP):
        copies[l].wait()
        for k in range(2):
            hi, lo = split(buf[l, pl.ds(k, NB, stride=2), :])
            hi_ref[l, :, k * W : (k + 1) * W] = hi
            lo_ref[l, :, k * W : (k + 1) * W] = lo
    bring.wait()


def parts(group, panel, partials, dep):
    out = vm((GROUP, NB, 2 * W), BF16)
    return call(
        functools.partial(parts_kernel, group),
        "parts",
        (out, out, vm((GROUP, NB, W))),
        hbm=(panel, partials),
        deps=(dep,),
        scratch=[pltpu.VMEM((GROUP, 2 * NB, W), F32), pltpu.SemaphoreType.DMA((GROUP + 1,))],
        mib=6,
        mb=12,
    )


STEP = 512


def update_kernel(a, b, c, d, ph0, pl0, part0, ph1, pl1, part1, out_ref, solved_ref, buf, sides, sem):
    row = lax.axis_index("row")
    z = lax.rem(row, NZ)
    for m, got in enumerate((a, b, c, d)):

        @pl.when(z == m)
        def _():
            sides[0] = got[...]

        @pl.when(z == m ^ 1)
        def _():
            sides[1] = got[...]

    left, right = sides[0], sides[1]
    low_half = lane_group((W, W)) < 2
    y0 = jnp.where(low_half, left, pltpu.roll(right, 64, 1))
    y1 = jnp.where(low_half, pltpu.roll(left, 64, 1), right)
    solved_ref[0] = y0
    solved_ref[1] = y1
    per = NB // STEP
    head = jnp.concatenate([jnp.where(row > 0, y0, 0.0), jnp.where(row > 1, y1, 0.0)], axis=0)
    rest = jnp.concatenate([y0, y1], axis=0)

    def copy(l, j):
        rows = pl.ds(pl.multiple_of(j * STEP, STEP), STEP)
        return pltpu.make_async_copy(buf.at[l, rows, :], out_ref.at[l, rows, :], sem.at[l * per + j])

    def block(group, l, w):
        hi, lo, part = ((ph0, pl0, part0), (ph1, pl1, part1))[group]
        for j in range(per):
            rows = pl.ds(j * STEP, STEP)
            prod = dot(hi[l, rows, :], w)
            low = dot(lo[l, rows, :], w[:, :W])
            at = group * GROUP + l
            buf[at, rows, :] = part[l, rows, :] + (prod[:, :W] + (prod[:, W:] + low))
            copy(at, j).start()

    block(0, 0, pair_of(head))
    w = pair_of(rest)

    def body(group, l, _):
        block(group, l, w)
        return 0

    lax.fori_loop(1, GROUP, functools.partial(body, 0), 0)
    lax.fori_loop(0, GROUP, functools.partial(body, 1), 0)

    def done(l, _):
        for j in range(per):
            copy(l, j).wait()
        return 0

    lax.fori_loop(0, 8, done, 0)


def update(got, parts0, parts1):
    return call(
        update_kernel,
        "update",
        (jax.ShapeDtypeStruct((8, NB, W), F32), jax.ShapeDtypeStruct((2, W, W), F32)),
        vmem=(*got, *parts0, *parts1),
        out_specs=(ANY, VMEM),
        scratch=[
            pltpu.VMEM((8, NB, W), F32),
            pltpu.VMEM((2, W, W), F32),
            pltpu.SemaphoreType.DMA((8 * NB // STEP,)),
        ],
        mib=10,
    )


def exchange(x, row_mask, col_mask):
    pairs = [(r * 8 + c, (r ^ row_mask) * 8 + (c ^ col_mask)) for r in range(16) for c in range(8)]
    return lax.ppermute(x, ("row", "col"), pairs)


def swap(x):
    return exchange(x, 0, 1)


def chips(x):
    return [x] + [exchange(x, 0, 2 * m) for m in (1, 2, 3)]


def rows_over(y, step):
    return [y] + [exchange(y, step * m, 0) for m in (1, 2, 3)]


def per_device(partials, panel, inverse, rhs):
    partials = partials.reshape(8, NB, W)
    panel = panel.reshape(8, 2 * NB, W)
    send, keep = start(partials)
    mine, other = add(keep, swap(send))
    tile = first_tile(panel, send)
    inv, rhs = prep(inverse, rhs, mine)
    inv_got = swap(inv)
    even, odd, tile = order(mine, exchange(other, 1, 0), tile)
    parts0 = parts(0, panel, partials, even)
    sums = chips(even)
    tile = odd_tile(tile, exchange(tile, 1, 0), (*sums[1:], parts0[0]))
    tile_got = swap(tile)
    y0, u = first(rhs, sums, odd, inv, inv_got, tile, tile_got)
    parts1 = parts(1, panel, partials, u)
    keep, send = second(rhs, chips(u), inv, inv_got, y0, parts1[0])
    y = choose(rows_over(merge(keep, swap(send)), NZ))
    new, solved = update(rows_over(y, 1), parts0, parts1)
    return new[None, :, None], solved


def solution(mesh):
    return jax.shard_map(
        per_device,
        mesh=mesh,
        in_specs=(
            P("col", None, "row", None, None),
            P(None, "row", None, None, "col"),
            P(None, "col", None),
            P(),
        ),
        out_specs=(P("col", None, "row", None, None), P(None, "col", None)),
        check_vma=False,
    )
```

time: 70.6 us -> 63.4 us (0.90)
  the two profiles are of different devices: /device:TPU:1 before, /device:TPU:0 now
where the time goes in v3:
time: 63.4 us; the launch traced here: 63.2 us
  waiting for transfers between devices  23.1 us (36%)
  starting transfers between devices  21.3 us (34%)
  Pallas kernels  18.1 us (29%)
  between operations  0.76 us (1%)
    ppermute x18, waiting for transfers between devices, exchange(): return lax.ppermute(x, ('row', 'col'), pairs)  23.1 us
    ppermute x18, starting transfers between devices, exchange(): return lax.ppermute(x, ('row', 'col'), pairs)  21.3 us
    pallas_call x13, Pallas kernels, call(): pl.pallas_call(kernel, out_shape=out, in_specs=[ANY] * len(hbm) + [VMEM]...  18.1 us
  transfers between devices with their start and end apart: 18, of which 13 were waited for; matrix products, arithmetic and copies ran while one was open for 0% of the time, Pallas kernels for 15%

profile of v3, /device:TPU:0, one launch (start us, length us, event | category | flops | bytes accessed | tf_op | source)
XLA Modules:
  0.0 63.2 jit_solution(11571776964948300706)
XLA Ops:
  0.6 1.6 %start.1 = (f32[2,256,128]{2,1,0:T(8,128)S(1)}, f32[2,256,128]{2,1,0:T(8,128)S(1)}) custom-call(f32[8,1024,128]{2,1,0:T(8,128)} %bitcast.8), custom_call_target="tpu_custom_call" | custom-call | tf_op jit(solution)/shard_map/start/pallas_call | solution.py:36
  2.3 1.5 %collective-permute-done.b_ref = f32[2,256,128]{2,1,0:T(8,128)S(1)} collective-permute-done((f32[2,256,128]{2,1,0:T(8,128)S(1)}, f32[2,256,128]{2,1,0:T(8,128)S(1)}, u32[]{:S(2)}, u32[]{:S(2)}) %collective-permute-start) | collective-permute-done | bytes 262176 | tf_op jit(solution)/shard_map/ppermute | solution.py:395
  3.9 2.1 %collective-permute-start.1 = (f32[256,128]{1,0:T(8,128)S(1)}, f32[256,128]{1,0:T(8,128)S(1)}, u32[]{:S(2)}, u32[]{:S(2)}) collective-permute-start(f32[256,128]{1,0:T(8,128)S(1)} %get-tuple-element.27), channel_id=1, source_target_pairs={{0,8},{1,9},{2,10},{3,11},{4,12},{5,13},{6,14},{7,15},{8,0},{9,1},... | collective-permute-start | bytes 393224 | tf_op jit(solution)/shard_map/ppermute | solution.py:395
  6.0 1.3 %tile.1._ = f32[1024,128]{1,0:T(8,128)S(1)} custom-call(f32[8,2048,128]{2,1,0:T(8,128)} %bitcast.5, f32[2,256,128]{2,1,0:T(8,128)S(1)} %get-tuple-element.24.dep_ref), custom_call_target="tpu_custom_call" | custom-call | bytes 8388608 | tf_op jit(solution)/shard_map/tile/pallas_call | solution.py:36
  7.2 2.1 %prep.1 = (f32[2,128,1024]{2,1,0:T(8,128)S(1)}, f32[2,256,128]{2,1,0:T(8,128)S(1)}) custom-call(f32[2,128,1024]{2,1,0:T(8,128)} %inv_ref.1, f32[2,1024,128]{2,1,0:T(8,128)} %rhs_ref.1, f32[256,128]{1,0:T(8,128)S(1)} %get-tuple-element.25.dep_ref.mine_ref), custom_call_target="tpu_custom_call" | custom-call | bytes 8388608 | tf_op jit(solution)/shard_map/prep/pallas_call | solution.py:36
  9.8 1.8 %collective-permute-start.6 = (f32[1024,128]{1,0:T(8,128)S(1)}, f32[1024,128]{1,0:T(8,128)S(1)}, u32[]{:S(2)}, u32[]{:S(2)}) collective-permute-start(f32[1024,128]{1,0:T(8,128)S(1)} %get-tuple-element.31.own_ref), channel_id=1, source_target_pairs={{0,8},{1,9},{2,10},{3,11},{4,12},{5,13},{6,14},{7,15},{8,0},{9,1},... | collective-permute-start | bytes 1572872 | tf_op jit(solution)/shard_map/ppermute | solution.py:395
  11.6 3.0 %collective-permute-start.4 = (f32[256,128]{1,0:T(8,128)S(1)}, f32[256,128]{1,0:T(8,128)S(1)}, u32[]{:S(2)}, u32[]{:S(2)}) collective-permute-start(f32[256,128]{1,0:T(8,128)S(1)} %get-tuple-element.28.dep_ref.a), channel_id=1, source_target_pairs={{0,6},{1,7},{2,4},{3,5},{4,2},{5,3},{6,0},{7,1},{8,14},{9,15},{10,... | collective-permute-start | bytes 393224 | tf_op jit(solution)/shard_map/ppermute | solution.py:395
  14.6 0.6 collective-permute-start.3
  15.7 2.9 %parts.2 = (bf16[4,1024,256]{2,1,0:T(8,128)(2,1)S(1)}, bf16[4,1024,256]{2,1,0:T(8,128)(2,1)S(1)}, f32[4,1024,128]{2,1,0:T(8,128)S(1)}) custom-call(f32[8,2048,128]{2,1,0:T(8,128)} %bitcast.6, f32[8,1024,128]{2,1,0:T(8,128)} %bitcast.9, f32[256,128]{1,0:T(8,128)S(1)} %get-tuple-element.28.dep_ref.a), custom_call_target="tpu_custom_call" | custom-call | bytes 12582912 | tf_op jit(solution)/shard_map/parts/pallas_call | solution.py:36
  18.6 2.2 %collective-permute-done.4.dep2.d = f32[256,128]{1,0:T(8,128)S(1)} collective-permute-done((f32[256,128]{1,0:T(8,128)S(1)}, f32[256,128]{1,0:T(8,128)S(1)}, u32[]{:S(2)}, u32[]{:S(2)}) %collective-permute-start.4) | collective-permute-done | bytes 131104 | tf_op jit(solution)/shard_map/ppermute | solution.py:395
  20.9 1.6 %collective-permute-done.3.dep1.c = f32[256,128]{1,0:T(8,128)S(1)} collective-permute-done((f32[256,128]{1,0:T(8,128)S(1)}, f32[256,128]{1,0:T(8,128)S(1)}, u32[]{:S(2)}, u32[]{:S(2)}) %collective-permute-start.3) | collective-permute-done | bytes 131104 | tf_op jit(solution)/shard_map/ppermute | solution.py:395
  22.5 0.8 %collective-permute-done.6.got_ref = f32[1024,128]{1,0:T(8,128)S(1)} collective-permute-done((f32[1024,128]{1,0:T(8,128)S(1)}, f32[1024,128]{1,0:T(8,128)S(1)}, u32[]{:S(2)}, u32[]{:S(2)}) %collective-permute-start.6) | collective-permute-done | bytes 524320 | tf_op jit(solution)/shard_map/ppermute | solution.py:395
  23.4 1.9 %collective-permute-done.7.t_got = f32[1024,128]{1,0:T(8,128)S(1)} collective-permute-done((f32[1024,128]{1,0:T(8,128)S(1)}, f32[1024,128]{1,0:T(8,128)S(1)}, u32[]{:S(2)}, u32[]{:S(2)}) %collective-permute-start.7) | collective-permute-done | bytes 524320 | tf_op jit(solution)/shard_map/ppermute | solution.py:395
  25.3 1.3 %first.1 = (f32[2,128,128]{2,1,0:T(8,128)S(1)}, f32[256,128]{1,0:T(8,128)S(1)}) custom-call(f32[2,256,128]{2,1,0:T(8,128)S(1)} %get-tuple-element.26.rhs_ref, f32[256,128]{1,0:T(8,128)S(1)} %get-tuple-element.28.dep_ref.a, f32[256,128]{1,0:T(8,128)S(1)} %collective-permute-done.2.dep0.b, f32[256,128]{1,0:T(8,128)S(1)} %collective-permute-done.3.dep1.c, ...), custom_call_target="tpu_custom_call" | custom-call | tf_op jit(solution)/shard_map/first/pallas_call | solution.py:36
  26.6 3.0 %collective-permute-start.10 = (f32[256,128]{1,0:T(8,128)S(1)}, f32[256,128]{1,0:T(8,128)S(1)}, u32[]{:S(2)}, u32[]{:S(2)}) collective-permute-start(f32[256,128]{1,0:T(8,128)S(1)} %get-tuple-element.33.dep_ref.a), channel_id=1, source_target_pairs={{0,6},{1,7},{2,4},{3,5},{4,2},{5,3},{6,0},{7,1},{8,14},{9,15},{10,... | collective-permute-start | bytes 393224 | tf_op jit(solution)/shard_map/ppermute | solution.py:395
  29.6 0.6 collective-permute-start.9
  30.2 0.5 collective-permute-start.8
  30.8 2.9 %parts.3 = (bf16[4,1024,256]{2,1,0:T(8,128)(2,1)S(1)}, bf16[4,1024,256]{2,1,0:T(8,128)(2,1)S(1)}, f32[4,1024,128]{2,1,0:T(8,128)S(1)}) custom-call(f32[8,2048,128]{2,1,0:T(8,128)} %bitcast.7, f32[8,1024,128]{2,1,0:T(8,128)} %bitcast.10, f32[256,128]{1,0:T(8,128)S(1)} %get-tuple-element.33.dep_ref.a), custom_call_target="tpu_custom_call" | custom-call | bytes 12582912 | tf_op jit(solution)/shard_map/parts/pallas_call | solution.py:36
  33.7 1.8 %collective-permute-done.10.d = f32[256,128]{1,0:T(8,128)S(1)} collective-permute-done((f32[256,128]{1,0:T(8,128)S(1)}, f32[256,128]{1,0:T(8,128)S(1)}, u32[]{:S(2)}, u32[]{:S(2)}) %collective-permute-start.10) | collective-permute-done | bytes 131104 | tf_op jit(solution)/shard_map/ppermute | solution.py:395
  35.5 2.0 %collective-permute-done.9.c = f32[256,128]{1,0:T(8,128)S(1)} collective-permute-done((f32[256,128]{1,0:T(8,128)S(1)}, f32[256,128]{1,0:T(8,128)S(1)}, u32[]{:S(2)}, u32[]{:S(2)}) %collective-permute-start.9) | collective-permute-done | bytes 131104 | tf_op jit(solution)/shard_map/ppermute | solution.py:395
  37.5 0.7 %second.1 = (f32[128,128]{1,0:T(8,128)S(1)}, f32[128,128]{1,0:T(8,128)S(1)}) custom-call(f32[2,256,128]{2,1,0:T(8,128)S(1)} %get-tuple-element.26.rhs_ref, f32[256,128]{1,0:T(8,128)S(1)} %get-tuple-element.33.dep_ref.a, f32[256,128]{1,0:T(8,128)S(1)} %collective-permute-done.8.b, f32[256,128]{1,0:T(8,128)S(1)} %collective-permute-done.9.c, ...), custom_call_target="tpu_custom_call" | custom-call | tf_op jit(solution)/shard_map/second/pallas_call | solution.py:36
  38.3 1.2 %collective-permute-done.11.got_ref = f32[128,128]{1,0:T(8,128)S(1)} collective-permute-done((f32[128,128]{1,0:T(8,128)S(1)}, f32[128,128]{1,0:T(8,128)S(1)}, u32[]{:S(2)}, u32[]{:S(2)}) %collective-permute-start.11) | collective-permute-done | bytes 65568 | tf_op jit(solution)/shard_map/ppermute | solution.py:395
  39.6 2.8 %collective-permute-start.14 = (f32[128,128]{1,0:T(8,128)S(1)}, f32[128,128]{1,0:T(8,128)S(1)}, u32[]{:S(2)}, u32[]{:S(2)}) collective-permute-start(f32[128,128]{1,0:T(8,128)S(1)} %merge.1.a), channel_id=1, source_target_pairs={{0,96},{1,97},{2,98},{3,99},{4,100},{5,101},{6,102},{7,103},{8,104... | collective-permute-start | bytes 196616 | tf_op jit(solution)/shard_map/ppermute | solution.py:395
  42.4 0.8 %collective-permute-start.13 = (f32[128,128]{1,0:T(8,128)S(1)}, f32[128,128]{1,0:T(8,128)S(1)}, u32[]{:S(2)}, u32[]{:S(2)}) collective-permute-start(f32[128,128]{1,0:T(8,128)S(1)} %merge.1.a), channel_id=1, source_target_pairs={{0,64},{1,65},{2,66},{3,67},{4,68},{5,69},{6,70},{7,71},{8,72},{9,... | collective-permute-start | bytes 196616 | tf_op jit(solution)/shard_map/ppermute | solution.py:395
  43.2 0.5 collective-permute-start.12
  43.8 1.5 %collective-permute-done.14.d = f32[128,128]{1,0:T(8,128)S(1)} collective-permute-done((f32[128,128]{1,0:T(8,128)S(1)}, f32[128,128]{1,0:T(8,128)S(1)}, u32[]{:S(2)}, u32[]{:S(2)}) %collective-permute-start.14) | collective-permute-done | bytes 65568 | tf_op jit(solution)/shard_map/ppermute | solution.py:395
  45.3 3.2 %collective-permute-done.13.c = f32[128,128]{1,0:T(8,128)S(1)} collective-permute-done((f32[128,128]{1,0:T(8,128)S(1)}, f32[128,128]{1,0:T(8,128)S(1)}, u32[]{:S(2)}, u32[]{:S(2)}) %collective-permute-start.13) | collective-permute-done | bytes 65568 | tf_op jit(solution)/shard_map/ppermute | solution.py:395
  48.5 3.7 %collective-permute-start.17 = (f32[128,128]{1,0:T(8,128)S(1)}, f32[128,128]{1,0:T(8,128)S(1)}, u32[]{:S(2)}, u32[]{:S(2)}) collective-permute-start(f32[128,128]{1,0:T(8,128)S(1)} %choose.1.a), channel_id=1, source_target_pairs={{0,24},{1,25},{2,26},{3,27},{4,28},{5,29},{6,30},{7,31},{8,16},{9,... | collective-permute-start | bytes 196616 | tf_op jit(solution)/shard_map/ppermute | solution.py:395
  52.3 0.9 %collective-permute-start.15 = (f32[128,128]{1,0:T(8,128)S(1)}, f32[128,128]{1,0:T(8,128)S(1)}, u32[]{:S(2)}, u32[]{:S(2)}) collective-permute-start(f32[128,128]{1,0:T(8,128)S(1)} %choose.1.a), channel_id=1, source_target_pairs={{0,8},{1,9},{2,10},{3,11},{4,12},{5,13},{6,14},{7,15},{8,0},{9,1},... | collective-permute-start | bytes 196616 | tf_op jit(solution)/shard_map/ppermute | solution.py:395
  53.2 1.6 %collective-permute-done.17.d = f32[128,128]{1,0:T(8,128)S(1)} collective-permute-done((f32[128,128]{1,0:T(8,128)S(1)}, f32[128,128]{1,0:T(8,128)S(1)}, u32[]{:S(2)}, u32[]{:S(2)}) %collective-permute-start.17) | collective-permute-done | bytes 65568 | tf_op jit(solution)/shard_map/ppermute | solution.py:395
  54.8 3.3 %collective-permute-done.16.c = f32[128,128]{1,0:T(8,128)S(1)} collective-permute-done((f32[128,128]{1,0:T(8,128)S(1)}, f32[128,128]{1,0:T(8,128)S(1)}, u32[]{:S(2)}, u32[]{:S(2)}) %collective-permute-start.16) | collective-permute-done | bytes 65568 | tf_op jit(solution)/shard_map/ppermute | solution.py:395
  58.0 5.1 %update.1 = (f32[8,1024,128]{2,1,0:T(8,128)}, f32[2,128,128]{2,1,0:T(8,128)}) custom-call(f32[128,128]{1,0:T(8,128)S(1)} %choose.1.a, f32[128,128]{1,0:T(8,128)S(1)} %collective-permute-done.15.b, f32[128,128]{1,0:T(8,128)S(1)} %collective-permute-done.16.c, f32[128,128]{1,0:T(8,128)S(1)} %collective-permute-done.17.d, ...), custom_call_target="tpu_custom_call" | custom-call | tf_op jit(solution)/shard_map/update/pallas_call | solution.py:36
  (17 shorter events, 1.2 us)
Async XLA Ops:
  2.2 1.6 %collective-permute-start = (f32[2,256,128]{2,1,0:T(8,128)S(1)}, f32[2,256,128]{2,1,0:T(8,128)S(1)}, u32[]{:S(2)}, u32[]{:S(2)}) collective-permute-start(f32[2,256,128]{2,1,0:T(8,128)S(1)} %get-tuple-element.24.dep_ref), channel_id=1, source_target_pairs={{0,1},{1,0},{2,3},{3,2},{4,5},{5,4},{6,7},{7,6},{8,9},{9,8},{10,11... | collective-permute-start | bytes 786440 | tf_op jit(solution)/shard_map/ppermute | solution.py:395
  3.9 5.9 %collective-permute-start.1 = (f32[256,128]{1,0:T(8,128)S(1)}, f32[256,128]{1,0:T(8,128)S(1)}, u32[]{:S(2)}, u32[]{:S(2)}) collective-permute-start(f32[256,128]{1,0:T(8,128)S(1)} %get-tuple-element.27), channel_id=1, source_target_pairs={{0,8},{1,9},{2,10},{3,11},{4,12},{5,13},{6,14},{7,15},{8,0},{9,1},... | collective-permute-start | bytes 393224 | tf_op jit(solution)/shard_map/ppermute | solution.py:395
  9.8 13.5 %collective-permute-start.6 = (f32[1024,128]{1,0:T(8,128)S(1)}, f32[1024,128]{1,0:T(8,128)S(1)}, u32[]{:S(2)}, u32[]{:S(2)}) collective-permute-start(f32[1024,128]{1,0:T(8,128)S(1)} %get-tuple-element.31.own_ref), channel_id=1, source_target_pairs={{0,8},{1,9},{2,10},{3,11},{4,12},{5,13},{6,14},{7,15},{8,0},{9,1},... | collective-permute-start | bytes 1572872 | tf_op jit(solution)/shard_map/ppermute | solution.py:395
  11.6 11.8 %collective-permute-start.5 = (f32[2,128,1024]{2,1,0:T(8,128)S(1)}, f32[2,128,1024]{2,1,0:T(8,128)S(1)}, u32[]{:S(2)}, u32[]{:S(2)}) collective-permute-start(f32[2,128,1024]{2,1,0:T(8,128)S(1)} %get-tuple-element.30.own_ref), channel_id=1, source_target_pairs={{0,1},{1,0},{2,3},{3,2},{4,5},{5,4},{6,7},{7,6},{8,9},{9,8},{10,11... | collective-permute-start | bytes 3145736 | tf_op jit(solution)/shard_map/ppermute | solution.py:395
  11.6 9.3 %collective-permute-start.4 = (f32[256,128]{1,0:T(8,128)S(1)}, f32[256,128]{1,0:T(8,128)S(1)}, u32[]{:S(2)}, u32[]{:S(2)}) collective-permute-start(f32[256,128]{1,0:T(8,128)S(1)} %get-tuple-element.28.dep_ref.a), channel_id=1, source_target_pairs={{0,6},{1,7},{2,4},{3,5},{4,2},{5,3},{6,0},{7,1},{8,14},{9,15},{10,... | collective-permute-start | bytes 393224 | tf_op jit(solution)/shard_map/ppermute | solution.py:395
  14.6 7.8 %collective-permute-start.3 = (f32[256,128]{1,0:T(8,128)S(1)}, f32[256,128]{1,0:T(8,128)S(1)}, u32[]{:S(2)}, u32[]{:S(2)}) collective-permute-start(f32[256,128]{1,0:T(8,128)S(1)} %get-tuple-element.28.dep_ref.a), channel_id=1, source_target_pairs={{0,4},{1,5},{2,6},{3,7},{4,0},{5,1},{6,2},{7,3},{8,12},{9,13},{10,... | collective-permute-start | bytes 393224 | tf_op jit(solution)/shard_map/ppermute | solution.py:395
  15.2 7.2 %collective-permute-start.2 = (f32[256,128]{1,0:T(8,128)S(1)}, f32[256,128]{1,0:T(8,128)S(1)}, u32[]{:S(2)}, u32[]{:S(2)}) collective-permute-start(f32[256,128]{1,0:T(8,128)S(1)} %get-tuple-element.28.dep_ref.a), channel_id=1, source_target_pairs={{0,2},{1,3},{2,0},{3,1},{4,6},{5,7},{6,4},{7,5},{8,10},{9,11},{10,... | collective-permute-start | bytes 393224 | tf_op jit(solution)/shard_map/ppermute | solution.py:395
  23.3 2.0 %collective-permute-start.7 = (f32[1024,128]{1,0:T(8,128)S(1)}, f32[1024,128]{1,0:T(8,128)S(1)}, u32[]{:S(2)}, u32[]{:S(2)}) collective-permute-start(f32[1024,128]{1,0:T(8,128)S(1)} %odd.1.t_own), channel_id=1, source_target_pairs={{0,1},{1,0},{2,3},{3,2},{4,5},{5,4},{6,7},{7,6},{8,9},{9,8},{10,11... | collective-permute-start | bytes 1572872 | tf_op jit(solution)/shard_map/ppermute | solution.py:395
  26.6 8.9 %collective-permute-start.10 = (f32[256,128]{1,0:T(8,128)S(1)}, f32[256,128]{1,0:T(8,128)S(1)}, u32[]{:S(2)}, u32[]{:S(2)}) collective-permute-start(f32[256,128]{1,0:T(8,128)S(1)} %get-tuple-element.33.dep_ref.a), channel_id=1, source_target_pairs={{0,6},{1,7},{2,4},{3,5},{4,2},{5,3},{6,0},{7,1},{8,14},{9,15},{10,... | collective-permute-start | bytes 393224 | tf_op jit(solution)/shard_map/ppermute | solution.py:395
  29.6 7.9 %collective-permute-start.9 = (f32[256,128]{1,0:T(8,128)S(1)}, f32[256,128]{1,0:T(8,128)S(1)}, u32[]{:S(2)}, u32[]{:S(2)}) collective-permute-start(f32[256,128]{1,0:T(8,128)S(1)} %get-tuple-element.33.dep_ref.a), channel_id=1, source_target_pairs={{0,4},{1,5},{2,6},{3,7},{4,0},{5,1},{6,2},{7,3},{8,12},{9,13},{10,... | collective-permute-start | bytes 393224 | tf_op jit(solution)/shard_map/ppermute | solution.py:395
  30.2 7.3 %collective-permute-start.8 = (f32[256,128]{1,0:T(8,128)S(1)}, f32[256,128]{1,0:T(8,128)S(1)}, u32[]{:S(2)}, u32[]{:S(2)}) collective-permute-start(f32[256,128]{1,0:T(8,128)S(1)} %get-tuple-element.33.dep_ref.a), channel_id=1, source_target_pairs={{0,2},{1,3},{2,0},{3,1},{4,6},{5,7},{6,4},{7,5},{8,10},{9,11},{10,... | collective-permute-start | bytes 393224 | tf_op jit(solution)/shard_map/ppermute | solution.py:395
  38.2 1.3 %collective-permute-start.11 = (f32[128,128]{1,0:T(8,128)S(1)}, f32[128,128]{1,0:T(8,128)S(1)}, u32[]{:S(2)}, u32[]{:S(2)}) collective-permute-start(f32[128,128]{1,0:T(8,128)S(1)} %get-tuple-element.37), channel_id=1, source_target_pairs={{0,1},{1,0},{2,3},{3,2},{4,5},{5,4},{6,7},{7,6},{8,9},{9,8},{10,11... | collective-permute-start | bytes 196616 | tf_op jit(solution)/shard_map/ppermute | solution.py:395
  39.6 5.7 %collective-permute-start.14 = (f32[128,128]{1,0:T(8,128)S(1)}, f32[128,128]{1,0:T(8,128)S(1)}, u32[]{:S(2)}, u32[]{:S(2)}) collective-permute-start(f32[128,128]{1,0:T(8,128)S(1)} %merge.1.a), channel_id=1, source_target_pairs={{0,96},{1,97},{2,98},{3,99},{4,100},{5,101},{6,102},{7,103},{8,104... | collective-permute-start | bytes 196616 | tf_op jit(solution)/shard_map/ppermute | solution.py:395
  42.4 6.1 %collective-permute-start.13 = (f32[128,128]{1,0:T(8,128)S(1)}, f32[128,128]{1,0:T(8,128)S(1)}, u32[]{:S(2)}, u32[]{:S(2)}) collective-permute-start(f32[128,128]{1,0:T(8,128)S(1)} %merge.1.a), channel_id=1, source_target_pairs={{0,64},{1,65},{2,66},{3,67},{4,68},{5,69},{6,70},{7,71},{8,72},{9,... | collective-permute-start | bytes 196616 | tf_op jit(solution)/shard_map/ppermute | solution.py:395
  43.2 5.3 %collective-permute-start.12 = (f32[128,128]{1,0:T(8,128)S(1)}, f32[128,128]{1,0:T(8,128)S(1)}, u32[]{:S(2)}, u32[]{:S(2)}) collective-permute-start(f32[128,128]{1,0:T(8,128)S(1)} %merge.1.a), channel_id=1, source_target_pairs={{0,32},{1,33},{2,34},{3,35},{4,36},{5,37},{6,38},{7,39},{8,40},{9,... | collective-permute-start | bytes 196616 | tf_op jit(solution)/shard_map/ppermute | solution.py:395
  48.5 6.3 %collective-permute-start.17 = (f32[128,128]{1,0:T(8,128)S(1)}, f32[128,128]{1,0:T(8,128)S(1)}, u32[]{:S(2)}, u32[]{:S(2)}) collective-permute-start(f32[128,128]{1,0:T(8,128)S(1)} %choose.1.a), channel_id=1, source_target_pairs={{0,24},{1,25},{2,26},{3,27},{4,28},{5,29},{6,30},{7,31},{8,16},{9,... | collective-permute-start | bytes 196616 | tf_op jit(solution)/shard_map/ppermute | solution.py:395
  52.3 5.8 %collective-permute-start.16 = (f32[128,128]{1,0:T(8,128)S(1)}, f32[128,128]{1,0:T(8,128)S(1)}, u32[]{:S(2)}, u32[]{:S(2)}) collective-permute-start(f32[128,128]{1,0:T(8,128)S(1)} %choose.1.a), channel_id=1, source_target_pairs={{0,16},{1,17},{2,18},{3,19},{4,20},{5,21},{6,22},{7,23},{8,24},{9,... | collective-permute-start | bytes 196616 | tf_op jit(solution)/shard_map/ppermute | solution.py:395
  52.3 5.8 %collective-permute-start.15 = (f32[128,128]{1,0:T(8,128)S(1)}, f32[128,128]{1,0:T(8,128)S(1)}, u32[]{:S(2)}, u32[]{:S(2)}) collective-permute-start(f32[128,128]{1,0:T(8,128)S(1)} %choose.1.a), channel_id=1, source_target_pairs={{0,8},{1,9},{2,10},{3,11},{4,12},{5,13},{6,14},{7,15},{8,0},{9,1},... | collective-permute-start | bytes 196616 | tf_op jit(solution)/shard_map/ppermute | solution.py:395

commit v4 on v3

v4 whole, which is shorter than its diff:
```python
import functools

import jax
import jax.numpy as jnp
from jax import lax
from jax.experimental import pallas as pl
from jax.experimental.pallas import tpu as pltpu
from jax.sharding import PartitionSpec as P

F32 = jnp.float32
BF16 = jnp.bfloat16
NZ = 4
W = 128
NB = 1024
PACK = NB // 4
VMEM = pl.BlockSpec(memory_space=pltpu.VMEM)
ANY = pl.BlockSpec(memory_space=pl.ANY)


def in_vmem(x):
    return pltpu.with_memory_space_constraint(x, pltpu.VMEM)


def in_hbm(x):
    return pltpu.with_memory_space_constraint(x, pltpu.HBM)


def vm(shape, dtype=F32):
    return pltpu.VMEM(shape, dtype)


PACKED = vm((PACK, W))


def call(kernel, name, out, hbm=(), vmem=(), deps=(), scratch=(), mib=4, out_specs=None, mb=None, aliases={}):
    return pl.pallas_call(
        kernel,
        out_shape=out,
        in_specs=[ANY] * len(hbm) + [VMEM] * len(vmem) + [ANY] * len(deps),
        out_specs=out_specs or (VMEM,) * len(out),
        scratch_shapes=scratch,
        compiler_params=pltpu.CompilerParams(vmem_limit_bytes=mib * 2**20),
        input_output_aliases=aliases,
        cost_estimate=mb and pl.CostEstimate(flops=0, bytes_accessed=mb * 2**20, transcendentals=0),
        name=name,
    )(*[in_hbm(v) for v in hbm], *[in_vmem(v) for v in vmem], *deps)


def split(x):
    hi = x.astype(BF16)
    return hi, (x - hi.astype(F32)).astype(BF16)


def dot(a, b):
    return jnp.dot(a, b, preferred_element_type=F32)


def pair_of(b):
    bh, bl = split(b)
    return jnp.concatenate([bh, bl], axis=1)


def lhs_of(*blocks):
    parts = [split(b) for b in blocks]
    return jnp.concatenate([hi for hi, _ in parts] + [lo for _, lo in parts], axis=0)


def dot3(lhs, both):
    n = lhs.shape[0] // 2
    prod = dot(lhs, both)
    return prod[:n, :W] + (prod[:n, W:] + prod[n:, :W])


def core():
    return lax.rem(lax.axis_index("col"), 2)


def chip():
    return lax.axis_index("col") // 2


def side():
    return lax.rem(core() + chip() + odd_row(), 2)


def odd_row():
    return lax.rem(lax.axis_index("row"), 2)


def lane_group(shape):
    return lax.broadcasted_iota(jnp.int32, shape, 1) // 32


def on_chain(kernel):
    @functools.wraps(kernel)
    def gated(*refs):
        @pl.when(lax.axis_index("row") < 2)
        def _():
            kernel(*refs)

    return gated


def pack(src, b):
    out = None
    for g in range(4):
        rows = src[PACK * g : PACK * (g + 1)]
        shift = 32 * ((g - b) % 4)
        rows = pltpu.roll(rows, shift, 1) if shift else rows
        out = rows if out is None else jnp.where(lane_group(rows.shape) == g, rows, out)
    return out


def unpack(p):
    out = []
    for g in range(4):
        m = jnp.where(lane_group(p.shape) == g, p, 0.0)
        m = m + pltpu.roll(m, 32, 1)
        out.append(m + pltpu.roll(m, 64, 1))
    return jnp.concatenate(out, axis=0)


@on_chain
def start_kernel(p_ref, panel_ref, send_ref, keep_ref, tile_ref, p_buf, t_buf, q_buf, sem):
    h = side()
    one = pltpu.make_async_copy(p_ref.at[0], p_buf, sem.at[0])
    two = pltpu.make_async_copy(panel_ref.at[0], t_buf, sem.at[1])
    one.start()
    two.start()
    one.wait()
    for b in range(4):
        q_buf[b] = pack(p_buf, b)
    for r in range(2):
        keep_ref[r] = q_buf[2 * r + h]
        send_ref[r] = q_buf[2 * r + 1 - h]
    two.wait()
    tile_ref[...] = t_buf[pl.ds(0, NB, stride=2), :]


def start(partials, panel):
    return call(
        start_kernel,
        "start",
        (vm((2, PACK, W)), vm((2, PACK, W)), vm((NB, W))),
        hbm=(partials, panel),
        scratch=[
            pltpu.VMEM((NB, W), F32),
            pltpu.VMEM((2 * NB, W), F32),
            pltpu.VMEM((4, PACK, W), F32),
            pltpu.SemaphoreType.DMA((2,)),
        ],
    )


@on_chain
def prep_kernel(inv_ref, rhs_ref, dep_ref, inv_out, rhs_out, r_buf, q_buf, sem):
    one = pltpu.make_async_copy(rhs_ref, r_buf, sem.at[0])
    two = pltpu.make_async_copy(inv_ref, inv_out, sem.at[1])
    one.start()
    two.start()
    one.wait()
    b = 2 * odd_row() + side()
    for k in range(2):
        for at in range(4):
            q_buf[at] = pack(r_buf.at[k], at)
        rhs_out[k] = q_buf[b]
    two.wait()


def prep(inverse, rhs, dep):
    return call(
        prep_kernel,
        "prep",
        (vm((2, W, NB)), vm((2, PACK, W))),
        hbm=(inverse, rhs),
        deps=(dep,),
        scratch=[
            pltpu.VMEM((2, NB, W), F32),
            pltpu.VMEM((4, PACK, W), F32),
            pltpu.SemaphoreType.DMA((2,)),
        ],
        mb=8,
    )


@on_chain
def add_kernel(a_ref, b_ref, mine_ref, other_ref):
    r = odd_row()
    mine_ref[...] = a_ref[r] + b_ref[r]
    other_ref[...] = a_ref[1 - r] + b_ref[1 - r]


def add(a, b):
    return call(add_kernel, "add", (PACKED, PACKED), vmem=(a, b))


@on_chain
def order_kernel(mine_ref, got_ref, _, even_ref, odd_ref, same_ref):
    r = odd_row()

    @pl.when(r == 0)
    def _():
        even_ref[...] = mine_ref[...]
        odd_ref[...] = got_ref[...]

    @pl.when(r == 1)
    def _():
        even_ref[...] = got_ref[...]
        odd_ref[...] = mine_ref[...]


def order(mine, got, inv):
    return call(
        order_kernel, "order", (PACKED, PACKED, vm(inv.shape)), vmem=(mine, got, inv), aliases={2: 2}
    )


@on_chain
def odd_kernel(own_ref, got_ref, dep0, dep1, dep2, dep3, out_ref):
    r = odd_row()

    @pl.when(r == 1)
    def _():
        out_ref[...] = own_ref[...]

    @pl.when(r == 0)
    def _():
        out_ref[...] = got_ref[...]


def odd_tile(own, got, deps):
    return call(odd_kernel, "odd", (vm((NB, W)),), vmem=(own, got), deps=deps)[0]


@on_chain
def first_kernel(rhs_ref, a, b, c, d, odd_ref, own_ref, got_ref, t_a, t_b, y_ref, u_ref):
    total = (a[...] + b[...]) + (c[...] + d[...])
    y = dot3(lhs_of(own_ref[0], got_ref[0]), pair_of(unpack(rhs_ref[0] - total)))
    y_ref[0] = y[:W]
    y_ref[1] = y[W:]
    both = pair_of(jnp.where(odd_row() == 1, y, jnp.concatenate([y[W:], y[:W]], axis=0)))
    out = odd_ref[...]
    group = lane_group(out.shape)
    for g in range(4):
        rows = pl.ds(PACK * g, PACK)
        hi, lo = split(jnp.concatenate([t_a[rows, :], t_b[rows, :]], axis=1))
        prod = dot(hi, both)
        u = prod[:, :W] + (prod[:, W:] + dot(lo, both[:, :W]))
        out = jnp.where(group == g, out + u, out)
    u_ref[...] = out


def first(rhs, sums, odd, own, got, t_a, t_b):
    return call(
        first_kernel,
        "first",
        (vm((2, W, W)), PACKED),
        vmem=(rhs, *sums, odd, own, got, t_a, t_b),
        mib=8,
    )


@on_chain
def second_kernel(rhs_ref, a, b, c, d, own_ref, got_ref, y_ref, dep_ref, out_ref):
    total = (a[...] + b[...]) + (c[...] + d[...])
    y = dot3(lhs_of(own_ref[1], got_ref[1]), pair_of(unpack(rhs_ref[1] - total)))
    group = lane_group((W, W))
    own = jnp.where(group < 2, y_ref[0], y[:W])
    got = jnp.where(group < 2, y_ref[1], y[W:])
    out_ref[...] = jnp.where(group % 2 == core(), own, got)


def second(rhs, sums, own, got, y0, dep):
    return call(
        second_kernel, "second", (vm((W, W)),), vmem=(rhs, *sums, own, got, y0), deps=(dep,), mib=8
    )[0]


def choose_kernel(a, b, c, d, out_ref):
    x = lax.axis_index("row") // NZ
    for m, got in enumerate((a, b, c, d)):

        @pl.when(x == m)
        def _():
            out_ref[...] = got[...]


def choose(got):
    return call(choose_kernel, "choose", (vm((W, W)),), vmem=got)[0]


GROUP = 4


def parts_kernel(group, panel_ref, p_ref, dep_ref, hi_ref, lo_ref, part_ref, buf, sem):
    bring = pltpu.make_async_copy(p_ref.at[pl.ds(group * GROUP, GROUP)], part_ref, sem.at[GROUP])
    copies = [
        pltpu.make_async_copy(panel_ref.at[group * GROUP + l], buf.at[l], sem.at[l]) for l in range(GROUP)
    ]
    for c in copies:
        c.start()
    bring.start()
    for l in range(GROUP):
        copies[l].wait()
        for k in range(2):
            hi, lo = split(buf[l, pl.ds(k, NB, stride=2), :])
            hi_ref[l, :, k * W : (k + 1) * W] = hi
            lo_ref[l, :, k * W : (k + 1) * W] = lo
    bring.wait()


def parts(group, panel, partials, dep):
    out = vm((GROUP, NB, 2 * W), BF16)
    return call(
        functools.partial(parts_kernel, group),
        "parts",
        (out, out, vm((GROUP, NB, W))),
        hbm=(panel, partials),
        deps=(dep,),
        scratch=[pltpu.VMEM((GROUP, 2 * NB, W), F32), pltpu.SemaphoreType.DMA((GROUP + 1,))],
        mib=6,
        mb=12,
    )


def deal_kernel(a, b, c, d, keep_ref, send_ref, sides):
    z = lax.rem(lax.axis_index("row"), NZ)
    for m, got in enumerate((a, b, c, d)):

        @pl.when(z == m)
        def _():
            sides[0] = got[...]

        @pl.when(z == m ^ 1)
        def _():
            sides[1] = got[...]

    left, right = sides[0], sides[1]
    group = lane_group((W, W))

    def lanes(parts):
        (p, i), (q, j), (r, k), (t, n) = parts
        turn = lambda v, shift: pltpu.roll(v, shift, 1) if shift else v
        low = jnp.where(group == 0, turn(p, i), turn(q, j))
        return jnp.where(group < 2, low, jnp.where(group == 2, turn(r, k), turn(t, n)))

    zero = lanes(((left, 0), (left, 96), (right, 64), (right, 32)))
    one = lanes(((left, 96), (left, 64), (right, 32), (right, 0)))
    h = core()
    keep_ref[...] = jnp.where(h == 0, zero, one)
    send_ref[...] = jnp.where(h == 0, one, zero)


def deal(got):
    return call(
        deal_kernel, "deal", (vm((W, W)), vm((W, W))), vmem=got, scratch=[pltpu.VMEM((2, W, W), F32)]
    )


def update_kernel(keep_ref, got_ref, ph0, pl0, part0, ph1, pl1, part1, out_ref, solved_ref, buf, sem):
    row = lax.axis_index("row")
    x, z = row // NZ, lax.rem(row, NZ)
    way = core() + chip() + jnp.where(x == 0, 0, 1)
    left = lax.rem(way + jnp.where(z == 0, 0, 1), 2)
    right = lax.rem(way + jnp.where(z == 1, 0, 1) + 1, 2)
    group = lane_group((W, W))
    mine = group == jnp.where(group < 2, left, 2 + right)
    keep, got = keep_ref[...], got_ref[...]
    even = group % 2 == 0

    def block(k):
        if k == 0:
            spread = lambda v: jnp.where(even, v, pltpu.roll(v, 32, 1))
        else:
            spread = lambda v: jnp.where(even, pltpu.roll(v, 96, 1), v)
        return jnp.where(mine, spread(keep), spread(got))

    y0, y1 = block(0), block(1)
    solved_ref[0] = y0
    solved_ref[1] = y1
    head = pair_of(jnp.concatenate([jnp.where(row > 0, y0, 0.0), jnp.where(row > 1, y1, 0.0)], axis=0))
    rest = pair_of(jnp.concatenate([y0, y1], axis=0))

    def copy(l):
        return pltpu.make_async_copy(buf.at[l], out_ref.at[l], sem.at[l])

    for l in range(8):
        hi, lo, part = ((ph0, pl0, part0), (ph1, pl1, part1))[l // GROUP]
        w = head if l == 0 else rest
        prod = dot(hi[l % GROUP], w)
        low = dot(lo[l % GROUP], w[:, :W])
        buf[l] = part[l % GROUP] + (prod[:, :W] + (prod[:, W:] + low))
        copy(l).start()
    for l in range(8):
        copy(l).wait()


def update(keep, got, parts0, parts1):
    return call(
        update_kernel,
        "update",
        (jax.ShapeDtypeStruct((8, NB, W), F32), jax.ShapeDtypeStruct((2, W, W), F32)),
        vmem=(keep, got, *parts0, *parts1),
        out_specs=(ANY, VMEM),
        scratch=[
            pltpu.VMEM((8, NB, W), F32),
            pltpu.SemaphoreType.DMA((8,)),
        ],
        mib=10,
    )


def exchange(x, row_mask, col_mask):
    pairs = [(r * 8 + c, (r ^ row_mask) * 8 + (c ^ col_mask)) for r in range(16) for c in range(8)]
    return lax.ppermute(x, ("row", "col"), pairs)


def swap(x):
    return exchange(x, 0, 1)


def chips(x):
    return [x] + [exchange(x, 0, mask) for mask in (3, 4, 7)]


def rows_over(y, step):
    return [y] + [exchange(y, step * m, 1) for m in (1, 2, 3)]


def per_device(partials, panel, inverse, rhs):
    partials = partials.reshape(8, NB, W)
    panel = panel.reshape(8, 2 * NB, W)
    send, keep, tile = start(partials, panel)
    tile_odd = exchange(tile, 1, 1)
    mine, other = add(keep, swap(send))
    inv, rhs = prep(inverse, rhs, mine)
    even, odd, inv = order(mine, exchange(other, 1, 1), inv)
    inv_got = swap(inv)
    parts0 = parts(0, panel, partials, even)
    sums = chips(even)
    tile = odd_tile(tile, tile_odd, (*sums[1:], parts0[0]))
    y0, u = first(rhs, sums, odd, inv, inv_got, tile, swap(tile))
    parts1 = parts(1, panel, partials, u)
    y = second(rhs, chips(u), inv, inv_got, y0, parts1[0])
    keep, send = deal(rows_over(choose(rows_over(y, NZ)), 1))
    new, solved = update(keep, swap(send), parts0, parts1)
    return new[None, :, None], solved


def solution(mesh):
    return jax.shard_map(
        per_device,
        mesh=mesh,
        in_specs=(
            P("col", None, "row", None, None),
            P(None, "row", None, None, "col"),
            P(None, "col", None),
            P(),
        ),
        out_specs=(P("col", None, "row", None, None), P(None, "col", None)),
        check_vma=False,
    )
```

time: 63.4 us -> 57.3 us (0.904)
  the two profiles are of different devices: /device:TPU:0 before, /device:TPU:1 now
where the time goes in v4:
time: 57.3 us; the launch traced here: 57.1 us
  waiting for transfers between devices  20.4 us (36%)
  starting transfers between devices  19.9 us (35%)
  Pallas kernels  16 us (28%)
  between operations  0.75 us (1%)
    ppermute x18, waiting for transfers between devices, exchange(): return lax.ppermute(x, ('row', 'col'), pairs)  20.4 us
    ppermute x18, starting transfers between devices, exchange(): return lax.ppermute(x, ('row', 'col'), pairs)  19.9 us
    pallas_call x12, Pallas kernels, call(): pl.pallas_call(kernel, out_shape=out, in_specs=[ANY] * len(hbm) + [VMEM]...  16 us
  transfers between devices with their start and end apart: 18, of which 12 were waited for; matrix products, arithmetic and copies ran while one was open for 0% of the time, Pallas kernels for 14%

profile of v4, /device:TPU:1, one launch (start us, length us, event | category | flops | bytes accessed | tf_op | source)
XLA Modules:
  0.0 57.1 jit_solution(12120578478451268137)
XLA Ops:
  0.6 1.7 %start.1 = (f32[2,256,128]{2,1,0:T(8,128)S(1)}, f32[2,256,128]{2,1,0:T(8,128)S(1)}, f32[1024,128]{1,0:T(8,128)S(1)}) custom-call(f32[8,1024,128]{2,1,0:T(8,128)} %bitcast.8, f32[8,2048,128]{2,1,0:T(8,128)} %bitcast.5), custom_call_target="tpu_custom_call" | custom-call | tf_op jit(solution)/shard_map/start/pallas_call | solution.py:36
  2.3 1.5 %collective-permute-start = (f32[2,256,128]{2,1,0:T(8,128)S(1)}, f32[2,256,128]{2,1,0:T(8,128)S(1)}, u32[]{:S(2)}, u32[]{:S(2)}) collective-permute-start(f32[2,256,128]{2,1,0:T(8,128)S(1)} %get-tuple-element.25), channel_id=1, source_target_pairs={{0,1},{1,0},{2,3},{3,2},{4,5},{5,4},{6,7},{7,6},{8,9},{9,8},{10,11... | collective-permute-start | bytes 786440 | tf_op jit(solution)/shard_map/ppermute | solution.py:415
  3.8 1.2 %collective-permute-done.b_ref = f32[2,256,128]{2,1,0:T(8,128)S(1)} collective-permute-done((f32[2,256,128]{2,1,0:T(8,128)S(1)}, f32[2,256,128]{2,1,0:T(8,128)S(1)}, u32[]{:S(2)}, u32[]{:S(2)}) %collective-permute-start) | collective-permute-done | bytes 262176 | tf_op jit(solution)/shard_map/ppermute | solution.py:415
  5.0 2.1 %collective-permute-start.1 = (f32[256,128]{1,0:T(8,128)S(1)}, f32[256,128]{1,0:T(8,128)S(1)}, u32[]{:S(2)}, u32[]{:S(2)}) collective-permute-start(f32[256,128]{1,0:T(8,128)S(1)} %get-tuple-element.28), channel_id=1, source_target_pairs={{0,9},{1,8},{2,11},{3,10},{4,13},{5,12},{6,15},{7,14},{8,1},{9,0},... | collective-permute-start | bytes 393224 | tf_op jit(solution)/shard_map/ppermute | solution.py:415
  7.1 2.1 %prep.1 = (f32[2,128,1024]{2,1,0:T(8,128)S(1)}, f32[2,256,128]{2,1,0:T(8,128)S(1)}) custom-call(f32[2,128,1024]{2,1,0:T(8,128)} %inv_ref.1, f32[2,1024,128]{2,1,0:T(8,128)} %rhs_ref.1, f32[256,128]{1,0:T(8,128)S(1)} %get-tuple-element.26.dep_ref.mine_ref), custom_call_target="tpu_custom_call" | custom-call | bytes 8388608 | tf_op jit(solution)/shard_map/prep/pallas_call | solution.py:36
  9.3 2.0 %collective-permute-done.1.got_ref = f32[256,128]{1,0:T(8,128)S(1)} collective-permute-done((f32[256,128]{1,0:T(8,128)S(1)}, f32[256,128]{1,0:T(8,128)S(1)}, u32[]{:S(2)}, u32[]{:S(2)}) %collective-permute-start.1) | collective-permute-done | bytes 131104 | tf_op jit(solution)/shard_map/ppermute | solution.py:415
  11.4 3.1 %collective-permute-start.4 = (f32[256,128]{1,0:T(8,128)S(1)}, f32[256,128]{1,0:T(8,128)S(1)}, u32[]{:S(2)}, u32[]{:S(2)}) collective-permute-start(f32[256,128]{1,0:T(8,128)S(1)} %get-tuple-element.30.dep_ref.a), channel_id=1, source_target_pairs={{0,7},{1,6},{2,5},{3,4},{4,3},{5,2},{6,1},{7,0},{8,15},{9,14},{10,... | collective-permute-start | bytes 393224 | tf_op jit(solution)/shard_map/ppermute | solution.py:415
  14.6 0.4 collective-permute-start.3
  14.9 0.5 collective-permute-start.2
  15.4 2.9 %parts.2 = (bf16[4,1024,256]{2,1,0:T(8,128)(2,1)S(1)}, bf16[4,1024,256]{2,1,0:T(8,128)(2,1)S(1)}, f32[4,1024,128]{2,1,0:T(8,128)S(1)}) custom-call(f32[8,2048,128]{2,1,0:T(8,128)} %bitcast.6, f32[8,1024,128]{2,1,0:T(8,128)} %bitcast.9, f32[256,128]{1,0:T(8,128)S(1)} %get-tuple-element.30.dep_ref.a), custom_call_target="tpu_custom_call" | custom-call | bytes 12582912 | tf_op jit(solution)/shard_map/parts/pallas_call | solution.py:36
  18.3 3.7 %collective-permute-done.6.got_ref = f32[1024,128]{1,0:T(8,128)S(1)} collective-permute-done((f32[1024,128]{1,0:T(8,128)S(1)}, f32[1024,128]{1,0:T(8,128)S(1)}, u32[]{:S(2)}, u32[]{:S(2)}) %collective-permute-start.6) | collective-permute-done | bytes 524320 | tf_op jit(solution)/shard_map/ppermute | solution.py:415
  22.1 0.4 collective-permute-start.7
  22.6 1.5 %collective-permute-done.7.t_b = f32[1024,128]{1,0:T(8,128)S(1)} collective-permute-done((f32[1024,128]{1,0:T(8,128)S(1)}, f32[1024,128]{1,0:T(8,128)S(1)}, u32[]{:S(2)}, u32[]{:S(2)}) %collective-permute-start.7) | collective-permute-done | bytes 524320 | tf_op jit(solution)/shard_map/ppermute | solution.py:415
  24.1 1.5 %first.1 = (f32[2,128,128]{2,1,0:T(8,128)S(1)}, f32[256,128]{1,0:T(8,128)S(1)}) custom-call(f32[2,256,128]{2,1,0:T(8,128)S(1)} %get-tuple-element.27.rhs_ref, f32[256,128]{1,0:T(8,128)S(1)} %get-tuple-element.30.dep_ref.a, f32[256,128]{1,0:T(8,128)S(1)} %collective-permute-done.2.dep0.b, f32[256,128]{1,0:T(8,128)S(1)} %collective-permute-done.3.dep1.c, ...), custom_call_target="tpu_custom_call" | custom-call | tf_op jit(solution)/shard_map/first/pallas_call | solution.py:36
  25.7 2.8 %collective-permute-start.10 = (f32[256,128]{1,0:T(8,128)S(1)}, f32[256,128]{1,0:T(8,128)S(1)}, u32[]{:S(2)}, u32[]{:S(2)}) collective-permute-start(f32[256,128]{1,0:T(8,128)S(1)} %get-tuple-element.35.dep_ref.a), channel_id=1, source_target_pairs={{0,7},{1,6},{2,5},{3,4},{4,3},{5,2},{6,1},{7,0},{8,15},{9,14},{10,... | collective-permute-start | bytes 393224 | tf_op jit(solution)/shard_map/ppermute | solution.py:415
  28.5 0.3 collective-permute-start.9
  28.8 0.8 %collective-permute-start.8 = (f32[256,128]{1,0:T(8,128)S(1)}, f32[256,128]{1,0:T(8,128)S(1)}, u32[]{:S(2)}, u32[]{:S(2)}) collective-permute-start(f32[256,128]{1,0:T(8,128)S(1)} %get-tuple-element.35.dep_ref.a), channel_id=1, source_target_pairs={{0,3},{1,2},{2,1},{3,0},{4,7},{5,6},{6,5},{7,4},{8,11},{9,10},{10,... | collective-permute-start | bytes 393224 | tf_op jit(solution)/shard_map/ppermute | solution.py:415
  29.6 2.9 %parts.3 = (bf16[4,1024,256]{2,1,0:T(8,128)(2,1)S(1)}, bf16[4,1024,256]{2,1,0:T(8,128)(2,1)S(1)}, f32[4,1024,128]{2,1,0:T(8,128)S(1)}) custom-call(f32[8,2048,128]{2,1,0:T(8,128)} %bitcast.7, f32[8,1024,128]{2,1,0:T(8,128)} %bitcast.10, f32[256,128]{1,0:T(8,128)S(1)} %get-tuple-element.35.dep_ref.a), custom_call_target="tpu_custom_call" | custom-call | bytes 12582912 | tf_op jit(solution)/shard_map/parts/pallas_call | solution.py:36
  32.5 1.6 %collective-permute-done.10.d = f32[256,128]{1,0:T(8,128)S(1)} collective-permute-done((f32[256,128]{1,0:T(8,128)S(1)}, f32[256,128]{1,0:T(8,128)S(1)}, u32[]{:S(2)}, u32[]{:S(2)}) %collective-permute-start.10) | collective-permute-done | bytes 131104 | tf_op jit(solution)/shard_map/ppermute | solution.py:415
  34.1 0.7 %collective-permute-done.9.c = f32[256,128]{1,0:T(8,128)S(1)} collective-permute-done((f32[256,128]{1,0:T(8,128)S(1)}, f32[256,128]{1,0:T(8,128)S(1)}, u32[]{:S(2)}, u32[]{:S(2)}) %collective-permute-start.9) | collective-permute-done | bytes 131104 | tf_op jit(solution)/shard_map/ppermute | solution.py:415
  34.9 1.3 %collective-permute-done.8.b = f32[256,128]{1,0:T(8,128)S(1)} collective-permute-done((f32[256,128]{1,0:T(8,128)S(1)}, f32[256,128]{1,0:T(8,128)S(1)}, u32[]{:S(2)}, u32[]{:S(2)}) %collective-permute-start.8) | collective-permute-done | bytes 131104 | tf_op jit(solution)/shard_map/ppermute | solution.py:415
  36.1 0.6 %second.1.a = f32[128,128]{1,0:T(8,128)S(1)} custom-call(f32[2,256,128]{2,1,0:T(8,128)S(1)} %get-tuple-element.27.rhs_ref, f32[256,128]{1,0:T(8,128)S(1)} %get-tuple-element.35.dep_ref.a, f32[256,128]{1,0:T(8,128)S(1)} %collective-permute-done.8.b, f32[256,128]{1,0:T(8,128)S(1)} %collective-permute-done.9.c, f32[256,128]{1,0:T(8,128)S(1)} %collective-permute-done.10.d, ...), custom_call_target="tpu_custom_call" | custom-call | tf_op jit(solution)/shard_map/second/pallas_call | solution.py:36
  36.9 3.7 %collective-permute-start.11 = (f32[128,128]{1,0:T(8,128)S(1)}, f32[128,128]{1,0:T(8,128)S(1)}, u32[]{:S(2)}, u32[]{:S(2)}) collective-permute-start(f32[128,128]{1,0:T(8,128)S(1)} %second.1.a), channel_id=1, source_target_pairs={{0,33},{1,32},{2,35},{3,34},{4,37},{5,36},{6,39},{7,38},{8,41},{9,... | collective-permute-start | bytes 196616 | tf_op jit(solution)/shard_map/ppermute | solution.py:415
  40.7 2.9 %collective-permute-done.13.d = f32[128,128]{1,0:T(8,128)S(1)} collective-permute-done((f32[128,128]{1,0:T(8,128)S(1)}, f32[128,128]{1,0:T(8,128)S(1)}, u32[]{:S(2)}, u32[]{:S(2)}) %collective-permute-start.13) | collective-permute-done | bytes 65568 | tf_op jit(solution)/shard_map/ppermute | solution.py:415
  43.6 0.6 collective-permute-done.11.b
  44.1 0.3 collective-permute-start.16
  44.4 3.4 %collective-permute-start.15 = (f32[128,128]{1,0:T(8,128)S(1)}, f32[128,128]{1,0:T(8,128)S(1)}, u32[]{:S(2)}, u32[]{:S(2)}) collective-permute-start(f32[128,128]{1,0:T(8,128)S(1)} %choose.1.a), channel_id=1, source_target_pairs={{0,17},{1,16},{2,19},{3,18},{4,21},{5,20},{6,23},{7,22},{8,25},{9,... | collective-permute-start | bytes 196616 | tf_op jit(solution)/shard_map/ppermute | solution.py:415
  47.8 3.0 %collective-permute-done.16.d = f32[128,128]{1,0:T(8,128)S(1)} collective-permute-done((f32[128,128]{1,0:T(8,128)S(1)}, f32[128,128]{1,0:T(8,128)S(1)}, u32[]{:S(2)}, u32[]{:S(2)}) %collective-permute-start.16) | collective-permute-done | bytes 65568 | tf_op jit(solution)/shard_map/ppermute | solution.py:415
  50.8 0.9 %collective-permute-done.14.b = f32[128,128]{1,0:T(8,128)S(1)} collective-permute-done((f32[128,128]{1,0:T(8,128)S(1)}, f32[128,128]{1,0:T(8,128)S(1)}, u32[]{:S(2)}, u32[]{:S(2)}) %collective-permute-start.14) | collective-permute-done | bytes 65568 | tf_op jit(solution)/shard_map/ppermute | solution.py:415
  51.8 0.3 collective-permute-start.17
  52.1 1.0 %collective-permute-done.17.got_ref = f32[128,128]{1,0:T(8,128)S(1)} collective-permute-done((f32[128,128]{1,0:T(8,128)S(1)}, f32[128,128]{1,0:T(8,128)S(1)}, u32[]{:S(2)}, u32[]{:S(2)}) %collective-permute-start.17) | collective-permute-done | bytes 65568 | tf_op jit(solution)/shard_map/ppermute | solution.py:415
  53.2 4.0 %update.1 = (f32[8,1024,128]{2,1,0:T(8,128)}, f32[2,128,128]{2,1,0:T(8,128)}) custom-call(f32[128,128]{1,0:T(8,128)S(1)} %get-tuple-element.38.keep_ref, f32[128,128]{1,0:T(8,128)S(1)} %collective-permute-done.17.got_ref, bf16[4,1024,256]{2,1,0:T(8,128)(2,1)S(1)} %get-tuple-element.34.dep3.ph0, bf16[4,1024,256]{2,1,0:T(8,128)(2,1)S(1)} %get-tuple-element.40.pl0, ...), custom_call_target="tpu_custom_call" | custom-call | tf_op jit(solution)/shard_map/update/pallas_call | solution.py:36
  (16 shorter events, 0.6 us)
Async XLA Ops:
  2.3 2.7 %collective-permute-start = (f32[2,256,128]{2,1,0:T(8,128)S(1)}, f32[2,256,128]{2,1,0:T(8,128)S(1)}, u32[]{:S(2)}, u32[]{:S(2)}) collective-permute-start(f32[2,256,128]{2,1,0:T(8,128)S(1)} %get-tuple-element.25), channel_id=1, source_target_pairs={{0,1},{1,0},{2,3},{3,2},{4,5},{5,4},{6,7},{7,6},{8,9},{9,8},{10,11... | collective-permute-start | bytes 786440 | tf_op jit(solution)/shard_map/ppermute | solution.py:415
  5.0 6.3 %collective-permute-start.1 = (f32[256,128]{1,0:T(8,128)S(1)}, f32[256,128]{1,0:T(8,128)S(1)}, u32[]{:S(2)}, u32[]{:S(2)}) collective-permute-start(f32[256,128]{1,0:T(8,128)S(1)} %get-tuple-element.28), channel_id=1, source_target_pairs={{0,9},{1,8},{2,11},{3,10},{4,13},{5,12},{6,15},{7,14},{8,1},{9,0},... | collective-permute-start | bytes 393224 | tf_op jit(solution)/shard_map/ppermute | solution.py:415
  7.0 15.0 %collective-permute-start.6 = (f32[1024,128]{1,0:T(8,128)S(1)}, f32[1024,128]{1,0:T(8,128)S(1)}, u32[]{:S(2)}, u32[]{:S(2)}) collective-permute-start(f32[1024,128]{1,0:T(8,128)S(1)} %get-tuple-element.33.own_ref), channel_id=1, source_target_pairs={{0,9},{1,8},{2,11},{3,10},{4,13},{5,12},{6,15},{7,14},{8,1},{9,0},... | collective-permute-start | bytes 1572872 | tf_op jit(solution)/shard_map/ppermute | solution.py:415
  11.4 12.8 %collective-permute-start.5 = (f32[2,128,1024]{2,1,0:T(8,128)S(1)}, f32[2,128,1024]{2,1,0:T(8,128)S(1)}, u32[]{:S(2)}, u32[]{:S(2)}) collective-permute-start(f32[2,128,1024]{2,1,0:T(8,128)S(1)} %get-tuple-element.32.own_ref), channel_id=1, source_target_pairs={{0,1},{1,0},{2,3},{3,2},{4,5},{5,4},{6,7},{7,6},{8,9},{9,8},{10,11... | collective-permute-start | bytes 3145736 | tf_op jit(solution)/shard_map/ppermute | solution.py:415
  11.4 10.6 %collective-permute-start.4 = (f32[256,128]{1,0:T(8,128)S(1)}, f32[256,128]{1,0:T(8,128)S(1)}, u32[]{:S(2)}, u32[]{:S(2)}) collective-permute-start(f32[256,128]{1,0:T(8,128)S(1)} %get-tuple-element.30.dep_ref.a), channel_id=1, source_target_pairs={{0,7},{1,6},{2,5},{3,4},{4,3},{5,2},{6,1},{7,0},{8,15},{9,14},{10,... | collective-permute-start | bytes 393224 | tf_op jit(solution)/shard_map/ppermute | solution.py:415
  14.6 7.5 %collective-permute-start.3 = (f32[256,128]{1,0:T(8,128)S(1)}, f32[256,128]{1,0:T(8,128)S(1)}, u32[]{:S(2)}, u32[]{:S(2)}) collective-permute-start(f32[256,128]{1,0:T(8,128)S(1)} %get-tuple-element.30.dep_ref.a), channel_id=1, source_target_pairs={{0,4},{1,5},{2,6},{3,7},{4,0},{5,1},{6,2},{7,3},{8,12},{9,13},{10,... | collective-permute-start | bytes 393224 | tf_op jit(solution)/shard_map/ppermute | solution.py:415
  14.9 7.2 %collective-permute-start.2 = (f32[256,128]{1,0:T(8,128)S(1)}, f32[256,128]{1,0:T(8,128)S(1)}, u32[]{:S(2)}, u32[]{:S(2)}) collective-permute-start(f32[256,128]{1,0:T(8,128)S(1)} %get-tuple-element.30.dep_ref.a), channel_id=1, source_target_pairs={{0,3},{1,2},{2,1},{3,0},{4,7},{5,6},{6,5},{7,4},{8,11},{9,10},{10,... | collective-permute-start | bytes 393224 | tf_op jit(solution)/shard_map/ppermute | solution.py:415
  22.1 2.0 %collective-permute-start.7 = (f32[1024,128]{1,0:T(8,128)S(1)}, f32[1024,128]{1,0:T(8,128)S(1)}, u32[]{:S(2)}, u32[]{:S(2)}) collective-permute-start(f32[1024,128]{1,0:T(8,128)S(1)} %odd.1.t_a), channel_id=1, source_target_pairs={{0,1},{1,0},{2,3},{3,2},{4,5},{5,4},{6,7},{7,6},{8,9},{9,8},{10,11... | collective-permute-start | bytes 1572872 | tf_op jit(solution)/shard_map/ppermute | solution.py:415
  25.7 8.5 %collective-permute-start.10 = (f32[256,128]{1,0:T(8,128)S(1)}, f32[256,128]{1,0:T(8,128)S(1)}, u32[]{:S(2)}, u32[]{:S(2)}) collective-permute-start(f32[256,128]{1,0:T(8,128)S(1)} %get-tuple-element.35.dep_ref.a), channel_id=1, source_target_pairs={{0,7},{1,6},{2,5},{3,4},{4,3},{5,2},{6,1},{7,0},{8,15},{9,14},{10,... | collective-permute-start | bytes 393224 | tf_op jit(solution)/shard_map/ppermute | solution.py:415
  28.5 6.4 %collective-permute-start.9 = (f32[256,128]{1,0:T(8,128)S(1)}, f32[256,128]{1,0:T(8,128)S(1)}, u32[]{:S(2)}, u32[]{:S(2)}) collective-permute-start(f32[256,128]{1,0:T(8,128)S(1)} %get-tuple-element.35.dep_ref.a), channel_id=1, source_target_pairs={{0,4},{1,5},{2,6},{3,7},{4,0},{5,1},{6,2},{7,3},{8,12},{9,13},{10,... | collective-permute-start | bytes 393224 | tf_op jit(solution)/shard_map/ppermute | solution.py:415
  28.8 7.3 %collective-permute-start.8 = (f32[256,128]{1,0:T(8,128)S(1)}, f32[256,128]{1,0:T(8,128)S(1)}, u32[]{:S(2)}, u32[]{:S(2)}) collective-permute-start(f32[256,128]{1,0:T(8,128)S(1)} %get-tuple-element.35.dep_ref.a), channel_id=1, source_target_pairs={{0,3},{1,2},{2,1},{3,0},{4,7},{5,6},{6,5},{7,4},{8,11},{9,10},{10,... | collective-permute-start | bytes 393224 | tf_op jit(solution)/shard_map/ppermute | solution.py:415
  36.8 6.8 %collective-permute-start.13 = (f32[128,128]{1,0:T(8,128)S(1)}, f32[128,128]{1,0:T(8,128)S(1)}, u32[]{:S(2)}, u32[]{:S(2)}) collective-permute-start(f32[128,128]{1,0:T(8,128)S(1)} %second.1.a), channel_id=1, source_target_pairs={{0,97},{1,96},{2,99},{3,98},{4,101},{5,100},{6,103},{7,102},{8,105... | collective-permute-start | bytes 196616 | tf_op jit(solution)/shard_map/ppermute | solution.py:415
  36.8 6.7 %collective-permute-start.12 = (f32[128,128]{1,0:T(8,128)S(1)}, f32[128,128]{1,0:T(8,128)S(1)}, u32[]{:S(2)}, u32[]{:S(2)}) collective-permute-start(f32[128,128]{1,0:T(8,128)S(1)} %second.1.a), channel_id=1, source_target_pairs={{0,65},{1,64},{2,67},{3,66},{4,69},{5,68},{6,71},{7,70},{8,73},{9,... | collective-permute-start | bytes 196616 | tf_op jit(solution)/shard_map/ppermute | solution.py:415
  36.9 7.2 %collective-permute-start.11 = (f32[128,128]{1,0:T(8,128)S(1)}, f32[128,128]{1,0:T(8,128)S(1)}, u32[]{:S(2)}, u32[]{:S(2)}) collective-permute-start(f32[128,128]{1,0:T(8,128)S(1)} %second.1.a), channel_id=1, source_target_pairs={{0,33},{1,32},{2,35},{3,34},{4,37},{5,36},{6,39},{7,38},{8,41},{9,... | collective-permute-start | bytes 196616 | tf_op jit(solution)/shard_map/ppermute | solution.py:415
  44.1 6.7 %collective-permute-start.16 = (f32[128,128]{1,0:T(8,128)S(1)}, f32[128,128]{1,0:T(8,128)S(1)}, u32[]{:S(2)}, u32[]{:S(2)}) collective-permute-start(f32[128,128]{1,0:T(8,128)S(1)} %choose.1.a), channel_id=1, source_target_pairs={{0,25},{1,24},{2,27},{3,26},{4,29},{5,28},{6,31},{7,30},{8,17},{9,... | collective-permute-start | bytes 196616 | tf_op jit(solution)/shard_map/ppermute | solution.py:415
  44.4 6.4 %collective-permute-start.15 = (f32[128,128]{1,0:T(8,128)S(1)}, f32[128,128]{1,0:T(8,128)S(1)}, u32[]{:S(2)}, u32[]{:S(2)}) collective-permute-start(f32[128,128]{1,0:T(8,128)S(1)} %choose.1.a), channel_id=1, source_target_pairs={{0,17},{1,16},{2,19},{3,18},{4,21},{5,20},{6,23},{7,22},{8,25},{9,... | collective-permute-start | bytes 196616 | tf_op jit(solution)/shard_map/ppermute | solution.py:415
  47.8 3.9 %collective-permute-start.14 = (f32[128,128]{1,0:T(8,128)S(1)}, f32[128,128]{1,0:T(8,128)S(1)}, u32[]{:S(2)}, u32[]{:S(2)}) collective-permute-start(f32[128,128]{1,0:T(8,128)S(1)} %choose.1.a), channel_id=1, source_target_pairs={{0,9},{1,8},{2,11},{3,10},{4,13},{5,12},{6,15},{7,14},{8,1},{9,0},... | collective-permute-start | bytes 196616 | tf_op jit(solution)/shard_map/ppermute | solution.py:415
  51.8 1.3 %collective-permute-start.17 = (f32[128,128]{1,0:T(8,128)S(1)}, f32[128,128]{1,0:T(8,128)S(1)}, u32[]{:S(2)}, u32[]{:S(2)}) collective-permute-start(f32[128,128]{1,0:T(8,128)S(1)} %get-tuple-element.39), channel_id=1, source_target_pairs={{0,1},{1,0},{2,3},{3,2},{4,5},{5,4},{6,7},{7,6},{8,9},{9,8},{10,11... | collective-permute-start | bytes 196616 | tf_op jit(solution)/shard_map/ppermute | solution.py:415

commit v5 on v4

--- a/solution.py
+++ b/solution.py
@@ -10,6 +10,8 @@
 F32 = jnp.float32
 BF16 = jnp.bfloat16
 NZ = 4
+X_STEPS = (0, 2, 3, 1)
+Z_STEPS = (0, 1, 3, 2)
 W = 128
 NB = 1024
 PACK = NB // 4
@@ -233,52 +235,65 @@
 
 
 @on_chain
-def first_kernel(rhs_ref, a, b, c, d, odd_ref, own_ref, got_ref, t_a, t_b, y_ref, u_ref):
+def rows_kernel(own_ref, got_ref, out_ref):
+    for k in range(2):
+        out_ref[k] = lhs_of(own_ref[k], got_ref[k])
+
+
+def inverse_rows(own, got):
+    return call(rows_kernel, "rows", (vm((2, 4 * W, NB), BF16),), vmem=(own, got), mib=8)[0]
+
+
+def times_tile(out, tile_ref, y):
+    both = pair_of(y)
+    group = lane_group(out.shape)
+    for g in range(4):
+        u = dot3(lhs_of(tile_ref[pl.ds(PACK * g, PACK), :]), both)
+        out = jnp.where(group == g, out + u, out)
+    return out
+
+
+@on_chain
+def first_kernel(rhs_ref, a, b, c, d, inv_ref, y_ref):
     total = (a[...] + b[...]) + (c[...] + d[...])
-    y = dot3(lhs_of(own_ref[0], got_ref[0]), pair_of(unpack(rhs_ref[0] - total)))
+    y = dot3(inv_ref[0], pair_of(unpack(rhs_ref[0] - total)))
     y_ref[0] = y[:W]
     y_ref[1] = y[W:]
-    both = pair_of(jnp.where(odd_row() == 1, y, jnp.concatenate([y[W:], y[:W]], axis=0)))
-    out = odd_ref[...]
-    group = lane_group(out.shape)
-    for g in range(4):
-        rows = pl.ds(PACK * g, PACK)
-        hi, lo = split(jnp.concatenate([t_a[rows, :], t_b[rows, :]], axis=1))
-        prod = dot(hi, both)
-        u = prod[:, :W] + (prod[:, W:] + dot(lo, both[:, :W]))
-        out = jnp.where(group == g, out + u, out)
-    u_ref[...] = out
-
-
-def first(rhs, sums, odd, own, got, t_a, t_b):
-    return call(
-        first_kernel,
-        "first",
-        (vm((2, W, W)), PACKED),
-        vmem=(rhs, *sums, odd, own, got, t_a, t_b),
-        mib=8,
-    )
-
-
-@on_chain
-def second_kernel(rhs_ref, a, b, c, d, own_ref, got_ref, y_ref, dep_ref, out_ref):
+
+
+def first(rhs, sums, inv):
+    return call(first_kernel, "first", (vm((2, W, W)),), vmem=(rhs, *sums, inv), mib=8)[0]
+
+
+@on_chain
+def rest_kernel(turn, u_ref, y_ref, tile_ref, out_ref):
+    y = jnp.where(odd_row() == turn, y_ref[0], y_ref[1])
+    out_ref[...] = times_tile(u_ref[...], tile_ref, y)
+
+
+def rest(turn, u, y, tile):
+    return call(functools.partial(rest_kernel, turn), "rest", (PACKED,), vmem=(u, y, tile), mib=8)[0]
+
+
+@on_chain
+def second_kernel(rhs_ref, a, b, c, d, inv_ref, y_ref, dep_ref, out_ref):
     total = (a[...] + b[...]) + (c[...] + d[...])
-    y = dot3(lhs_of(own_ref[1], got_ref[1]), pair_of(unpack(rhs_ref[1] - total)))
+    y = dot3(inv_ref[1], pair_of(unpack(rhs_ref[1] - total)))
     group = lane_group((W, W))
     own = jnp.where(group < 2, y_ref[0], y[:W])
     got = jnp.where(group < 2, y_ref[1], y[W:])
     out_ref[...] = jnp.where(group % 2 == core(), own, got)
 
 
-def second(rhs, sums, own, got, y0, dep):
-    return call(
-        second_kernel, "second", (vm((W, W)),), vmem=(rhs, *sums, own, got, y0), deps=(dep,), mib=8
+def second(rhs, sums, inv, y0, dep):
+    return call(
+        second_kernel, "second", (vm((W, W)),), vmem=(rhs, *sums, inv, y0), deps=(dep,), mib=8
     )[0]
 
 
 def choose_kernel(a, b, c, d, out_ref):
     x = lax.axis_index("row") // NZ
-    for m, got in enumerate((a, b, c, d)):
+    for m, got in zip(X_STEPS, (a, b, c, d)):
 
         @pl.when(x == m)
         def _():
@@ -325,7 +340,7 @@
 
 def deal_kernel(a, b, c, d, keep_ref, send_ref, sides):
     z = lax.rem(lax.axis_index("row"), NZ)
-    for m, got in enumerate((a, b, c, d)):
+    for m, got in zip(Z_STEPS, (a, b, c, d)):
 
         @pl.when(z == m)
         def _():
@@ -420,11 +435,22 @@
 
 
 def chips(x):
-    return [x] + [exchange(x, 0, mask) for mask in (3, 4, 7)]
-
-
-def rows_over(y, step):
-    return [y] + [exchange(y, step * m, 1) for m in (1, 2, 3)]
+    return [x] + [exchange(x, 0, mask) for mask in (7, 3, 4)]
+
+
+def step(x, place):
+    pairs = [(r * 8 + c, place(r // NZ, r % NZ) * 8 + (c ^ 1)) for r in range(16) for c in range(8)]
+    return lax.ppermute(x, ("row", "col"), pairs)
+
+
+def along_x(y):
+    place = lambda m: lambda x, z: (x ^ m) * NZ + z
+    return [y] + [step(y, place(m)) for m in X_STEPS[1:]]
+
+
+def along_z(y):
+    place = lambda m: lambda x, z: x * NZ + (z ^ m)
+    return [y] + [step(y, place(m)) for m in Z_STEPS[1:]]
 
 
 def per_device(partials, panel, inverse, rhs):
@@ -435,14 +461,15 @@
     mine, other = add(keep, swap(send))
     inv, rhs = prep(inverse, rhs, mine)
     even, odd, inv = order(mine, exchange(other, 1, 1), inv)
-    inv_got = swap(inv)
     parts0 = parts(0, panel, partials, even)
+    inv = inverse_rows(inv, swap(inv))
     sums = chips(even)
     tile = odd_tile(tile, tile_odd, (*sums[1:], parts0[0]))
-    y0, u = first(rhs, sums, odd, inv, inv_got, tile, swap(tile))
+    y0 = first(rhs, sums, inv)
+    u = rest(0, rest(1, odd, y0, tile), y0, swap(tile))
     parts1 = parts(1, panel, partials, u)
-    y = second(rhs, chips(u), inv, inv_got, y0, parts1[0])
-    keep, send = deal(rows_over(choose(rows_over(y, NZ)), 1))
+    y = second(rhs, chips(u), inv, y0, parts1[0])
+    keep, send = deal(along_z(choose(along_x(y))))
     new, solved = update(keep, swap(send), parts0, parts1)
     return new[None, :, None], solved
 

time: 57.3 us -> 55.5 us (0.969)
  waiting for transfers between devices: 20.4 us -> 17.3 us
  starting transfers between devices: 19.9 us -> 21 us
    ppermute x18 -> x12, waiting for transfers between devices: 20.4 us -> 10.4 us  [exchange(): return lax.ppermute(x, ('row', 'col'), pairs)]
    ppermute x0 -> x6, starting transfers between devices: none -> 7.85 us  [step(): return lax.ppermute(x, ('row', 'col'), pairs)]
    ppermute x0 -> x6, waiting for transfers between devices: none -> 6.84 us  [step(): return lax.ppermute(x, ('row', 'col'), pairs)]
    ppermute x18 -> x12, starting transfers between devices: 19.9 us -> 13.1 us  [exchange(): return lax.ppermute(x, ('row', 'col'), pairs)]
    pallas_call x12 -> x15, Pallas kernels: 16 us -> 16.3 us  [call(): pl.pallas_call(kernel, out_shape=out, in_specs=[ANY] * len(hbm) + [VMEM]...]
  transfers between devices with their start and end apart: 18 -> 18, of which waited for: 12 -> 11; matrix products, arithmetic and copies ran while one was open for 0% -> 0% of each run, Pallas kernels for 14% -> 17%
where the time goes in v5:
time: 55.5 us; the launch traced here: 55.4 us
  starting transfers between devices  21 us (38%)
  waiting for transfers between devices  17.3 us (31%)
  Pallas kernels  16.3 us (29%)
  between operations  0.77 us (1%)
    pallas_call x15, Pallas kernels, call(): pl.pallas_call(kernel, out_shape=out, in_specs=[ANY] * len(hbm) + [VMEM]...  16.3 us
    ppermute x12, starting transfers between devices, exchange(): return lax.ppermute(x, ('row', 'col'), pairs)  13.1 us
    ppermute x12, waiting for transfers between devices, exchange(): return lax.ppermute(x, ('row', 'col'), pairs)  10.4 us
    ppermute x6, starting transfers between devices, step(): return lax.ppermute(x, ('row', 'col'), pairs)  7.85 us
    ppermute x6, waiting for transfers between devices, step(): return lax.ppermute(x, ('row', 'col'), pairs)  6.84 us
  transfers between devices with their start and end apart: 18, of which 11 were waited for; matrix products, arithmetic and copies ran while one was open for 0% of the time, Pallas kernels for 17%

profile of v5, /device:TPU:1, one launch (start us, length us, event | category | flops | bytes accessed | tf_op | source)
XLA Modules:
  0.0 55.4 jit_solution(5690347249999081149)
XLA Ops:
  0.6 1.7 %start.1 = (f32[2,256,128]{2,1,0:T(8,128)S(1)}, f32[2,256,128]{2,1,0:T(8,128)S(1)}, f32[1024,128]{1,0:T(8,128)S(1)}) custom-call(f32[8,1024,128]{2,1,0:T(8,128)} %bitcast.8, f32[8,2048,128]{2,1,0:T(8,128)} %bitcast.5), custom_call_target="tpu_custom_call" | custom-call | tf_op jit(solution)/shard_map/start/pallas_call | solution.py:38
  2.3 1.5 %collective-permute-start = (f32[2,256,128]{2,1,0:T(8,128)S(1)}, f32[2,256,128]{2,1,0:T(8,128)S(1)}, u32[]{:S(2)}, u32[]{:S(2)}) collective-permute-start(f32[2,256,128]{2,1,0:T(8,128)S(1)} %get-tuple-element.23), channel_id=1, source_target_pairs={{0,1},{1,0},{2,3},{3,2},{4,5},{5,4},{6,7},{7,6},{8,9},{9,8},{10,11... | collective-permute-start | bytes 786440 | tf_op jit(solution)/shard_map/ppermute | solution.py:430
  3.8 1.2 %collective-permute-done.b_ref = f32[2,256,128]{2,1,0:T(8,128)S(1)} collective-permute-done((f32[2,256,128]{2,1,0:T(8,128)S(1)}, f32[2,256,128]{2,1,0:T(8,128)S(1)}, u32[]{:S(2)}, u32[]{:S(2)}) %collective-permute-start) | collective-permute-done | bytes 262176 | tf_op jit(solution)/shard_map/ppermute | solution.py:430
  5.0 2.1 %collective-permute-start.1 = (f32[256,128]{1,0:T(8,128)S(1)}, f32[256,128]{1,0:T(8,128)S(1)}, u32[]{:S(2)}, u32[]{:S(2)}) collective-permute-start(f32[256,128]{1,0:T(8,128)S(1)} %get-tuple-element.26), channel_id=1, source_target_pairs={{0,9},{1,8},{2,11},{3,10},{4,13},{5,12},{6,15},{7,14},{8,1},{9,0},... | collective-permute-start | bytes 393224 | tf_op jit(solution)/shard_map/ppermute | solution.py:430
  7.1 2.1 %prep.1 = (f32[2,128,1024]{2,1,0:T(8,128)S(1)}, f32[2,256,128]{2,1,0:T(8,128)S(1)}) custom-call(f32[2,128,1024]{2,1,0:T(8,128)} %inv_ref.1, f32[2,1024,128]{2,1,0:T(8,128)} %rhs_ref.1, f32[256,128]{1,0:T(8,128)S(1)} %get-tuple-element.24.dep_ref.mine_ref), custom_call_target="tpu_custom_call" | custom-call | bytes 8388608 | tf_op jit(solution)/shard_map/prep/pallas_call | solution.py:38
  9.3 2.0 %collective-permute-done.1.got_ref = f32[256,128]{1,0:T(8,128)S(1)} collective-permute-done((f32[256,128]{1,0:T(8,128)S(1)}, f32[256,128]{1,0:T(8,128)S(1)}, u32[]{:S(2)}, u32[]{:S(2)}) %collective-permute-start.1) | collective-permute-done | bytes 131104 | tf_op jit(solution)/shard_map/ppermute | solution.py:430
  11.4 3.0 %collective-permute-start.4 = (f32[256,128]{1,0:T(8,128)S(1)}, f32[256,128]{1,0:T(8,128)S(1)}, u32[]{:S(2)}, u32[]{:S(2)}) collective-permute-start(f32[256,128]{1,0:T(8,128)S(1)} %get-tuple-element.29.a.dep_ref), channel_id=1, source_target_pairs={{0,4},{1,5},{2,6},{3,7},{4,0},{5,1},{6,2},{7,3},{8,12},{9,13},{10,... | collective-permute-start | bytes 393224 | tf_op jit(solution)/shard_map/ppermute | solution.py:430
  14.4 1.0 %collective-permute-start.3 = (f32[256,128]{1,0:T(8,128)S(1)}, f32[256,128]{1,0:T(8,128)S(1)}, u32[]{:S(2)}, u32[]{:S(2)}) collective-permute-start(f32[256,128]{1,0:T(8,128)S(1)} %get-tuple-element.29.a.dep_ref), channel_id=1, source_target_pairs={{0,3},{1,2},{2,1},{3,0},{4,7},{5,6},{6,5},{7,4},{8,11},{9,10},{10,... | collective-permute-start | bytes 393224 | tf_op jit(solution)/shard_map/ppermute | solution.py:430
  15.4 0.4 collective-permute-start.2
  15.8 2.9 %parts.2 = (bf16[4,1024,256]{2,1,0:T(8,128)(2,1)S(1)}, bf16[4,1024,256]{2,1,0:T(8,128)(2,1)S(1)}, f32[4,1024,128]{2,1,0:T(8,128)S(1)}) custom-call(f32[8,2048,128]{2,1,0:T(8,128)} %bitcast.6, f32[8,1024,128]{2,1,0:T(8,128)} %bitcast.9, f32[256,128]{1,0:T(8,128)S(1)} %get-tuple-element.29.a.dep_ref), custom_call_target="tpu_custom_call" | custom-call | bytes 12582912 | tf_op jit(solution)/shard_map/parts/pallas_call | solution.py:38
  18.7 3.1 %collective-permute-done.6.got_ref = f32[1024,128]{1,0:T(8,128)S(1)} collective-permute-done((f32[1024,128]{1,0:T(8,128)S(1)}, f32[1024,128]{1,0:T(8,128)S(1)}, u32[]{:S(2)}, u32[]{:S(2)}) %collective-permute-start.6) | collective-permute-done | bytes 524320 | tf_op jit(solution)/shard_map/ppermute | solution.py:430
  22.4 0.6 %first.1.y_ref = f32[2,128,128]{2,1,0:T(8,128)S(1)} custom-call(f32[2,256,128]{2,1,0:T(8,128)S(1)} %get-tuple-element.25.rhs_ref, f32[256,128]{1,0:T(8,128)S(1)} %get-tuple-element.29.a.dep_ref, f32[256,128]{1,0:T(8,128)S(1)} %collective-permute-done.2.b.dep0, f32[256,128]{1,0:T(8,128)S(1)} %collective-permute-done.3.c.dep1, ...), custom_call_target="tpu_custom_call" | custom-call | tf_op jit(solution)/shard_map/first/pallas_call | solution.py:38
  23.1 0.4 rest.2.u_ref
  23.5 0.3 collective-permute-done.7.tile_ref
  23.9 0.4 rest.3.dep_ref.a
  24.3 3.1 %collective-permute-start.10 = (f32[256,128]{1,0:T(8,128)S(1)}, f32[256,128]{1,0:T(8,128)S(1)}, u32[]{:S(2)}, u32[]{:S(2)}) collective-permute-start(f32[256,128]{1,0:T(8,128)S(1)} %rest.3.dep_ref.a), channel_id=1, source_target_pairs={{0,4},{1,5},{2,6},{3,7},{4,0},{5,1},{6,2},{7,3},{8,12},{9,13},{10,... | collective-permute-start | bytes 393224 | tf_op jit(solution)/shard_map/ppermute | solution.py:430
  27.4 0.9 %collective-permute-start.9 = (f32[256,128]{1,0:T(8,128)S(1)}, f32[256,128]{1,0:T(8,128)S(1)}, u32[]{:S(2)}, u32[]{:S(2)}) collective-permute-start(f32[256,128]{1,0:T(8,128)S(1)} %rest.3.dep_ref.a), channel_id=1, source_target_pairs={{0,3},{1,2},{2,1},{3,0},{4,7},{5,6},{6,5},{7,4},{8,11},{9,10},{10,... | collective-permute-start | bytes 393224 | tf_op jit(solution)/shard_map/ppermute | solution.py:430
  28.2 0.4 collective-permute-start.8
  28.6 2.9 %parts.3 = (bf16[4,1024,256]{2,1,0:T(8,128)(2,1)S(1)}, bf16[4,1024,256]{2,1,0:T(8,128)(2,1)S(1)}, f32[4,1024,128]{2,1,0:T(8,128)S(1)}) custom-call(f32[8,2048,128]{2,1,0:T(8,128)} %bitcast.7, f32[8,1024,128]{2,1,0:T(8,128)} %bitcast.10, f32[256,128]{1,0:T(8,128)S(1)} %rest.3.dep_ref.a), custom_call_target="tpu_custom_call" | custom-call | bytes 12582912 | tf_op jit(solution)/shard_map/parts/pallas_call | solution.py:38
  31.5 2.8 %collective-permute-done.9.c = f32[256,128]{1,0:T(8,128)S(1)} collective-permute-done((f32[256,128]{1,0:T(8,128)S(1)}, f32[256,128]{1,0:T(8,128)S(1)}, u32[]{:S(2)}, u32[]{:S(2)}) %collective-permute-start.9) | collective-permute-done | bytes 131104 | tf_op jit(solution)/shard_map/ppermute | solution.py:430
  34.5 0.6 %second.1.a = f32[128,128]{1,0:T(8,128)S(1)} custom-call(f32[2,256,128]{2,1,0:T(8,128)S(1)} %get-tuple-element.25.rhs_ref, f32[256,128]{1,0:T(8,128)S(1)} %rest.3.dep_ref.a, f32[256,128]{1,0:T(8,128)S(1)} %collective-permute-done.8.b, f32[256,128]{1,0:T(8,128)S(1)} %collective-permute-done.9.c, f32[256,128]{1,0:T(8,128)S(1)} %collective-permute-done.10.d, ...), custom_call_target="tpu_custom_call" | custom-call | tf_op jit(solution)/shard_map/second/pallas_call | solution.py:38
  35.2 0.3 collective-permute-start.12
  35.5 3.1 %collective-permute-start.11 = (f32[128,128]{1,0:T(8,128)S(1)}, f32[128,128]{1,0:T(8,128)S(1)}, u32[]{:S(2)}, u32[]{:S(2)}) collective-permute-start(f32[128,128]{1,0:T(8,128)S(1)} %second.1.a), channel_id=1, source_target_pairs={{0,65},{1,64},{2,67},{3,66},{4,69},{5,68},{6,71},{7,70},{8,73},{9,... | collective-permute-start | bytes 196616 | tf_op jit(solution)/shard_map/ppermute | solution.py:443
  38.6 0.6 %collective-permute-done.13.d = f32[128,128]{1,0:T(8,128)S(1)} collective-permute-done((f32[128,128]{1,0:T(8,128)S(1)}, f32[128,128]{1,0:T(8,128)S(1)}, u32[]{:S(2)}, u32[]{:S(2)}) %collective-permute-start.13) | collective-permute-done | bytes 65568 | tf_op jit(solution)/shard_map/ppermute | solution.py:443
  39.2 2.4 %collective-permute-done.12.c = f32[128,128]{1,0:T(8,128)S(1)} collective-permute-done((f32[128,128]{1,0:T(8,128)S(1)}, f32[128,128]{1,0:T(8,128)S(1)}, u32[]{:S(2)}, u32[]{:S(2)}) %collective-permute-start.12) | collective-permute-done | bytes 65568 | tf_op jit(solution)/shard_map/ppermute | solution.py:443
  41.6 2.4 %collective-permute-start.16 = (f32[128,128]{1,0:T(8,128)S(1)}, f32[128,128]{1,0:T(8,128)S(1)}, u32[]{:S(2)}, u32[]{:S(2)}) collective-permute-start(f32[128,128]{1,0:T(8,128)S(1)} %choose.1.a), channel_id=1, source_target_pairs={{0,17},{1,16},{2,19},{3,18},{4,21},{5,20},{6,23},{7,22},{8,25},{9,... | collective-permute-start | bytes 196616 | tf_op jit(solution)/shard_map/ppermute | solution.py:443
  44.1 1.9 %collective-permute-start.15 = (f32[128,128]{1,0:T(8,128)S(1)}, f32[128,128]{1,0:T(8,128)S(1)}, u32[]{:S(2)}, u32[]{:S(2)}) collective-permute-start(f32[128,128]{1,0:T(8,128)S(1)} %choose.1.a), channel_id=1, source_target_pairs={{0,25},{1,24},{2,27},{3,26},{4,29},{5,28},{6,31},{7,30},{8,17},{9,... | collective-permute-start | bytes 196616 | tf_op jit(solution)/shard_map/ppermute | solution.py:443
  46.0 0.9 %collective-permute-done.16.d = f32[128,128]{1,0:T(8,128)S(1)} collective-permute-done((f32[128,128]{1,0:T(8,128)S(1)}, f32[128,128]{1,0:T(8,128)S(1)}, u32[]{:S(2)}, u32[]{:S(2)}) %collective-permute-start.16) | collective-permute-done | bytes 65568 | tf_op jit(solution)/shard_map/ppermute | solution.py:443
  46.9 2.9 %collective-permute-done.15.c = f32[128,128]{1,0:T(8,128)S(1)} collective-permute-done((f32[128,128]{1,0:T(8,128)S(1)}, f32[128,128]{1,0:T(8,128)S(1)}, u32[]{:S(2)}, u32[]{:S(2)}) %collective-permute-start.15) | collective-permute-done | bytes 65568 | tf_op jit(solution)/shard_map/ppermute | solution.py:443
  50.0 0.5 collective-permute-start.17
  50.5 0.9 %collective-permute-done.17.got_ref = f32[128,128]{1,0:T(8,128)S(1)} collective-permute-done((f32[128,128]{1,0:T(8,128)S(1)}, f32[128,128]{1,0:T(8,128)S(1)}, u32[]{:S(2)}, u32[]{:S(2)}) %collective-permute-start.17) | collective-permute-done | bytes 65568 | tf_op jit(solution)/shard_map/ppermute | solution.py:430
  51.4 4.0 %update.1 = (f32[8,1024,128]{2,1,0:T(8,128)}, f32[2,128,128]{2,1,0:T(8,128)}) custom-call(f32[128,128]{1,0:T(8,128)S(1)} %get-tuple-element.34.keep_ref, f32[128,128]{1,0:T(8,128)S(1)} %collective-permute-done.17.got_ref, bf16[4,1024,256]{2,1,0:T(8,128)(2,1)S(1)} %get-tuple-element.32.dep3.ph0, bf16[4,1024,256]{2,1,0:T(8,128)(2,1)S(1)} %get-tuple-element.36.pl0, ...), custom_call_target="tpu_custom_call" | custom-call | tf_op jit(solution)/shard_map/update/pallas_call | solution.py:38
  (19 shorter events, 1.3 us)
Async XLA Ops:
  2.3 2.7 %collective-permute-start = (f32[2,256,128]{2,1,0:T(8,128)S(1)}, f32[2,256,128]{2,1,0:T(8,128)S(1)}, u32[]{:S(2)}, u32[]{:S(2)}) collective-permute-start(f32[2,256,128]{2,1,0:T(8,128)S(1)} %get-tuple-element.23), channel_id=1, source_target_pairs={{0,1},{1,0},{2,3},{3,2},{4,5},{5,4},{6,7},{7,6},{8,9},{9,8},{10,11... | collective-permute-start | bytes 786440 | tf_op jit(solution)/shard_map/ppermute | solution.py:430
  5.0 6.3 %collective-permute-start.1 = (f32[256,128]{1,0:T(8,128)S(1)}, f32[256,128]{1,0:T(8,128)S(1)}, u32[]{:S(2)}, u32[]{:S(2)}) collective-permute-start(f32[256,128]{1,0:T(8,128)S(1)} %get-tuple-element.26), channel_id=1, source_target_pairs={{0,9},{1,8},{2,11},{3,10},{4,13},{5,12},{6,15},{7,14},{8,1},{9,0},... | collective-permute-start | bytes 393224 | tf_op jit(solution)/shard_map/ppermute | solution.py:430
  7.0 14.7 %collective-permute-start.6 = (f32[1024,128]{1,0:T(8,128)S(1)}, f32[1024,128]{1,0:T(8,128)S(1)}, u32[]{:S(2)}, u32[]{:S(2)}) collective-permute-start(f32[1024,128]{1,0:T(8,128)S(1)} %get-tuple-element.31.own_ref), channel_id=1, source_target_pairs={{0,9},{1,8},{2,11},{3,10},{4,13},{5,12},{6,15},{7,14},{8,1},{9,0},... | collective-permute-start | bytes 1572872 | tf_op jit(solution)/shard_map/ppermute | solution.py:430
  11.4 10.8 %collective-permute-start.5 = (f32[2,128,1024]{2,1,0:T(8,128)S(1)}, f32[2,128,1024]{2,1,0:T(8,128)S(1)}, u32[]{:S(2)}, u32[]{:S(2)}) collective-permute-start(f32[2,128,1024]{2,1,0:T(8,128)S(1)} %get-tuple-element.30.own_ref), channel_id=1, source_target_pairs={{0,1},{1,0},{2,3},{3,2},{4,5},{5,4},{6,7},{7,6},{8,9},{9,8},{10,11... | collective-permute-start | bytes 3145736 | tf_op jit(solution)/shard_map/ppermute | solution.py:430
  11.4 10.3 %collective-permute-start.4 = (f32[256,128]{1,0:T(8,128)S(1)}, f32[256,128]{1,0:T(8,128)S(1)}, u32[]{:S(2)}, u32[]{:S(2)}) collective-permute-start(f32[256,128]{1,0:T(8,128)S(1)} %get-tuple-element.29.a.dep_ref), channel_id=1, source_target_pairs={{0,4},{1,5},{2,6},{3,7},{4,0},{5,1},{6,2},{7,3},{8,12},{9,13},{10,... | collective-permute-start | bytes 393224 | tf_op jit(solution)/shard_map/ppermute | solution.py:430
  14.4 7.4 %collective-permute-start.3 = (f32[256,128]{1,0:T(8,128)S(1)}, f32[256,128]{1,0:T(8,128)S(1)}, u32[]{:S(2)}, u32[]{:S(2)}) collective-permute-start(f32[256,128]{1,0:T(8,128)S(1)} %get-tuple-element.29.a.dep_ref), channel_id=1, source_target_pairs={{0,3},{1,2},{2,1},{3,0},{4,7},{5,6},{6,5},{7,4},{8,11},{9,10},{10,... | collective-permute-start | bytes 393224 | tf_op jit(solution)/shard_map/ppermute | solution.py:430
  15.4 6.4 %collective-permute-start.2 = (f32[256,128]{1,0:T(8,128)S(1)}, f32[256,128]{1,0:T(8,128)S(1)}, u32[]{:S(2)}, u32[]{:S(2)}) collective-permute-start(f32[256,128]{1,0:T(8,128)S(1)} %get-tuple-element.29.a.dep_ref), channel_id=1, source_target_pairs={{0,7},{1,6},{2,5},{3,4},{4,3},{5,2},{6,1},{7,0},{8,15},{9,14},{10,... | collective-permute-start | bytes 393224 | tf_op jit(solution)/shard_map/ppermute | solution.py:430
  21.9 2.0 %collective-permute-start.7 = (f32[1024,128]{1,0:T(8,128)S(1)}, f32[1024,128]{1,0:T(8,128)S(1)}, u32[]{:S(2)}, u32[]{:S(2)}) collective-permute-start(f32[1024,128]{1,0:T(8,128)S(1)} %odd.1.tile_ref), channel_id=1, source_target_pairs={{0,1},{1,0},{2,3},{3,2},{4,5},{5,4},{6,7},{7,6},{8,9},{9,8},{10,11... | collective-permute-start | bytes 1572872 | tf_op jit(solution)/shard_map/ppermute | solution.py:430
  24.3 7.2 %collective-permute-start.10 = (f32[256,128]{1,0:T(8,128)S(1)}, f32[256,128]{1,0:T(8,128)S(1)}, u32[]{:S(2)}, u32[]{:S(2)}) collective-permute-start(f32[256,128]{1,0:T(8,128)S(1)} %rest.3.dep_ref.a), channel_id=1, source_target_pairs={{0,4},{1,5},{2,6},{3,7},{4,0},{5,1},{6,2},{7,3},{8,12},{9,13},{10,... | collective-permute-start | bytes 393224 | tf_op jit(solution)/shard_map/ppermute | solution.py:430
  27.4 7.0 %collective-permute-start.9 = (f32[256,128]{1,0:T(8,128)S(1)}, f32[256,128]{1,0:T(8,128)S(1)}, u32[]{:S(2)}, u32[]{:S(2)}) collective-permute-start(f32[256,128]{1,0:T(8,128)S(1)} %rest.3.dep_ref.a), channel_id=1, source_target_pairs={{0,3},{1,2},{2,1},{3,0},{4,7},{5,6},{6,5},{7,4},{8,11},{9,10},{10,... | collective-permute-start | bytes 393224 | tf_op jit(solution)/shard_map/ppermute | solution.py:430
  28.2 6.3 %collective-permute-start.8 = (f32[256,128]{1,0:T(8,128)S(1)}, f32[256,128]{1,0:T(8,128)S(1)}, u32[]{:S(2)}, u32[]{:S(2)}) collective-permute-start(f32[256,128]{1,0:T(8,128)S(1)} %rest.3.dep_ref.a), channel_id=1, source_target_pairs={{0,7},{1,6},{2,5},{3,4},{4,3},{5,2},{6,1},{7,0},{8,15},{9,14},{10,... | collective-permute-start | bytes 393224 | tf_op jit(solution)/shard_map/ppermute | solution.py:430
  35.1 4.1 %collective-permute-start.13 = (f32[128,128]{1,0:T(8,128)S(1)}, f32[128,128]{1,0:T(8,128)S(1)}, u32[]{:S(2)}, u32[]{:S(2)}) collective-permute-start(f32[128,128]{1,0:T(8,128)S(1)} %second.1.a), channel_id=1, source_target_pairs={{0,33},{1,32},{2,35},{3,34},{4,37},{5,36},{6,39},{7,38},{8,41},{9,... | collective-permute-start | bytes 196616 | tf_op jit(solution)/shard_map/ppermute | solution.py:443
  35.2 6.4 %collective-permute-start.12 = (f32[128,128]{1,0:T(8,128)S(1)}, f32[128,128]{1,0:T(8,128)S(1)}, u32[]{:S(2)}, u32[]{:S(2)}) collective-permute-start(f32[128,128]{1,0:T(8,128)S(1)} %second.1.a), channel_id=1, source_target_pairs={{0,97},{1,96},{2,99},{3,98},{4,101},{5,100},{6,103},{7,102},{8,105... | collective-permute-start | bytes 196616 | tf_op jit(solution)/shard_map/ppermute | solution.py:443
  35.5 6.1 %collective-permute-start.11 = (f32[128,128]{1,0:T(8,128)S(1)}, f32[128,128]{1,0:T(8,128)S(1)}, u32[]{:S(2)}, u32[]{:S(2)}) collective-permute-start(f32[128,128]{1,0:T(8,128)S(1)} %second.1.a), channel_id=1, source_target_pairs={{0,65},{1,64},{2,67},{3,66},{4,69},{5,68},{6,71},{7,70},{8,73},{9,... | collective-permute-start | bytes 196616 | tf_op jit(solution)/shard_map/ppermute | solution.py:443
  41.6 5.3 %collective-permute-start.16 = (f32[128,128]{1,0:T(8,128)S(1)}, f32[128,128]{1,0:T(8,128)S(1)}, u32[]{:S(2)}, u32[]{:S(2)}) collective-permute-start(f32[128,128]{1,0:T(8,128)S(1)} %choose.1.a), channel_id=1, source_target_pairs={{0,17},{1,16},{2,19},{3,18},{4,21},{5,20},{6,23},{7,22},{8,25},{9,... | collective-permute-start | bytes 196616 | tf_op jit(solution)/shard_map/ppermute | solution.py:443
  44.1 5.8 %collective-permute-start.15 = (f32[128,128]{1,0:T(8,128)S(1)}, f32[128,128]{1,0:T(8,128)S(1)}, u32[]{:S(2)}, u32[]{:S(2)}) collective-permute-start(f32[128,128]{1,0:T(8,128)S(1)} %choose.1.a), channel_id=1, source_target_pairs={{0,25},{1,24},{2,27},{3,26},{4,29},{5,28},{6,31},{7,30},{8,17},{9,... | collective-permute-start | bytes 196616 | tf_op jit(solution)/shard_map/ppermute | solution.py:443
  46.0 3.8 %collective-permute-start.14 = (f32[128,128]{1,0:T(8,128)S(1)}, f32[128,128]{1,0:T(8,128)S(1)}, u32[]{:S(2)}, u32[]{:S(2)}) collective-permute-start(f32[128,128]{1,0:T(8,128)S(1)} %choose.1.a), channel_id=1, source_target_pairs={{0,9},{1,8},{2,11},{3,10},{4,13},{5,12},{6,15},{7,14},{8,1},{9,0},... | collective-permute-start | bytes 196616 | tf_op jit(solution)/shard_map/ppermute | solution.py:443
  50.0 1.4 %collective-permute-start.17 = (f32[128,128]{1,0:T(8,128)S(1)}, f32[128,128]{1,0:T(8,128)S(1)}, u32[]{:S(2)}, u32[]{:S(2)}) collective-permute-start(f32[128,128]{1,0:T(8,128)S(1)} %get-tuple-element.35), channel_id=1, source_target_pairs={{0,1},{1,0},{2,3},{3,2},{4,5},{5,4},{6,7},{7,6},{8,9},{9,8},{10,11... | collective-permute-start | bytes 196616 | tf_op jit(solution)/shard_map/ppermute | solution.py:430

commit v6 on v5

--- a/solution.py
+++ b/solution.py
@@ -11,7 +11,6 @@
 BF16 = jnp.bfloat16
 NZ = 4
 X_STEPS = (0, 2, 3, 1)
-Z_STEPS = (0, 1, 3, 2)
 W = 128
 NB = 1024
 PACK = NB // 4
@@ -103,55 +102,81 @@
     return gated
 
 
-def pack(src, b):
-    out = None
-    for g in range(4):
-        rows = src[PACK * g : PACK * (g + 1)]
-        shift = 32 * ((g - b) % 4)
-        rows = pltpu.roll(rows, shift, 1) if shift else rows
-        out = rows if out is None else jnp.where(lane_group(rows.shape) == g, rows, out)
+def packed(rows):
+    group = lane_group(rows[0].shape)
+    high, odd = group >= 2, group % 2 == 1
+    out = list(rows)
+    for g in range(2):
+        a, b = out[g], out[g + 2]
+        turned = pltpu.roll(jnp.where(high, a, b), 64, 1)
+        out[g], out[g + 2] = jnp.where(high, turned, a), jnp.where(high, b, turned)
+    for g in (0, 2):
+        a, b = out[g], out[g + 1]
+        out[g], out[g + 1] = jnp.where(odd, pltpu.roll(b, 32, 1), a), jnp.where(odd, b, pltpu.roll(a, 96, 1))
     return out
 
 
 def unpack(p):
+    group = lane_group(p.shape)
+    turned = [p] + [pltpu.roll(p, 32 * n, 1) for n in (1, 2, 3)]
     out = []
     for g in range(4):
-        m = jnp.where(lane_group(p.shape) == g, p, 0.0)
-        m = m + pltpu.roll(m, 32, 1)
-        out.append(m + pltpu.roll(m, 64, 1))
+        m = p
+        for n in (1, 2, 3):
+            m = jnp.where(group == (g + n) % 4, turned[n], m)
+        out.append(m)
     return jnp.concatenate(out, axis=0)
 
 
 @on_chain
-def start_kernel(p_ref, panel_ref, send_ref, keep_ref, tile_ref, p_buf, t_buf, q_buf, sem):
+def start_kernel(p_ref, send_ref, keep_ref, p_buf, q_buf, sem):
     h = side()
-    one = pltpu.make_async_copy(p_ref.at[0], p_buf, sem.at[0])
-    two = pltpu.make_async_copy(panel_ref.at[0], t_buf, sem.at[1])
-    one.start()
-    two.start()
-    one.wait()
-    for b in range(4):
-        q_buf[b] = pack(p_buf, b)
+    copies = [
+        pltpu.make_async_copy(p_ref.at[0, pl.ds(PACK * g, PACK), :], p_buf.at[g], sem.at[g]) for g in range(4)
+    ]
+    for c in copies:
+        c.start()
+    for c in copies:
+        c.wait()
+    for b, block in enumerate(packed([p_buf[g] for g in range(4)])):
+        q_buf[b] = block
     for r in range(2):
         keep_ref[r] = q_buf[2 * r + h]
         send_ref[r] = q_buf[2 * r + 1 - h]
-    two.wait()
-    tile_ref[...] = t_buf[pl.ds(0, NB, stride=2), :]
-
-
-def start(partials, panel):
+
+
+def start(partials):
     return call(
         start_kernel,
         "start",
-        (vm((2, PACK, W)), vm((2, PACK, W)), vm((NB, W))),
-        hbm=(partials, panel),
+        (vm((2, PACK, W)), vm((2, PACK, W))),
+        hbm=(partials,),
         scratch=[
-            pltpu.VMEM((NB, W), F32),
-            pltpu.VMEM((2 * NB, W), F32),
             pltpu.VMEM((4, PACK, W), F32),
-            pltpu.SemaphoreType.DMA((2,)),
+            pltpu.VMEM((4, PACK, W), F32),
+            pltpu.SemaphoreType.DMA((4,)),
         ],
     )
+
+
+@on_chain
+def tile_kernel(panel_ref, dep_ref, out_ref, buf, sem):
+    copy = pltpu.make_async_copy(panel_ref.at[0], buf, sem.at[0])
+    copy.start()
+    copy.wait()
+    out_ref[...] = buf[pl.ds(0, NB, stride=2), :]
+
+
+def first_tile(panel, dep):
+    return call(
+        tile_kernel,
+        "tile",
+        (vm((NB, W)),),
+        hbm=(panel,),
+        deps=(dep,),
+        scratch=[pltpu.VMEM((2 * NB, W), F32), pltpu.SemaphoreType.DMA((1,))],
+        mb=8,
+    )[0]
 
 
 @on_chain
@@ -163,8 +188,8 @@
     one.wait()
     b = 2 * odd_row() + side()
     for k in range(2):
-        for at in range(4):
-            q_buf[at] = pack(r_buf.at[k], at)
+        for at, block in enumerate(packed([r_buf[k, PACK * g : PACK * (g + 1)] for g in range(4)])):
+            q_buf[at] = block
         rhs_out[k] = q_buf[b]
     two.wait()
 
@@ -186,14 +211,14 @@
 
 
 @on_chain
-def add_kernel(a_ref, b_ref, mine_ref, other_ref):
+def add_kernel(a_ref, b_ref, dep_ref, mine_ref, other_ref):
     r = odd_row()
     mine_ref[...] = a_ref[r] + b_ref[r]
     other_ref[...] = a_ref[1 - r] + b_ref[1 - r]
 
 
-def add(a, b):
-    return call(add_kernel, "add", (PACKED, PACKED), vmem=(a, b))
+def add(a, b, dep):
+    return call(add_kernel, "add", (PACKED, PACKED), vmem=(a, b), deps=(dep,))
 
 
 @on_chain
@@ -340,15 +365,12 @@
 
 def deal_kernel(a, b, c, d, keep_ref, send_ref, sides):
     z = lax.rem(lax.axis_index("row"), NZ)
-    for m, got in zip(Z_STEPS, (a, b, c, d)):
-
-        @pl.when(z == m)
+    for at, (from_0, from_1) in enumerate(((a, d), (b, a), (d, c), (c, b))):
+
+        @pl.when(z == at)
         def _():
-            sides[0] = got[...]
-
-        @pl.when(z == m ^ 1)
-        def _():
-            sides[1] = got[...]
+            sides[0] = from_0[...]
+            sides[1] = from_1[...]
 
     left, right = sides[0], sides[1]
     group = lane_group((W, W))
@@ -372,7 +394,7 @@
     )
 
 
-def update_kernel(keep_ref, got_ref, ph0, pl0, part0, ph1, pl1, part1, out_ref, solved_ref, buf, sem):
+def update_kernel(keep_ref, got_ref, ph0, pl0, part0, ph1, pl1, part1, out_ref, solved_ref, buf, y_buf, sem):
     row = lax.axis_index("row")
     x, z = row // NZ, lax.rem(row, NZ)
     way = core() + chip() + jnp.where(x == 0, 0, 1)
@@ -391,23 +413,27 @@
         return jnp.where(mine, spread(keep), spread(got))
 
     y0, y1 = block(0), block(1)
-    solved_ref[0] = y0
-    solved_ref[1] = y1
+    y_buf[0] = y0
+    y_buf[1] = y1
+    solved = pltpu.make_async_copy(y_buf, solved_ref, sem.at[9])
+    solved.start()
     head = pair_of(jnp.concatenate([jnp.where(row > 0, y0, 0.0), jnp.where(row > 1, y1, 0.0)], axis=0))
     rest = pair_of(jnp.concatenate([y0, y1], axis=0))
 
-    def copy(l):
-        return pltpu.make_async_copy(buf.at[l], out_ref.at[l], sem.at[l])
-
-    for l in range(8):
+    pieces = [(l, 0, NB) for l in range(7)] + [(7, 0, NB // 2), (7, NB // 2, NB // 2)]
+    copies = []
+    for n, (l, at, size) in enumerate(pieces):
         hi, lo, part = ((ph0, pl0, part0), (ph1, pl1, part1))[l // GROUP]
         w = head if l == 0 else rest
-        prod = dot(hi[l % GROUP], w)
-        low = dot(lo[l % GROUP], w[:, :W])
-        buf[l] = part[l % GROUP] + (prod[:, :W] + (prod[:, W:] + low))
-        copy(l).start()
-    for l in range(8):
-        copy(l).wait()
+        rows = pl.ds(at, size)
+        prod = dot(hi[l % GROUP, rows, :], w)
+        low = dot(lo[l % GROUP, rows, :], w[:, :W])
+        buf[l, rows, :] = part[l % GROUP, rows, :] + (prod[:, :W] + (prod[:, W:] + low))
+        copies.append(pltpu.make_async_copy(buf.at[l, rows, :], out_ref.at[l, rows, :], sem.at[n]))
+        copies[-1].start()
+    for c in copies:
+        c.wait()
+    solved.wait()
 
 
 def update(keep, got, parts0, parts1):
@@ -416,17 +442,22 @@
         "update",
         (jax.ShapeDtypeStruct((8, NB, W), F32), jax.ShapeDtypeStruct((2, W, W), F32)),
         vmem=(keep, got, *parts0, *parts1),
-        out_specs=(ANY, VMEM),
+        out_specs=(ANY, ANY),
         scratch=[
             pltpu.VMEM((8, NB, W), F32),
-            pltpu.SemaphoreType.DMA((8,)),
+            pltpu.VMEM((2, W, W), F32),
+            pltpu.SemaphoreType.DMA((10,)),
         ],
         mib=10,
     )
 
 
 def exchange(x, row_mask, col_mask):
-    pairs = [(r * 8 + c, (r ^ row_mask) * 8 + (c ^ col_mask)) for r in range(16) for c in range(8)]
+    pairs = []
+    for r in range(16):
+        for c in range(8):
+            chain = r < 2
+            pairs.append((r * 8 + c, (r ^ row_mask) * 8 + (c ^ col_mask) if chain else r * 8 + (c ^ 1)))
     return lax.ppermute(x, ("row", "col"), pairs)
 
 
@@ -444,21 +475,24 @@
 
 
 def along_x(y):
-    place = lambda m: lambda x, z: (x ^ m) * NZ + z
+    cycles = {1: {0: 1, 1: 0}, 2: {0: 2, 2: 1, 1: 0}, 3: {0: 3, 3: 0}}
+    place = lambda m: lambda x, z: (cycles[m].get(x, x) if z < 2 else x) * NZ + z
     return [y] + [step(y, place(m)) for m in X_STEPS[1:]]
 
 
 def along_z(y):
-    place = lambda m: lambda x, z: x * NZ + (z ^ m)
-    return [y] + [step(y, place(m)) for m in Z_STEPS[1:]]
+    cycles = ({0: 2, 1: 0, 2: 1}, {0: 3, 3: 0, 1: 2, 2: 1}, {0: 1, 1: 3, 3: 0})
+    place = lambda cycle: lambda x, z: x * NZ + cycle.get(z, z)
+    return [y] + [step(y, place(cycle)) for cycle in cycles[::-1]]
 
 
 def per_device(partials, panel, inverse, rhs):
     partials = partials.reshape(8, NB, W)
     panel = panel.reshape(8, 2 * NB, W)
-    send, keep, tile = start(partials, panel)
+    send, keep = start(partials)
+    tile = first_tile(panel, send)
     tile_odd = exchange(tile, 1, 1)
-    mine, other = add(keep, swap(send))
+    mine, other = add(keep, swap(send), tile)
     inv, rhs = prep(inverse, rhs, mine)
     even, odd, inv = order(mine, exchange(other, 1, 1), inv)
     parts0 = parts(0, panel, partials, even)

time: 55.5 us -> 51.4 us (0.926)
  starting transfers between devices: 21 us -> 16.2 us
  waiting for transfers between devices: 17.3 us -> 17.9 us
    ppermute x6, starting transfers between devices: 7.85 us -> 3.46 us  [step(): return lax.ppermute(x, ('row', 'col'), pairs)]
    ppermute x6, waiting for transfers between devices: 6.84 us -> 7.96 us  [step(): return lax.ppermute(x, ('row', 'col'), pairs)]
    pallas_call x15 -> x16, Pallas kernels: 16.3 us -> 16.3 us  [call(): pl.pallas_call(kernel, out_shape=out, in_specs=[ANY] * len(hbm) + [VMEM]...]
  transfers between devices with their start and end apart: 18 -> 18, of which waited for: 11 -> 11; matrix products, arithmetic and copies ran while one was open for 0% -> 0% of each run, Pallas kernels for 17% -> 20%
where the time goes in v6:
time: 51.4 us; the launch traced here: 51.2 us
  waiting for transfers between devices  17.9 us (35%)
  Pallas kernels  16.3 us (32%)
  starting transfers between devices  16.2 us (32%)
  between operations  0.83 us (2%)
    pallas_call x16, Pallas kernels, call(): pl.pallas_call(kernel, out_shape=out, in_specs=[ANY] * len(hbm) + [VMEM]...  16.3 us
    ppermute x12, starting transfers between devices, exchange(): return lax.ppermute(x, ('row', 'col'), pairs)  12.8 us
    ppermute x12, waiting for transfers between devices, exchange(): return lax.ppermute(x, ('row', 'col'), pairs)  9.91 us
    ppermute x6, waiting for transfers between devices, step(): return lax.ppermute(x, ('row', 'col'), pairs)  7.96 us
    ppermute x6, starting transfers between devices, step(): return lax.ppermute(x, ('row', 'col'), pairs)  3.46 us
  transfers between devices with their start and end apart: 18, of which 11 were waited for; matrix products, arithmetic and copies ran while one was open for 0% of the time, Pallas kernels for 20%

profile of v6, /device:TPU:1, one launch (start us, length us, event | category | flops | bytes accessed | tf_op | source)
XLA Modules:
  0.0 51.2 jit_solution(174196393589289906)
XLA Ops:
  0.6 1.5 %start.1 = (f32[2,256,128]{2,1,0:T(8,128)S(1)}, f32[2,256,128]{2,1,0:T(8,128)S(1)}) custom-call(f32[8,1024,128]{2,1,0:T(8,128)} %bitcast.8), custom_call_target="tpu_custom_call" | custom-call | tf_op jit(solution)/shard_map/start/pallas_call | solution.py:37
  2.2 1.5 %collective-permute-start = (f32[2,256,128]{2,1,0:T(8,128)S(1)}, f32[2,256,128]{2,1,0:T(8,128)S(1)}, u32[]{:S(2)}, u32[]{:S(2)}) collective-permute-start(f32[2,256,128]{2,1,0:T(8,128)S(1)} %get-tuple-element.22.dep_ref), channel_id=1, source_target_pairs={{0,1},{1,0},{2,3},{3,2},{4,5},{5,4},{6,7},{7,6},{8,9},{9,8},{10,11... | collective-permute-start | bytes 786440 | tf_op jit(solution)/shard_map/ppermute | solution.py:461
  3.7 1.3 %tile.1.dep_ref.own_ref = f32[1024,128]{1,0:T(8,128)S(1)} custom-call(f32[8,2048,128]{2,1,0:T(8,128)} %bitcast.5, f32[2,256,128]{2,1,0:T(8,128)S(1)} %get-tuple-element.22.dep_ref), custom_call_target="tpu_custom_call" | custom-call | bytes 8388608 | tf_op jit(solution)/shard_map/tile/pallas_call | solution.py:37
  5.0 1.9 %collective-permute-start.1 = (f32[256,128]{1,0:T(8,128)S(1)}, f32[256,128]{1,0:T(8,128)S(1)}, u32[]{:S(2)}, u32[]{:S(2)}) collective-permute-start(f32[256,128]{1,0:T(8,128)S(1)} %get-tuple-element.25), channel_id=1, source_target_pairs={{0,9},{1,8},{2,11},{3,10},{4,13},{5,12},{6,15},{7,14},{8,1},{9,0},... | collective-permute-start | bytes 393224 | tf_op jit(solution)/shard_map/ppermute | solution.py:461
  7.0 1.8 %prep.1 = (f32[2,128,1024]{2,1,0:T(8,128)S(1)}, f32[2,256,128]{2,1,0:T(8,128)S(1)}) custom-call(f32[2,128,1024]{2,1,0:T(8,128)} %inv_ref.1, f32[2,1024,128]{2,1,0:T(8,128)} %rhs_ref.1, f32[256,128]{1,0:T(8,128)S(1)} %get-tuple-element.23.dep_ref.mine_ref), custom_call_target="tpu_custom_call" | custom-call | bytes 8388608 | tf_op jit(solution)/shard_map/prep/pallas_call | solution.py:37
  8.8 2.3 %collective-permute-done.1.got_ref = f32[256,128]{1,0:T(8,128)S(1)} collective-permute-done((f32[256,128]{1,0:T(8,128)S(1)}, f32[256,128]{1,0:T(8,128)S(1)}, u32[]{:S(2)}, u32[]{:S(2)}) %collective-permute-start.1) | collective-permute-done | bytes 131104 | tf_op jit(solution)/shard_map/ppermute | solution.py:461
  11.3 3.0 %collective-permute-start.4 = (f32[256,128]{1,0:T(8,128)S(1)}, f32[256,128]{1,0:T(8,128)S(1)}, u32[]{:S(2)}, u32[]{:S(2)}) collective-permute-start(f32[256,128]{1,0:T(8,128)S(1)} %get-tuple-element.28.a.dep_ref), channel_id=1, source_target_pairs={{0,4},{1,5},{2,6},{3,7},{4,0},{5,1},{6,2},{7,3},{8,12},{9,13},{10,... | collective-permute-start | bytes 393224 | tf_op jit(solution)/shard_map/ppermute | solution.py:461
  14.3 1.0 %collective-permute-start.3 = (f32[256,128]{1,0:T(8,128)S(1)}, f32[256,128]{1,0:T(8,128)S(1)}, u32[]{:S(2)}, u32[]{:S(2)}) collective-permute-start(f32[256,128]{1,0:T(8,128)S(1)} %get-tuple-element.28.a.dep_ref), channel_id=1, source_target_pairs={{0,3},{1,2},{2,1},{3,0},{4,7},{5,6},{6,5},{7,4},{8,11},{9,10},{10,... | collective-permute-start | bytes 393224 | tf_op jit(solution)/shard_map/ppermute | solution.py:461
  15.3 0.4 collective-permute-start.2
  15.7 2.9 %parts.2 = (bf16[4,1024,256]{2,1,0:T(8,128)(2,1)S(1)}, bf16[4,1024,256]{2,1,0:T(8,128)(2,1)S(1)}, f32[4,1024,128]{2,1,0:T(8,128)S(1)}) custom-call(f32[8,2048,128]{2,1,0:T(8,128)} %bitcast.6, f32[8,1024,128]{2,1,0:T(8,128)} %bitcast.9, f32[256,128]{1,0:T(8,128)S(1)} %get-tuple-element.28.a.dep_ref), custom_call_target="tpu_custom_call" | custom-call | bytes 12582912 | tf_op jit(solution)/shard_map/parts/pallas_call | solution.py:37
  18.6 3.2 %collective-permute-done.6.got_ref = f32[1024,128]{1,0:T(8,128)S(1)} collective-permute-done((f32[1024,128]{1,0:T(8,128)S(1)}, f32[1024,128]{1,0:T(8,128)S(1)}, u32[]{:S(2)}, u32[]{:S(2)}) %collective-permute-start.6) | collective-permute-done | bytes 524320 | tf_op jit(solution)/shard_map/ppermute | solution.py:461
  21.9 0.4 collective-permute-start.7
  22.3 0.3 rows.1.inv_ref
  22.6 0.6 %first.1.y_ref = f32[2,128,128]{2,1,0:T(8,128)S(1)} custom-call(f32[2,256,128]{2,1,0:T(8,128)S(1)} %get-tuple-element.24.rhs_ref, f32[256,128]{1,0:T(8,128)S(1)} %get-tuple-element.28.a.dep_ref, f32[256,128]{1,0:T(8,128)S(1)} %collective-permute-done.2.b.dep0, f32[256,128]{1,0:T(8,128)S(1)} %collective-permute-done.3.c.dep1, ...), custom_call_target="tpu_custom_call" | custom-call | tf_op jit(solution)/shard_map/first/pallas_call | solution.py:37
  23.2 0.4 rest.2.u_ref
  23.7 0.2 collective-permute-done.7.tile_ref
  23.9 0.4 rest.3.dep_ref.a
  24.3 3.0 %collective-permute-start.10 = (f32[256,128]{1,0:T(8,128)S(1)}, f32[256,128]{1,0:T(8,128)S(1)}, u32[]{:S(2)}, u32[]{:S(2)}) collective-permute-start(f32[256,128]{1,0:T(8,128)S(1)} %rest.3.dep_ref.a), channel_id=1, source_target_pairs={{0,4},{1,5},{2,6},{3,7},{4,0},{5,1},{6,2},{7,3},{8,12},{9,13},{10,... | collective-permute-start | bytes 393224 | tf_op jit(solution)/shard_map/ppermute | solution.py:461
  27.3 0.9 %collective-permute-start.9 = (f32[256,128]{1,0:T(8,128)S(1)}, f32[256,128]{1,0:T(8,128)S(1)}, u32[]{:S(2)}, u32[]{:S(2)}) collective-permute-start(f32[256,128]{1,0:T(8,128)S(1)} %rest.3.dep_ref.a), channel_id=1, source_target_pairs={{0,3},{1,2},{2,1},{3,0},{4,7},{5,6},{6,5},{7,4},{8,11},{9,10},{10,... | collective-permute-start | bytes 393224 | tf_op jit(solution)/shard_map/ppermute | solution.py:461
  28.2 0.4 collective-permute-start.8
  28.6 2.9 %parts.3 = (bf16[4,1024,256]{2,1,0:T(8,128)(2,1)S(1)}, bf16[4,1024,256]{2,1,0:T(8,128)(2,1)S(1)}, f32[4,1024,128]{2,1,0:T(8,128)S(1)}) custom-call(f32[8,2048,128]{2,1,0:T(8,128)} %bitcast.7, f32[8,1024,128]{2,1,0:T(8,128)} %bitcast.10, f32[256,128]{1,0:T(8,128)S(1)} %rest.3.dep_ref.a), custom_call_target="tpu_custom_call" | custom-call | bytes 12582912 | tf_op jit(solution)/shard_map/parts/pallas_call | solution.py:37
  31.5 2.7 %collective-permute-done.9.c = f32[256,128]{1,0:T(8,128)S(1)} collective-permute-done((f32[256,128]{1,0:T(8,128)S(1)}, f32[256,128]{1,0:T(8,128)S(1)}, u32[]{:S(2)}, u32[]{:S(2)}) %collective-permute-start.9) | collective-permute-done | bytes 131104 | tf_op jit(solution)/shard_map/ppermute | solution.py:461
  34.4 0.6 %second.1.a = f32[128,128]{1,0:T(8,128)S(1)} custom-call(f32[2,256,128]{2,1,0:T(8,128)S(1)} %get-tuple-element.24.rhs_ref, f32[256,128]{1,0:T(8,128)S(1)} %rest.3.dep_ref.a, f32[256,128]{1,0:T(8,128)S(1)} %collective-permute-done.8.b, f32[256,128]{1,0:T(8,128)S(1)} %collective-permute-done.9.c, f32[256,128]{1,0:T(8,128)S(1)} %collective-permute-done.10.d, ...), custom_call_target="tpu_custom_call" | custom-call | tf_op jit(solution)/shard_map/second/pallas_call | solution.py:37
  35.3 4.3 %collective-permute-done.13.d = f32[128,128]{1,0:T(8,128)S(1)} collective-permute-done((f32[128,128]{1,0:T(8,128)S(1)}, f32[128,128]{1,0:T(8,128)S(1)}, u32[]{:S(2)}, u32[]{:S(2)}) %collective-permute-start.13) | collective-permute-done | bytes 65568 | tf_op jit(solution)/shard_map/ppermute | solution.py:474
  39.6 0.5 collective-permute-done.12.c
  40.3 3.1 %collective-permute-start.14 = (f32[128,128]{1,0:T(8,128)S(1)}, f32[128,128]{1,0:T(8,128)S(1)}, u32[]{:S(2)}, u32[]{:S(2)}) collective-permute-start(f32[128,128]{1,0:T(8,128)S(1)} %choose.1.a), channel_id=1, source_target_pairs={{0,9},{1,8},{2,11},{3,10},{4,13},{5,12},{6,15},{7,14},{8,25},{9,24... | collective-permute-start | bytes 196616 | tf_op jit(solution)/shard_map/ppermute | solution.py:474
  43.3 1.1 %collective-permute-done.16.d = f32[128,128]{1,0:T(8,128)S(1)} collective-permute-done((f32[128,128]{1,0:T(8,128)S(1)}, f32[128,128]{1,0:T(8,128)S(1)}, u32[]{:S(2)}, u32[]{:S(2)}) %collective-permute-start.16) | collective-permute-done | bytes 65568 | tf_op jit(solution)/shard_map/ppermute | solution.py:474
  44.4 1.6 %collective-permute-done.15.c = f32[128,128]{1,0:T(8,128)S(1)} collective-permute-done((f32[128,128]{1,0:T(8,128)S(1)}, f32[128,128]{1,0:T(8,128)S(1)}, u32[]{:S(2)}, u32[]{:S(2)}) %collective-permute-start.15) | collective-permute-done | bytes 65568 | tf_op jit(solution)/shard_map/ppermute | solution.py:474
  46.0 0.5 collective-permute-done.14.b
  46.5 0.2 deal.1
  46.7 1.2 %collective-permute-done.17.got_ref = f32[128,128]{1,0:T(8,128)S(1)} collective-permute-done((f32[128,128]{1,0:T(8,128)S(1)}, f32[128,128]{1,0:T(8,128)S(1)}, u32[]{:S(2)}, u32[]{:S(2)}) %collective-permute-start.17) | collective-permute-done | bytes 65568 | tf_op jit(solution)/shard_map/ppermute | solution.py:461
  48.0 3.3 %update.1 = (f32[8,1024,128]{2,1,0:T(8,128)}, f32[2,128,128]{2,1,0:T(8,128)}) custom-call(f32[128,128]{1,0:T(8,128)S(1)} %get-tuple-element.32.keep_ref, f32[128,128]{1,0:T(8,128)S(1)} %collective-permute-done.17.got_ref, bf16[4,1024,256]{2,1,0:T(8,128)(2,1)S(1)} %get-tuple-element.30.dep3.ph0, bf16[4,1024,256]{2,1,0:T(8,128)(2,1)S(1)} %get-tuple-element.34.pl0, ...), custom_call_target="tpu_custom_call" | custom-call | tf_op jit(solution)/shard_map/update/pallas_call | solution.py:37
  (20 shorter events, 1.0 us)
Async XLA Ops:
  2.2 2.8 %collective-permute-start = (f32[2,256,128]{2,1,0:T(8,128)S(1)}, f32[2,256,128]{2,1,0:T(8,128)S(1)}, u32[]{:S(2)}, u32[]{:S(2)}) collective-permute-start(f32[2,256,128]{2,1,0:T(8,128)S(1)} %get-tuple-element.22.dep_ref), channel_id=1, source_target_pairs={{0,1},{1,0},{2,3},{3,2},{4,5},{5,4},{6,7},{7,6},{8,9},{9,8},{10,11... | collective-permute-start | bytes 786440 | tf_op jit(solution)/shard_map/ppermute | solution.py:461
  5.0 6.2 %collective-permute-start.1 = (f32[256,128]{1,0:T(8,128)S(1)}, f32[256,128]{1,0:T(8,128)S(1)}, u32[]{:S(2)}, u32[]{:S(2)}) collective-permute-start(f32[256,128]{1,0:T(8,128)S(1)} %get-tuple-element.25), channel_id=1, source_target_pairs={{0,9},{1,8},{2,11},{3,10},{4,13},{5,12},{6,15},{7,14},{8,1},{9,0},... | collective-permute-start | bytes 393224 | tf_op jit(solution)/shard_map/ppermute | solution.py:461
  6.9 14.9 %collective-permute-start.6 = (f32[1024,128]{1,0:T(8,128)S(1)}, f32[1024,128]{1,0:T(8,128)S(1)}, u32[]{:S(2)}, u32[]{:S(2)}) collective-permute-start(f32[1024,128]{1,0:T(8,128)S(1)} %tile.1.dep_ref.own_ref), channel_id=1, source_target_pairs={{0,9},{1,8},{2,11},{3,10},{4,13},{5,12},{6,15},{7,14},{8,1},{9,0},... | collective-permute-start | bytes 1572872 | tf_op jit(solution)/shard_map/ppermute | solution.py:461
  11.2 11.1 %collective-permute-start.5 = (f32[2,128,1024]{2,1,0:T(8,128)S(1)}, f32[2,128,1024]{2,1,0:T(8,128)S(1)}, u32[]{:S(2)}, u32[]{:S(2)}) collective-permute-start(f32[2,128,1024]{2,1,0:T(8,128)S(1)} %get-tuple-element.29.own_ref), channel_id=1, source_target_pairs={{0,1},{1,0},{2,3},{3,2},{4,5},{5,4},{6,7},{7,6},{8,9},{9,8},{10,11... | collective-permute-start | bytes 3145736 | tf_op jit(solution)/shard_map/ppermute | solution.py:461
  11.3 10.5 %collective-permute-start.4 = (f32[256,128]{1,0:T(8,128)S(1)}, f32[256,128]{1,0:T(8,128)S(1)}, u32[]{:S(2)}, u32[]{:S(2)}) collective-permute-start(f32[256,128]{1,0:T(8,128)S(1)} %get-tuple-element.28.a.dep_ref), channel_id=1, source_target_pairs={{0,4},{1,5},{2,6},{3,7},{4,0},{5,1},{6,2},{7,3},{8,12},{9,13},{10,... | collective-permute-start | bytes 393224 | tf_op jit(solution)/shard_map/ppermute | solution.py:461
  14.3 7.5 %collective-permute-start.3 = (f32[256,128]{1,0:T(8,128)S(1)}, f32[256,128]{1,0:T(8,128)S(1)}, u32[]{:S(2)}, u32[]{:S(2)}) collective-permute-start(f32[256,128]{1,0:T(8,128)S(1)} %get-tuple-element.28.a.dep_ref), channel_id=1, source_target_pairs={{0,3},{1,2},{2,1},{3,0},{4,7},{5,6},{6,5},{7,4},{8,11},{9,10},{10,... | collective-permute-start | bytes 393224 | tf_op jit(solution)/shard_map/ppermute | solution.py:461
  15.3 6.5 %collective-permute-start.2 = (f32[256,128]{1,0:T(8,128)S(1)}, f32[256,128]{1,0:T(8,128)S(1)}, u32[]{:S(2)}, u32[]{:S(2)}) collective-permute-start(f32[256,128]{1,0:T(8,128)S(1)} %get-tuple-element.28.a.dep_ref), channel_id=1, source_target_pairs={{0,7},{1,6},{2,5},{3,4},{4,3},{5,2},{6,1},{7,0},{8,15},{9,14},{10,... | collective-permute-start | bytes 393224 | tf_op jit(solution)/shard_map/ppermute | solution.py:461
  21.9 2.0 %collective-permute-start.7 = (f32[1024,128]{1,0:T(8,128)S(1)}, f32[1024,128]{1,0:T(8,128)S(1)}, u32[]{:S(2)}, u32[]{:S(2)}) collective-permute-start(f32[1024,128]{1,0:T(8,128)S(1)} %odd.1.tile_ref), channel_id=1, source_target_pairs={{0,1},{1,0},{2,3},{3,2},{4,5},{5,4},{6,7},{7,6},{8,9},{9,8},{10,11... | collective-permute-start | bytes 1572872 | tf_op jit(solution)/shard_map/ppermute | solution.py:461
  24.3 7.2 %collective-permute-start.10 = (f32[256,128]{1,0:T(8,128)S(1)}, f32[256,128]{1,0:T(8,128)S(1)}, u32[]{:S(2)}, u32[]{:S(2)}) collective-permute-start(f32[256,128]{1,0:T(8,128)S(1)} %rest.3.dep_ref.a), channel_id=1, source_target_pairs={{0,4},{1,5},{2,6},{3,7},{4,0},{5,1},{6,2},{7,3},{8,12},{9,13},{10,... | collective-permute-start | bytes 393224 | tf_op jit(solution)/shard_map/ppermute | solution.py:461
  27.3 7.0 %collective-permute-start.9 = (f32[256,128]{1,0:T(8,128)S(1)}, f32[256,128]{1,0:T(8,128)S(1)}, u32[]{:S(2)}, u32[]{:S(2)}) collective-permute-start(f32[256,128]{1,0:T(8,128)S(1)} %rest.3.dep_ref.a), channel_id=1, source_target_pairs={{0,3},{1,2},{2,1},{3,0},{4,7},{5,6},{6,5},{7,4},{8,11},{9,10},{10,... | collective-permute-start | bytes 393224 | tf_op jit(solution)/shard_map/ppermute | solution.py:461
  28.2 6.2 %collective-permute-start.8 = (f32[256,128]{1,0:T(8,128)S(1)}, f32[256,128]{1,0:T(8,128)S(1)}, u32[]{:S(2)}, u32[]{:S(2)}) collective-permute-start(f32[256,128]{1,0:T(8,128)S(1)} %rest.3.dep_ref.a), channel_id=1, source_target_pairs={{0,7},{1,6},{2,5},{3,4},{4,3},{5,2},{6,1},{7,0},{8,15},{9,14},{10,... | collective-permute-start | bytes 393224 | tf_op jit(solution)/shard_map/ppermute | solution.py:461
  35.0 4.6 %collective-permute-start.13 = (f32[128,128]{1,0:T(8,128)S(1)}, f32[128,128]{1,0:T(8,128)S(1)}, u32[]{:S(2)}, u32[]{:S(2)}) collective-permute-start(f32[128,128]{1,0:T(8,128)S(1)} %second.1.a), channel_id=1, source_target_pairs={{0,33},{1,32},{2,35},{3,34},{4,37},{5,36},{6,39},{7,38},{8,41},{9,... | collective-permute-start | bytes 196616 | tf_op jit(solution)/shard_map/ppermute | solution.py:474
  35.1 5.0 %collective-permute-start.12 = (f32[128,128]{1,0:T(8,128)S(1)}, f32[128,128]{1,0:T(8,128)S(1)}, u32[]{:S(2)}, u32[]{:S(2)}) collective-permute-start(f32[128,128]{1,0:T(8,128)S(1)} %second.1.a), channel_id=1, source_target_pairs={{0,97},{1,96},{2,99},{3,98},{4,101},{5,100},{6,103},{7,102},{8,105... | collective-permute-start | bytes 196616 | tf_op jit(solution)/shard_map/ppermute | solution.py:474
  35.2 4.9 %collective-permute-start.11 = (f32[128,128]{1,0:T(8,128)S(1)}, f32[128,128]{1,0:T(8,128)S(1)}, u32[]{:S(2)}, u32[]{:S(2)}) collective-permute-start(f32[128,128]{1,0:T(8,128)S(1)} %second.1.a), channel_id=1, source_target_pairs={{0,65},{1,64},{2,67},{3,66},{4,69},{5,68},{6,71},{7,70},{8,73},{9,... | collective-permute-start | bytes 196616 | tf_op jit(solution)/shard_map/ppermute | solution.py:474
  40.1 4.3 %collective-permute-start.16 = (f32[128,128]{1,0:T(8,128)S(1)}, f32[128,128]{1,0:T(8,128)S(1)}, u32[]{:S(2)}, u32[]{:S(2)}) collective-permute-start(f32[128,128]{1,0:T(8,128)S(1)} %choose.1.a), channel_id=1, source_target_pairs={{0,17},{1,16},{2,19},{3,18},{4,21},{5,20},{6,23},{7,22},{8,1},{9,0... | collective-permute-start | bytes 196616 | tf_op jit(solution)/shard_map/ppermute | solution.py:474
  40.2 5.8 %collective-permute-start.15 = (f32[128,128]{1,0:T(8,128)S(1)}, f32[128,128]{1,0:T(8,128)S(1)}, u32[]{:S(2)}, u32[]{:S(2)}) collective-permute-start(f32[128,128]{1,0:T(8,128)S(1)} %choose.1.a), channel_id=1, source_target_pairs={{0,25},{1,24},{2,27},{3,26},{4,29},{5,28},{6,31},{7,30},{8,17},{9,... | collective-permute-start | bytes 196616 | tf_op jit(solution)/shard_map/ppermute | solution.py:474
  40.3 6.2 %collective-permute-start.14 = (f32[128,128]{1,0:T(8,128)S(1)}, f32[128,128]{1,0:T(8,128)S(1)}, u32[]{:S(2)}, u32[]{:S(2)}) collective-permute-start(f32[128,128]{1,0:T(8,128)S(1)} %choose.1.a), channel_id=1, source_target_pairs={{0,9},{1,8},{2,11},{3,10},{4,13},{5,12},{6,15},{7,14},{8,25},{9,24... | collective-permute-start | bytes 196616 | tf_op jit(solution)/shard_map/ppermute | solution.py:474
  46.6 1.3 %collective-permute-start.17 = (f32[128,128]{1,0:T(8,128)S(1)}, f32[128,128]{1,0:T(8,128)S(1)}, u32[]{:S(2)}, u32[]{:S(2)}) collective-permute-start(f32[128,128]{1,0:T(8,128)S(1)} %get-tuple-element.33), channel_id=1, source_target_pairs={{0,1},{1,0},{2,3},{3,2},{4,5},{5,4},{6,7},{7,6},{8,9},{9,8},{10,11... | collective-permute-start | bytes 196616 | tf_op jit(solution)/shard_map/ppermute | solution.py:461

commit v7 on v6

--- a/solution.py
+++ b/solution.py
@@ -10,7 +10,7 @@
 F32 = jnp.float32
 BF16 = jnp.bfloat16
 NZ = 4
-X_STEPS = (0, 2, 3, 1)
+X_STEPS = (0, 1, 2, 3)
 W = 128
 NB = 1024
 PACK = NB // 4
@@ -335,7 +335,8 @@
 def parts_kernel(group, panel_ref, p_ref, dep_ref, hi_ref, lo_ref, part_ref, buf, sem):
     bring = pltpu.make_async_copy(p_ref.at[pl.ds(group * GROUP, GROUP)], part_ref, sem.at[GROUP])
     copies = [
-        pltpu.make_async_copy(panel_ref.at[group * GROUP + l], buf.at[l], sem.at[l]) for l in range(GROUP)
+        pltpu.make_async_copy(panel_ref.at[group * GROUP + l], buf.at[l, pl.ds(0, 2 * NB), :], sem.at[l])
+        for l in range(GROUP)
     ]
     for c in copies:
         c.start()
@@ -357,7 +358,7 @@
         (out, out, vm((GROUP, NB, W))),
         hbm=(panel, partials),
         deps=(dep,),
-        scratch=[pltpu.VMEM((GROUP, 2 * NB, W), F32), pltpu.SemaphoreType.DMA((GROUP + 1,))],
+        scratch=[pltpu.VMEM((GROUP, 2 * NB + 8, W), F32), pltpu.SemaphoreType.DMA((GROUP + 1,))],
         mib=6,
         mb=12,
     )

time: 51.4 us -> 51.4 us (level)
  starting transfers between devices: 16.2 us -> 17.9 us
  waiting for transfers between devices: 17.9 us -> 16.3 us
    ppermute x6, starting transfers between devices: 3.46 us -> 5.11 us  [step(): return lax.ppermute(x, ('row', 'col'), pairs)]
    ppermute x6, waiting for transfers between devices: 7.96 us -> 6.36 us  [step(): return lax.ppermute(x, ('row', 'col'), pairs)]
where the time goes in v7:
time: 51.4 us; the launch traced here: 51.3 us
  starting transfers between devices  17.9 us (35%)
  Pallas kernels  16.3 us (32%)
  waiting for transfers between devices  16.3 us (32%)
  between operations  0.81 us (2%)
    pallas_call x16, Pallas kernels, call(): pl.pallas_call(kernel, out_shape=out, in_specs=[ANY] * len(hbm) + [VMEM]...  16.3 us
    ppermute x12, starting transfers between devices, exchange(): return lax.ppermute(x, ('row', 'col'), pairs)  12.8 us
    ppermute x12, waiting for transfers between devices, exchange(): return lax.ppermute(x, ('row', 'col'), pairs)  9.91 us
    ppermute x6, waiting for transfers between devices, step(): return lax.ppermute(x, ('row', 'col'), pairs)  6.36 us
    ppermute x6, starting transfers between devices, step(): return lax.ppermute(x, ('row', 'col'), pairs)  5.11 us
  transfers between devices with their start and end apart: 18, of which 11 were waited for; matrix products, arithmetic and copies ran while one was open for 0% of the time, Pallas kernels for 20%

profile of v7, /device:TPU:1, one launch (start us, length us, event | category | flops | bytes accessed | tf_op | source)
XLA Modules:
  0.0 51.3 jit_solution(1792190076401868368)
XLA Ops:
  0.6 1.5 %start.1 = (f32[2,256,128]{2,1,0:T(8,128)S(1)}, f32[2,256,128]{2,1,0:T(8,128)S(1)}) custom-call(f32[8,1024,128]{2,1,0:T(8,128)} %bitcast.8), custom_call_target="tpu_custom_call" | custom-call | tf_op jit(solution)/shard_map/start/pallas_call | solution.py:37
  2.2 1.5 %collective-permute-start = (f32[2,256,128]{2,1,0:T(8,128)S(1)}, f32[2,256,128]{2,1,0:T(8,128)S(1)}, u32[]{:S(2)}, u32[]{:S(2)}) collective-permute-start(f32[2,256,128]{2,1,0:T(8,128)S(1)} %get-tuple-element.22.dep_ref), channel_id=1, source_target_pairs={{0,1},{1,0},{2,3},{3,2},{4,5},{5,4},{6,7},{7,6},{8,9},{9,8},{10,11... | collective-permute-start | bytes 786440 | tf_op jit(solution)/shard_map/ppermute | solution.py:462
  3.7 1.3 %tile.1.dep_ref.own_ref = f32[1024,128]{1,0:T(8,128)S(1)} custom-call(f32[8,2048,128]{2,1,0:T(8,128)} %bitcast.5, f32[2,256,128]{2,1,0:T(8,128)S(1)} %get-tuple-element.22.dep_ref), custom_call_target="tpu_custom_call" | custom-call | bytes 8388608 | tf_op jit(solution)/shard_map/tile/pallas_call | solution.py:37
  5.0 1.9 %collective-permute-start.1 = (f32[256,128]{1,0:T(8,128)S(1)}, f32[256,128]{1,0:T(8,128)S(1)}, u32[]{:S(2)}, u32[]{:S(2)}) collective-permute-start(f32[256,128]{1,0:T(8,128)S(1)} %get-tuple-element.25), channel_id=1, source_target_pairs={{0,9},{1,8},{2,11},{3,10},{4,13},{5,12},{6,15},{7,14},{8,1},{9,0},... | collective-permute-start | bytes 393224 | tf_op jit(solution)/shard_map/ppermute | solution.py:462
  7.0 1.8 %prep.1 = (f32[2,128,1024]{2,1,0:T(8,128)S(1)}, f32[2,256,128]{2,1,0:T(8,128)S(1)}) custom-call(f32[2,128,1024]{2,1,0:T(8,128)} %inv_ref.1, f32[2,1024,128]{2,1,0:T(8,128)} %rhs_ref.1, f32[256,128]{1,0:T(8,128)S(1)} %get-tuple-element.23.dep_ref.mine_ref), custom_call_target="tpu_custom_call" | custom-call | bytes 8388608 | tf_op jit(solution)/shard_map/prep/pallas_call | solution.py:37
  8.8 2.3 %collective-permute-done.1.got_ref = f32[256,128]{1,0:T(8,128)S(1)} collective-permute-done((f32[256,128]{1,0:T(8,128)S(1)}, f32[256,128]{1,0:T(8,128)S(1)}, u32[]{:S(2)}, u32[]{:S(2)}) %collective-permute-start.1) | collective-permute-done | bytes 131104 | tf_op jit(solution)/shard_map/ppermute | solution.py:462
  11.3 3.0 %collective-permute-start.4 = (f32[256,128]{1,0:T(8,128)S(1)}, f32[256,128]{1,0:T(8,128)S(1)}, u32[]{:S(2)}, u32[]{:S(2)}) collective-permute-start(f32[256,128]{1,0:T(8,128)S(1)} %get-tuple-element.28.a.dep_ref), channel_id=1, source_target_pairs={{0,4},{1,5},{2,6},{3,7},{4,0},{5,1},{6,2},{7,3},{8,12},{9,13},{10,... | collective-permute-start | bytes 393224 | tf_op jit(solution)/shard_map/ppermute | solution.py:462
  14.3 1.0 %collective-permute-start.3 = (f32[256,128]{1,0:T(8,128)S(1)}, f32[256,128]{1,0:T(8,128)S(1)}, u32[]{:S(2)}, u32[]{:S(2)}) collective-permute-start(f32[256,128]{1,0:T(8,128)S(1)} %get-tuple-element.28.a.dep_ref), channel_id=1, source_target_pairs={{0,3},{1,2},{2,1},{3,0},{4,7},{5,6},{6,5},{7,4},{8,11},{9,10},{10,... | collective-permute-start | bytes 393224 | tf_op jit(solution)/shard_map/ppermute | solution.py:462
  15.3 0.4 collective-permute-start.2
  15.7 2.9 %parts.2 = (bf16[4,1024,256]{2,1,0:T(8,128)(2,1)S(1)}, bf16[4,1024,256]{2,1,0:T(8,128)(2,1)S(1)}, f32[4,1024,128]{2,1,0:T(8,128)S(1)}) custom-call(f32[8,2048,128]{2,1,0:T(8,128)} %bitcast.6, f32[8,1024,128]{2,1,0:T(8,128)} %bitcast.9, f32[256,128]{1,0:T(8,128)S(1)} %get-tuple-element.28.a.dep_ref), custom_call_target="tpu_custom_call" | custom-call | bytes 12582912 | tf_op jit(solution)/shard_map/parts/pallas_call | solution.py:37
  18.6 3.2 %collective-permute-done.6.got_ref = f32[1024,128]{1,0:T(8,128)S(1)} collective-permute-done((f32[1024,128]{1,0:T(8,128)S(1)}, f32[1024,128]{1,0:T(8,128)S(1)}, u32[]{:S(2)}, u32[]{:S(2)}) %collective-permute-start.6) | collective-permute-done | bytes 524320 | tf_op jit(solution)/shard_map/ppermute | solution.py:462
  21.9 0.4 collective-permute-start.7
  22.3 0.3 rows.1.inv_ref
  22.6 0.6 %first.1.y_ref = f32[2,128,128]{2,1,0:T(8,128)S(1)} custom-call(f32[2,256,128]{2,1,0:T(8,128)S(1)} %get-tuple-element.24.rhs_ref, f32[256,128]{1,0:T(8,128)S(1)} %get-tuple-element.28.a.dep_ref, f32[256,128]{1,0:T(8,128)S(1)} %collective-permute-done.2.b.dep0, f32[256,128]{1,0:T(8,128)S(1)} %collective-permute-done.3.c.dep1, ...), custom_call_target="tpu_custom_call" | custom-call | tf_op jit(solution)/shard_map/first/pallas_call | solution.py:37
  23.2 0.4 rest.2.u_ref
  23.7 0.2 collective-permute-done.7.tile_ref
  23.9 0.4 rest.3.dep_ref.a
  24.3 3.0 %collective-permute-start.10 = (f32[256,128]{1,0:T(8,128)S(1)}, f32[256,128]{1,0:T(8,128)S(1)}, u32[]{:S(2)}, u32[]{:S(2)}) collective-permute-start(f32[256,128]{1,0:T(8,128)S(1)} %rest.3.dep_ref.a), channel_id=1, source_target_pairs={{0,4},{1,5},{2,6},{3,7},{4,0},{5,1},{6,2},{7,3},{8,12},{9,13},{10,... | collective-permute-start | bytes 393224 | tf_op jit(solution)/shard_map/ppermute | solution.py:462
  27.3 0.9 %collective-permute-start.9 = (f32[256,128]{1,0:T(8,128)S(1)}, f32[256,128]{1,0:T(8,128)S(1)}, u32[]{:S(2)}, u32[]{:S(2)}) collective-permute-start(f32[256,128]{1,0:T(8,128)S(1)} %rest.3.dep_ref.a), channel_id=1, source_target_pairs={{0,3},{1,2},{2,1},{3,0},{4,7},{5,6},{6,5},{7,4},{8,11},{9,10},{10,... | collective-permute-start | bytes 393224 | tf_op jit(solution)/shard_map/ppermute | solution.py:462
  28.2 0.4 collective-permute-start.8
  28.6 2.9 %parts.3 = (bf16[4,1024,256]{2,1,0:T(8,128)(2,1)S(1)}, bf16[4,1024,256]{2,1,0:T(8,128)(2,1)S(1)}, f32[4,1024,128]{2,1,0:T(8,128)S(1)}) custom-call(f32[8,2048,128]{2,1,0:T(8,128)} %bitcast.7, f32[8,1024,128]{2,1,0:T(8,128)} %bitcast.10, f32[256,128]{1,0:T(8,128)S(1)} %rest.3.dep_ref.a), custom_call_target="tpu_custom_call" | custom-call | bytes 12582912 | tf_op jit(solution)/shard_map/parts/pallas_call | solution.py:37
  31.5 2.7 %collective-permute-done.9.c = f32[256,128]{1,0:T(8,128)S(1)} collective-permute-done((f32[256,128]{1,0:T(8,128)S(1)}, f32[256,128]{1,0:T(8,128)S(1)}, u32[]{:S(2)}, u32[]{:S(2)}) %collective-permute-start.9) | collective-permute-done | bytes 131104 | tf_op jit(solution)/shard_map/ppermute | solution.py:462
  34.4 0.6 %second.1.a = f32[128,128]{1,0:T(8,128)S(1)} custom-call(f32[2,256,128]{2,1,0:T(8,128)S(1)} %get-tuple-element.24.rhs_ref, f32[256,128]{1,0:T(8,128)S(1)} %rest.3.dep_ref.a, f32[256,128]{1,0:T(8,128)S(1)} %collective-permute-done.8.b, f32[256,128]{1,0:T(8,128)S(1)} %collective-permute-done.9.c, f32[256,128]{1,0:T(8,128)S(1)} %collective-permute-done.10.d, ...), custom_call_target="tpu_custom_call" | custom-call | tf_op jit(solution)/shard_map/second/pallas_call | solution.py:37
  35.2 1.7 %collective-permute-start.11 = (f32[128,128]{1,0:T(8,128)S(1)}, f32[128,128]{1,0:T(8,128)S(1)}, u32[]{:S(2)}, u32[]{:S(2)}) collective-permute-start(f32[128,128]{1,0:T(8,128)S(1)} %second.1.a), channel_id=1, source_target_pairs={{0,33},{1,32},{2,35},{3,34},{4,37},{5,36},{6,39},{7,38},{8,41},{9,... | collective-permute-start | bytes 196616 | tf_op jit(solution)/shard_map/ppermute | solution.py:475
  36.9 3.1 %collective-permute-done.13.d = f32[128,128]{1,0:T(8,128)S(1)} collective-permute-done((f32[128,128]{1,0:T(8,128)S(1)}, f32[128,128]{1,0:T(8,128)S(1)}, u32[]{:S(2)}, u32[]{:S(2)}) %collective-permute-start.13) | collective-permute-done | bytes 65568 | tf_op jit(solution)/shard_map/ppermute | solution.py:475
  40.0 0.2 collective-permute-done.11.b
  40.3 3.1 %collective-permute-start.14 = (f32[128,128]{1,0:T(8,128)S(1)}, f32[128,128]{1,0:T(8,128)S(1)}, u32[]{:S(2)}, u32[]{:S(2)}) collective-permute-start(f32[128,128]{1,0:T(8,128)S(1)} %choose.1.a), channel_id=1, source_target_pairs={{0,9},{1,8},{2,11},{3,10},{4,13},{5,12},{6,15},{7,14},{8,25},{9,24... | collective-permute-start | bytes 196616 | tf_op jit(solution)/shard_map/ppermute | solution.py:475
  43.4 1.0 %collective-permute-done.16.d = f32[128,128]{1,0:T(8,128)S(1)} collective-permute-done((f32[128,128]{1,0:T(8,128)S(1)}, f32[128,128]{1,0:T(8,128)S(1)}, u32[]{:S(2)}, u32[]{:S(2)}) %collective-permute-start.16) | collective-permute-done | bytes 65568 | tf_op jit(solution)/shard_map/ppermute | solution.py:475
  44.4 1.6 %collective-permute-done.15.c = f32[128,128]{1,0:T(8,128)S(1)} collective-permute-done((f32[128,128]{1,0:T(8,128)S(1)}, f32[128,128]{1,0:T(8,128)S(1)}, u32[]{:S(2)}, u32[]{:S(2)}) %collective-permute-start.15) | collective-permute-done | bytes 65568 | tf_op jit(solution)/shard_map/ppermute | solution.py:475
  46.1 0.4 collective-permute-done.14.b
  46.8 1.2 %collective-permute-done.17.got_ref = f32[128,128]{1,0:T(8,128)S(1)} collective-permute-done((f32[128,128]{1,0:T(8,128)S(1)}, f32[128,128]{1,0:T(8,128)S(1)}, u32[]{:S(2)}, u32[]{:S(2)}) %collective-permute-start.17) | collective-permute-done | bytes 65568 | tf_op jit(solution)/shard_map/ppermute | solution.py:462
  48.0 3.3 %update.1 = (f32[8,1024,128]{2,1,0:T(8,128)}, f32[2,128,128]{2,1,0:T(8,128)}) custom-call(f32[128,128]{1,0:T(8,128)S(1)} %get-tuple-element.32.keep_ref, f32[128,128]{1,0:T(8,128)S(1)} %collective-permute-done.17.got_ref, bf16[4,1024,256]{2,1,0:T(8,128)(2,1)S(1)} %get-tuple-element.30.dep3.ph0, bf16[4,1024,256]{2,1,0:T(8,128)(2,1)S(1)} %get-tuple-element.34.pl0, ...), custom_call_target="tpu_custom_call" | custom-call | tf_op jit(solution)/shard_map/update/pallas_call | solution.py:37
  (20 shorter events, 0.9 us)
Async XLA Ops:
  2.2 2.8 %collective-permute-start = (f32[2,256,128]{2,1,0:T(8,128)S(1)}, f32[2,256,128]{2,1,0:T(8,128)S(1)}, u32[]{:S(2)}, u32[]{:S(2)}) collective-permute-start(f32[2,256,128]{2,1,0:T(8,128)S(1)} %get-tuple-element.22.dep_ref), channel_id=1, source_target_pairs={{0,1},{1,0},{2,3},{3,2},{4,5},{5,4},{6,7},{7,6},{8,9},{9,8},{10,11... | collective-permute-start | bytes 786440 | tf_op jit(solution)/shard_map/ppermute | solution.py:462
  5.0 6.2 %collective-permute-start.1 = (f32[256,128]{1,0:T(8,128)S(1)}, f32[256,128]{1,0:T(8,128)S(1)}, u32[]{:S(2)}, u32[]{:S(2)}) collective-permute-start(f32[256,128]{1,0:T(8,128)S(1)} %get-tuple-element.25), channel_id=1, source_target_pairs={{0,9},{1,8},{2,11},{3,10},{4,13},{5,12},{6,15},{7,14},{8,1},{9,0},... | collective-permute-start | bytes 393224 | tf_op jit(solution)/shard_map/ppermute | solution.py:462
  6.9 14.9 %collective-permute-start.6 = (f32[1024,128]{1,0:T(8,128)S(1)}, f32[1024,128]{1,0:T(8,128)S(1)}, u32[]{:S(2)}, u32[]{:S(2)}) collective-permute-start(f32[1024,128]{1,0:T(8,128)S(1)} %tile.1.dep_ref.own_ref), channel_id=1, source_target_pairs={{0,9},{1,8},{2,11},{3,10},{4,13},{5,12},{6,15},{7,14},{8,1},{9,0},... | collective-permute-start | bytes 1572872 | tf_op jit(solution)/shard_map/ppermute | solution.py:462
  11.2 11.1 %collective-permute-start.5 = (f32[2,128,1024]{2,1,0:T(8,128)S(1)}, f32[2,128,1024]{2,1,0:T(8,128)S(1)}, u32[]{:S(2)}, u32[]{:S(2)}) collective-permute-start(f32[2,128,1024]{2,1,0:T(8,128)S(1)} %get-tuple-element.29.own_ref), channel_id=1, source_target_pairs={{0,1},{1,0},{2,3},{3,2},{4,5},{5,4},{6,7},{7,6},{8,9},{9,8},{10,11... | collective-permute-start | bytes 3145736 | tf_op jit(solution)/shard_map/ppermute | solution.py:462
  11.3 10.5 %collective-permute-start.4 = (f32[256,128]{1,0:T(8,128)S(1)}, f32[256,128]{1,0:T(8,128)S(1)}, u32[]{:S(2)}, u32[]{:S(2)}) collective-permute-start(f32[256,128]{1,0:T(8,128)S(1)} %get-tuple-element.28.a.dep_ref), channel_id=1, source_target_pairs={{0,4},{1,5},{2,6},{3,7},{4,0},{5,1},{6,2},{7,3},{8,12},{9,13},{10,... | collective-permute-start | bytes 393224 | tf_op jit(solution)/shard_map/ppermute | solution.py:462
  14.3 7.5 %collective-permute-start.3 = (f32[256,128]{1,0:T(8,128)S(1)}, f32[256,128]{1,0:T(8,128)S(1)}, u32[]{:S(2)}, u32[]{:S(2)}) collective-permute-start(f32[256,128]{1,0:T(8,128)S(1)} %get-tuple-element.28.a.dep_ref), channel_id=1, source_target_pairs={{0,3},{1,2},{2,1},{3,0},{4,7},{5,6},{6,5},{7,4},{8,11},{9,10},{10,... | collective-permute-start | bytes 393224 | tf_op jit(solution)/shard_map/ppermute | solution.py:462
  15.3 6.5 %collective-permute-start.2 = (f32[256,128]{1,0:T(8,128)S(1)}, f32[256,128]{1,0:T(8,128)S(1)}, u32[]{:S(2)}, u32[]{:S(2)}) collective-permute-start(f32[256,128]{1,0:T(8,128)S(1)} %get-tuple-element.28.a.dep_ref), channel_id=1, source_target_pairs={{0,7},{1,6},{2,5},{3,4},{4,3},{5,2},{6,1},{7,0},{8,15},{9,14},{10,... | collective-permute-start | bytes 393224 | tf_op jit(solution)/shard_map/ppermute | solution.py:462
  21.9 2.0 %collective-permute-start.7 = (f32[1024,128]{1,0:T(8,128)S(1)}, f32[1024,128]{1,0:T(8,128)S(1)}, u32[]{:S(2)}, u32[]{:S(2)}) collective-permute-start(f32[1024,128]{1,0:T(8,128)S(1)} %odd.1.tile_ref), channel_id=1, source_target_pairs={{0,1},{1,0},{2,3},{3,2},{4,5},{5,4},{6,7},{7,6},{8,9},{9,8},{10,11... | collective-permute-start | bytes 1572872 | tf_op jit(solution)/shard_map/ppermute | solution.py:462
  24.3 7.2 %collective-permute-start.10 = (f32[256,128]{1,0:T(8,128)S(1)}, f32[256,128]{1,0:T(8,128)S(1)}, u32[]{:S(2)}, u32[]{:S(2)}) collective-permute-start(f32[256,128]{1,0:T(8,128)S(1)} %rest.3.dep_ref.a), channel_id=1, source_target_pairs={{0,4},{1,5},{2,6},{3,7},{4,0},{5,1},{6,2},{7,3},{8,12},{9,13},{10,... | collective-permute-start | bytes 393224 | tf_op jit(solution)/shard_map/ppermute | solution.py:462
  27.3 7.0 %collective-permute-start.9 = (f32[256,128]{1,0:T(8,128)S(1)}, f32[256,128]{1,0:T(8,128)S(1)}, u32[]{:S(2)}, u32[]{:S(2)}) collective-permute-start(f32[256,128]{1,0:T(8,128)S(1)} %rest.3.dep_ref.a), channel_id=1, source_target_pairs={{0,3},{1,2},{2,1},{3,0},{4,7},{5,6},{6,5},{7,4},{8,11},{9,10},{10,... | collective-permute-start | bytes 393224 | tf_op jit(solution)/shard_map/ppermute | solution.py:462
  28.2 6.2 %collective-permute-start.8 = (f32[256,128]{1,0:T(8,128)S(1)}, f32[256,128]{1,0:T(8,128)S(1)}, u32[]{:S(2)}, u32[]{:S(2)}) collective-permute-start(f32[256,128]{1,0:T(8,128)S(1)} %rest.3.dep_ref.a), channel_id=1, source_target_pairs={{0,7},{1,6},{2,5},{3,4},{4,3},{5,2},{6,1},{7,0},{8,15},{9,14},{10,... | collective-permute-start | bytes 393224 | tf_op jit(solution)/shard_map/ppermute | solution.py:462
  35.0 5.0 %collective-permute-start.13 = (f32[128,128]{1,0:T(8,128)S(1)}, f32[128,128]{1,0:T(8,128)S(1)}, u32[]{:S(2)}, u32[]{:S(2)}) collective-permute-start(f32[128,128]{1,0:T(8,128)S(1)} %second.1.a), channel_id=1, source_target_pairs={{0,97},{1,96},{2,99},{3,98},{4,101},{5,100},{6,103},{7,102},{8,105... | collective-permute-start | bytes 196616 | tf_op jit(solution)/shard_map/ppermute | solution.py:475
  35.1 4.9 %collective-permute-start.12 = (f32[128,128]{1,0:T(8,128)S(1)}, f32[128,128]{1,0:T(8,128)S(1)}, u32[]{:S(2)}, u32[]{:S(2)}) collective-permute-start(f32[128,128]{1,0:T(8,128)S(1)} %second.1.a), channel_id=1, source_target_pairs={{0,65},{1,64},{2,67},{3,66},{4,69},{5,68},{6,71},{7,70},{8,73},{9,... | collective-permute-start | bytes 196616 | tf_op jit(solution)/shard_map/ppermute | solution.py:475
  35.2 5.0 %collective-permute-start.11 = (f32[128,128]{1,0:T(8,128)S(1)}, f32[128,128]{1,0:T(8,128)S(1)}, u32[]{:S(2)}, u32[]{:S(2)}) collective-permute-start(f32[128,128]{1,0:T(8,128)S(1)} %second.1.a), channel_id=1, source_target_pairs={{0,33},{1,32},{2,35},{3,34},{4,37},{5,36},{6,39},{7,38},{8,41},{9,... | collective-permute-start | bytes 196616 | tf_op jit(solution)/shard_map/ppermute | solution.py:475
  40.2 4.3 %collective-permute-start.16 = (f32[128,128]{1,0:T(8,128)S(1)}, f32[128,128]{1,0:T(8,128)S(1)}, u32[]{:S(2)}, u32[]{:S(2)}) collective-permute-start(f32[128,128]{1,0:T(8,128)S(1)} %choose.1.a), channel_id=1, source_target_pairs={{0,17},{1,16},{2,19},{3,18},{4,21},{5,20},{6,23},{7,22},{8,1},{9,0... | collective-permute-start | bytes 196616 | tf_op jit(solution)/shard_map/ppermute | solution.py:475
  40.2 5.9 %collective-permute-start.15 = (f32[128,128]{1,0:T(8,128)S(1)}, f32[128,128]{1,0:T(8,128)S(1)}, u32[]{:S(2)}, u32[]{:S(2)}) collective-permute-start(f32[128,128]{1,0:T(8,128)S(1)} %choose.1.a), channel_id=1, source_target_pairs={{0,25},{1,24},{2,27},{3,26},{4,29},{5,28},{6,31},{7,30},{8,17},{9,... | collective-permute-start | bytes 196616 | tf_op jit(solution)/shard_map/ppermute | solution.py:475
  40.3 6.2 %collective-permute-start.14 = (f32[128,128]{1,0:T(8,128)S(1)}, f32[128,128]{1,0:T(8,128)S(1)}, u32[]{:S(2)}, u32[]{:S(2)}) collective-permute-start(f32[128,128]{1,0:T(8,128)S(1)} %choose.1.a), channel_id=1, source_target_pairs={{0,9},{1,8},{2,11},{3,10},{4,13},{5,12},{6,15},{7,14},{8,25},{9,24... | collective-permute-start | bytes 196616 | tf_op jit(solution)/shard_map/ppermute | solution.py:475
  46.7 1.3 %collective-permute-start.17 = (f32[128,128]{1,0:T(8,128)S(1)}, f32[128,128]{1,0:T(8,128)S(1)}, u32[]{:S(2)}, u32[]{:S(2)}) collective-permute-start(f32[128,128]{1,0:T(8,128)S(1)} %get-tuple-element.33), channel_id=1, source_target_pairs={{0,1},{1,0},{2,3},{3,2},{4,5},{5,4},{6,7},{7,6},{8,9},{9,8},{10,11... | collective-permute-start | bytes 196616 | tf_op jit(solution)/shard_map/ppermute | solution.py:462

commit v8 on v7

--- a/solution.py
+++ b/solution.py
@@ -164,14 +164,14 @@
     copy = pltpu.make_async_copy(panel_ref.at[0], buf, sem.at[0])
     copy.start()
     copy.wait()
-    out_ref[...] = buf[pl.ds(0, NB, stride=2), :]
+    out_ref[:NB] = buf[pl.ds(0, NB, stride=2), :]
 
 
 def first_tile(panel, dep):
     return call(
         tile_kernel,
         "tile",
-        (vm((NB, W)),),
+        (vm((NB + PACK, W)),),
         hbm=(panel,),
         deps=(dep,),
         scratch=[pltpu.VMEM((2 * NB, W), F32), pltpu.SemaphoreType.DMA((1,))],
@@ -211,35 +211,33 @@
 
 
 @on_chain
-def add_kernel(a_ref, b_ref, dep_ref, mine_ref, other_ref):
+def add_kernel(a_ref, b_ref, _, mine_ref, other_ref, tile_ref):
     r = odd_row()
     mine_ref[...] = a_ref[r] + b_ref[r]
-    other_ref[...] = a_ref[1 - r] + b_ref[1 - r]
-
-
-def add(a, b, dep):
-    return call(add_kernel, "add", (PACKED, PACKED), vmem=(a, b), deps=(dep,))
-
-
-@on_chain
-def order_kernel(mine_ref, got_ref, _, even_ref, odd_ref, same_ref):
+    other = a_ref[1 - r] + b_ref[1 - r]
+    other_ref[...] = other
+    tile_ref[NB:] = other
+
+
+def add(a, b, tile):
+    return call(add_kernel, "add", (PACKED, PACKED, vm(tile.shape)), vmem=(a, b, tile), aliases={2: 2})
+
+
+@on_chain
+def order_kernel(mine_ref, got_ref, _, even_ref, same_ref):
     r = odd_row()
 
     @pl.when(r == 0)
     def _():
         even_ref[...] = mine_ref[...]
-        odd_ref[...] = got_ref[...]
 
     @pl.when(r == 1)
     def _():
         even_ref[...] = got_ref[...]
-        odd_ref[...] = mine_ref[...]
-
-
-def order(mine, got, inv):
-    return call(
-        order_kernel, "order", (PACKED, PACKED, vm(inv.shape)), vmem=(mine, got, inv), aliases={2: 2}
-    )
+
+
+def order(mine, got, rhs):
+    return call(order_kernel, "order", (PACKED, vm(rhs.shape)), vmem=(mine, got, rhs), aliases={2: 1})
 
 
 @on_chain
@@ -248,11 +246,11 @@
 
     @pl.when(r == 1)
     def _():
-        out_ref[...] = own_ref[...]
+        out_ref[...] = own_ref[:NB]
 
     @pl.when(r == 0)
     def _():
-        out_ref[...] = got_ref[...]
+        out_ref[...] = got_ref[:NB]
 
 
 def odd_tile(own, got, deps):
@@ -291,13 +289,24 @@
 
 
 @on_chain
-def rest_kernel(turn, u_ref, y_ref, tile_ref, out_ref):
-    y = jnp.where(odd_row() == turn, y_ref[0], y_ref[1])
+def half_kernel(mine_ref, got_ref, y_ref, tile_ref, out_ref):
+    odd = odd_row() == 1
+    y = jnp.where(odd, y_ref[0], y_ref[1])
+    out_ref[...] = times_tile(jnp.where(odd, mine_ref[...], got_ref[NB:]), tile_ref, y)
+
+
+def half(mine, got, y, tile):
+    return call(half_kernel, "half", (PACKED,), vmem=(mine, got, y, tile), mib=8)[0]
+
+
+@on_chain
+def rest_kernel(u_ref, y_ref, tile_ref, out_ref):
+    y = jnp.where(odd_row() == 1, y_ref[1], y_ref[0])
     out_ref[...] = times_tile(u_ref[...], tile_ref, y)
 
 
-def rest(turn, u, y, tile):
-    return call(functools.partial(rest_kernel, turn), "rest", (PACKED,), vmem=(u, y, tile), mib=8)[0]
+def rest(u, y, tile):
+    return call(rest_kernel, "rest", (PACKED,), vmem=(u, y, tile), mib=8)[0]
 
 
 @on_chain
@@ -475,6 +484,10 @@
     return lax.ppermute(x, ("row", "col"), pairs)
 
 
+def around(cycle):
+    return lambda x, z: cycle.get(x * NZ + z, x * NZ + z)
+
+
 def along_x(y):
     cycles = {1: {0: 1, 1: 0}, 2: {0: 2, 2: 1, 1: 0}, 3: {0: 3, 3: 0}}
     place = lambda m: lambda x, z: (cycles[m].get(x, x) if z < 2 else x) * NZ + z
@@ -488,20 +501,23 @@
 
 
 def per_device(partials, panel, inverse, rhs):
+    inv_got = swap(inverse)
     partials = partials.reshape(8, NB, W)
     panel = panel.reshape(8, 2 * NB, W)
     send, keep = start(partials)
     tile = first_tile(panel, send)
-    tile_odd = exchange(tile, 1, 1)
-    mine, other = add(keep, swap(send), tile)
+    up = around({0: 1, 1: NZ + 1, NZ + 1: NZ, NZ: 0})
+    down = around({1: 0, 0: NZ, NZ: NZ + 1, NZ + 1: 1})
+    mine, other, tile = add(keep, swap(send), tile)
+    tile_odd = step(tile, down)
     inv, rhs = prep(inverse, rhs, mine)
-    even, odd, inv = order(mine, exchange(other, 1, 1), inv)
+    even, rhs = order(mine, step(other, up), rhs)
     parts0 = parts(0, panel, partials, even)
-    inv = inverse_rows(inv, swap(inv))
+    inv = inverse_rows(inv, inv_got)
     sums = chips(even)
     tile = odd_tile(tile, tile_odd, (*sums[1:], parts0[0]))
     y0 = first(rhs, sums, inv)
-    u = rest(0, rest(1, odd, y0, tile), y0, swap(tile))
+    u = rest(half(mine, tile_odd, y0, tile), y0, swap(tile))
     parts1 = parts(1, panel, partials, u)
     y = second(rhs, chips(u), inv, y0, parts1[0])
     keep, send = deal(along_z(choose(along_x(y))))

time: 51.4 us -> 51.4 us (level)
    ppermute x12 -> x10, waiting for transfers between devices: 9.91 us -> 7.61 us  [exchange(): return lax.ppermute(x, ('row', 'col'), pairs)]
    ppermute x6 -> x8, starting transfers between devices: 5.11 us -> 7.36 us  [step(): return lax.ppermute(x, ('row', 'col'), pairs)]
    ppermute x12 -> x10, starting transfers between devices: 12.8 us -> 10.6 us  [exchange(): return lax.ppermute(x, ('row', 'col'), pairs)]
    ppermute x6 -> x8, waiting for transfers between devices: 6.36 us -> 8.44 us  [step(): return lax.ppermute(x, ('row', 'col'), pairs)]
  transfers between devices with their start and end apart: 18 -> 18, of which waited for: 11 -> 12; matrix products, arithmetic and copies ran while one was open for 0% -> 0% of each run, Pallas kernels for 20% -> 20%
where the time goes in v8:
time: 51.4 us; the launch traced here: 51.3 us
  starting transfers between devices  18 us (35%)
  Pallas kernels  16.4 us (32%)
  waiting for transfers between devices  16.1 us (31%)
  between operations  0.81 us (2%)
    pallas_call x16, Pallas kernels, call(): pl.pallas_call(kernel, out_shape=out, in_specs=[ANY] * len(hbm) + [VMEM]...  16.4 us
    ppermute x10, starting transfers between devices, exchange(): return lax.ppermute(x, ('row', 'col'), pairs)  10.6 us
    ppermute x8, waiting for transfers between devices, step(): return lax.ppermute(x, ('row', 'col'), pairs)  8.44 us
    ppermute x10, waiting for transfers between devices, exchange(): return lax.ppermute(x, ('row', 'col'), pairs)  7.61 us
    ppermute x8, starting transfers between devices, step(): return lax.ppermute(x, ('row', 'col'), pairs)  7.36 us
  transfers between devices with their start and end apart: 18, of which 12 were waited for; matrix products, arithmetic and copies ran while one was open for 0% of the time, Pallas kernels for 20%

profile of v8, /device:TPU:1, one launch (start us, length us, event | category | flops | bytes accessed | tf_op | source)
XLA Modules:
  0.0 51.3 jit_solution(16450850908041293993)
XLA Ops:
  0.6 1.5 %start.1 = (f32[2,256,128]{2,1,0:T(8,128)S(1)}, f32[2,256,128]{2,1,0:T(8,128)S(1)}) custom-call(f32[8,1024,128]{2,1,0:T(8,128)} %bitcast.8), custom_call_target="tpu_custom_call" | custom-call | tf_op jit(solution)/shard_map/start/pallas_call | solution.py:37
  2.2 1.5 %collective-permute-start = (f32[2,256,128]{2,1,0:T(8,128)S(1)}, f32[2,256,128]{2,1,0:T(8,128)S(1)}, u32[]{:S(2)}, u32[]{:S(2)}) collective-permute-start(f32[2,256,128]{2,1,0:T(8,128)S(1)} %get-tuple-element.22.dep_ref), channel_id=1, source_target_pairs={{0,1},{1,0},{2,3},{3,2},{4,5},{5,4},{6,7},{7,6},{8,9},{9,8},{10,11... | collective-permute-start | bytes 786440 | tf_op jit(solution)/shard_map/ppermute | solution.py:471
  3.7 1.4 %tile.1._ = f32[1280,128]{1,0:T(8,128)S(1)} custom-call(f32[8,2048,128]{2,1,0:T(8,128)} %bitcast.5, f32[2,256,128]{2,1,0:T(8,128)S(1)} %get-tuple-element.22.dep_ref), custom_call_target="tpu_custom_call" | custom-call | bytes 8388608 | tf_op jit(solution)/shard_map/tile/pallas_call | solution.py:37
  5.2 0.2 collective-permute-start.6
  5.4 2.0 %collective-permute-start.1 = (f32[256,128]{1,0:T(8,128)S(1)}, f32[256,128]{1,0:T(8,128)S(1)}, u32[]{:S(2)}, u32[]{:S(2)}) collective-permute-start(f32[256,128]{1,0:T(8,128)S(1)} %get-tuple-element.24), channel_id=1, source_target_pairs={{0,9},{1,8},{2,11},{3,10},{4,13},{5,12},{6,15},{7,14},{8,41},{9,40... | collective-permute-start | bytes 393224 | tf_op jit(solution)/shard_map/ppermute | solution.py:484
  7.4 1.8 %prep.1 = (f32[2,128,1024]{2,1,0:T(8,128)S(1)}, f32[2,256,128]{2,1,0:T(8,128)S(1)}) custom-call(f32[2,128,1024]{2,1,0:T(8,128)} %inv_ref.1, f32[2,1024,128]{2,1,0:T(8,128)} %rhs_ref.1, f32[256,128]{1,0:T(8,128)S(1)} %get-tuple-element.23.dep_ref.mine_ref), custom_call_target="tpu_custom_call" | custom-call | bytes 8388608 | tf_op jit(solution)/shard_map/prep/pallas_call | solution.py:37
  9.2 2.0 %collective-permute-done.1.got_ref = f32[256,128]{1,0:T(8,128)S(1)} collective-permute-done((f32[256,128]{1,0:T(8,128)S(1)}, f32[256,128]{1,0:T(8,128)S(1)}, u32[]{:S(2)}, u32[]{:S(2)}) %collective-permute-start.1) | collective-permute-done | bytes 131104 | tf_op jit(solution)/shard_map/ppermute | solution.py:484
  11.2 3.1 %collective-permute-start.5 = (f32[256,128]{1,0:T(8,128)S(1)}, f32[256,128]{1,0:T(8,128)S(1)}, u32[]{:S(2)}, u32[]{:S(2)}) collective-permute-start(f32[256,128]{1,0:T(8,128)S(1)} %get-tuple-element.28.a.dep_ref), channel_id=1, source_target_pairs={{0,4},{1,5},{2,6},{3,7},{4,0},{5,1},{6,2},{7,3},{8,12},{9,13},{10,... | collective-permute-start | bytes 393224 | tf_op jit(solution)/shard_map/ppermute | solution.py:471
  14.3 0.6 %collective-permute-start.4 = (f32[256,128]{1,0:T(8,128)S(1)}, f32[256,128]{1,0:T(8,128)S(1)}, u32[]{:S(2)}, u32[]{:S(2)}) collective-permute-start(f32[256,128]{1,0:T(8,128)S(1)} %get-tuple-element.28.a.dep_ref), channel_id=1, source_target_pairs={{0,3},{1,2},{2,1},{3,0},{4,7},{5,6},{6,5},{7,4},{8,11},{9,10},{10,... | collective-permute-start | bytes 393224 | tf_op jit(solution)/shard_map/ppermute | solution.py:471
  14.9 0.4 collective-permute-start.3
  15.3 2.9 %parts.2 = (bf16[4,1024,256]{2,1,0:T(8,128)(2,1)S(1)}, bf16[4,1024,256]{2,1,0:T(8,128)(2,1)S(1)}, f32[4,1024,128]{2,1,0:T(8,128)S(1)}) custom-call(f32[8,2048,128]{2,1,0:T(8,128)} %bitcast.6, f32[8,1024,128]{2,1,0:T(8,128)} %bitcast.9, f32[256,128]{1,0:T(8,128)S(1)} %get-tuple-element.28.a.dep_ref), custom_call_target="tpu_custom_call" | custom-call | bytes 12582912 | tf_op jit(solution)/shard_map/parts/pallas_call | solution.py:37
  18.2 3.3 %collective-permute-done.4.c.dep1 = f32[256,128]{1,0:T(8,128)S(1)} collective-permute-done((f32[256,128]{1,0:T(8,128)S(1)}, f32[256,128]{1,0:T(8,128)S(1)}, u32[]{:S(2)}, u32[]{:S(2)}) %collective-permute-start.4) | collective-permute-done | bytes 131104 | tf_op jit(solution)/shard_map/ppermute | solution.py:471
  21.5 0.3 collective-permute-done.2.got_ref
  21.9 0.4 collective-permute-start.7
  22.4 0.3 rows.1.inv_ref
  22.7 0.6 %first.1.y_ref = f32[2,128,128]{2,1,0:T(8,128)S(1)} custom-call(f32[2,256,128]{2,1,0:T(8,128)S(1)} %get-tuple-element.26.rhs_ref, f32[256,128]{1,0:T(8,128)S(1)} %get-tuple-element.28.a.dep_ref, f32[256,128]{1,0:T(8,128)S(1)} %collective-permute-done.3.b.dep0, f32[256,128]{1,0:T(8,128)S(1)} %collective-permute-done.4.c.dep1, ...), custom_call_target="tpu_custom_call" | custom-call | tf_op jit(solution)/shard_map/first/pallas_call | solution.py:37
  23.3 0.4 half.1.u_ref
  23.9 0.4 rest.1.dep_ref.a
  24.3 3.0 %collective-permute-start.10 = (f32[256,128]{1,0:T(8,128)S(1)}, f32[256,128]{1,0:T(8,128)S(1)}, u32[]{:S(2)}, u32[]{:S(2)}) collective-permute-start(f32[256,128]{1,0:T(8,128)S(1)} %rest.1.dep_ref.a), channel_id=1, source_target_pairs={{0,4},{1,5},{2,6},{3,7},{4,0},{5,1},{6,2},{7,3},{8,12},{9,13},{10,... | collective-permute-start | bytes 393224 | tf_op jit(solution)/shard_map/ppermute | solution.py:471
  27.3 0.9 %collective-permute-start.9 = (f32[256,128]{1,0:T(8,128)S(1)}, f32[256,128]{1,0:T(8,128)S(1)}, u32[]{:S(2)}, u32[]{:S(2)}) collective-permute-start(f32[256,128]{1,0:T(8,128)S(1)} %rest.1.dep_ref.a), channel_id=1, source_target_pairs={{0,3},{1,2},{2,1},{3,0},{4,7},{5,6},{6,5},{7,4},{8,11},{9,10},{10,... | collective-permute-start | bytes 393224 | tf_op jit(solution)/shard_map/ppermute | solution.py:471
  28.3 0.4 collective-permute-start.8
  28.7 2.9 %parts.3 = (bf16[4,1024,256]{2,1,0:T(8,128)(2,1)S(1)}, bf16[4,1024,256]{2,1,0:T(8,128)(2,1)S(1)}, f32[4,1024,128]{2,1,0:T(8,128)S(1)}) custom-call(f32[8,2048,128]{2,1,0:T(8,128)} %bitcast.7, f32[8,1024,128]{2,1,0:T(8,128)} %bitcast.10, f32[256,128]{1,0:T(8,128)S(1)} %rest.1.dep_ref.a), custom_call_target="tpu_custom_call" | custom-call | bytes 12582912 | tf_op jit(solution)/shard_map/parts/pallas_call | solution.py:37
  31.6 2.7 %collective-permute-done.9.c = f32[256,128]{1,0:T(8,128)S(1)} collective-permute-done((f32[256,128]{1,0:T(8,128)S(1)}, f32[256,128]{1,0:T(8,128)S(1)}, u32[]{:S(2)}, u32[]{:S(2)}) %collective-permute-start.9) | collective-permute-done | bytes 131104 | tf_op jit(solution)/shard_map/ppermute | solution.py:471
  34.4 0.6 %second.1.a = f32[128,128]{1,0:T(8,128)S(1)} custom-call(f32[2,256,128]{2,1,0:T(8,128)S(1)} %get-tuple-element.26.rhs_ref, f32[256,128]{1,0:T(8,128)S(1)} %rest.1.dep_ref.a, f32[256,128]{1,0:T(8,128)S(1)} %collective-permute-done.8.b, f32[256,128]{1,0:T(8,128)S(1)} %collective-permute-done.9.c, f32[256,128]{1,0:T(8,128)S(1)} %collective-permute-done.10.d, ...), custom_call_target="tpu_custom_call" | custom-call | tf_op jit(solution)/shard_map/second/pallas_call | solution.py:37
  35.2 1.7 %collective-permute-start.11 = (f32[128,128]{1,0:T(8,128)S(1)}, f32[128,128]{1,0:T(8,128)S(1)}, u32[]{:S(2)}, u32[]{:S(2)}) collective-permute-start(f32[128,128]{1,0:T(8,128)S(1)} %second.1.a), channel_id=1, source_target_pairs={{0,33},{1,32},{2,35},{3,34},{4,37},{5,36},{6,39},{7,38},{8,41},{9,... | collective-permute-start | bytes 196616 | tf_op jit(solution)/shard_map/ppermute | solution.py:484
  36.9 3.1 %collective-permute-done.13.d = f32[128,128]{1,0:T(8,128)S(1)} collective-permute-done((f32[128,128]{1,0:T(8,128)S(1)}, f32[128,128]{1,0:T(8,128)S(1)}, u32[]{:S(2)}, u32[]{:S(2)}) %collective-permute-start.13) | collective-permute-done | bytes 65568 | tf_op jit(solution)/shard_map/ppermute | solution.py:484
  40.3 3.3 %collective-permute-start.14 = (f32[128,128]{1,0:T(8,128)S(1)}, f32[128,128]{1,0:T(8,128)S(1)}, u32[]{:S(2)}, u32[]{:S(2)}) collective-permute-start(f32[128,128]{1,0:T(8,128)S(1)} %choose.1.a), channel_id=1, source_target_pairs={{0,9},{1,8},{2,11},{3,10},{4,13},{5,12},{6,15},{7,14},{8,25},{9,24... | collective-permute-start | bytes 196616 | tf_op jit(solution)/shard_map/ppermute | solution.py:484
  43.6 0.9 %collective-permute-done.16.d = f32[128,128]{1,0:T(8,128)S(1)} collective-permute-done((f32[128,128]{1,0:T(8,128)S(1)}, f32[128,128]{1,0:T(8,128)S(1)}, u32[]{:S(2)}, u32[]{:S(2)}) %collective-permute-start.16) | collective-permute-done | bytes 65568 | tf_op jit(solution)/shard_map/ppermute | solution.py:484
  44.5 1.5 %collective-permute-done.15.c = f32[128,128]{1,0:T(8,128)S(1)} collective-permute-done((f32[128,128]{1,0:T(8,128)S(1)}, f32[128,128]{1,0:T(8,128)S(1)}, u32[]{:S(2)}, u32[]{:S(2)}) %collective-permute-start.15) | collective-permute-done | bytes 65568 | tf_op jit(solution)/shard_map/ppermute | solution.py:484
  46.0 0.5 collective-permute-done.14.b
  46.8 1.2 %collective-permute-done.17.got_ref = f32[128,128]{1,0:T(8,128)S(1)} collective-permute-done((f32[128,128]{1,0:T(8,128)S(1)}, f32[128,128]{1,0:T(8,128)S(1)}, u32[]{:S(2)}, u32[]{:S(2)}) %collective-permute-start.17) | collective-permute-done | bytes 65568 | tf_op jit(solution)/shard_map/ppermute | solution.py:471
  48.0 3.3 %update.1 = (f32[8,1024,128]{2,1,0:T(8,128)}, f32[2,128,128]{2,1,0:T(8,128)}) custom-call(f32[128,128]{1,0:T(8,128)S(1)} %get-tuple-element.32.keep_ref, f32[128,128]{1,0:T(8,128)S(1)} %collective-permute-done.17.got_ref, bf16[4,1024,256]{2,1,0:T(8,128)(2,1)S(1)} %get-tuple-element.30.dep3.ph0, bf16[4,1024,256]{2,1,0:T(8,128)(2,1)S(1)} %get-tuple-element.34.pl0, ...), custom_call_target="tpu_custom_call" | custom-call | tf_op jit(solution)/shard_map/update/pallas_call | solution.py:37
  (22 shorter events, 1.2 us)
Async XLA Ops:
  2.2 2.9 %collective-permute-start = (f32[2,256,128]{2,1,0:T(8,128)S(1)}, f32[2,256,128]{2,1,0:T(8,128)S(1)}, u32[]{:S(2)}, u32[]{:S(2)}) collective-permute-start(f32[2,256,128]{2,1,0:T(8,128)S(1)} %get-tuple-element.22.dep_ref), channel_id=1, source_target_pairs={{0,1},{1,0},{2,3},{3,2},{4,5},{5,4},{6,7},{7,6},{8,9},{9,8},{10,11... | collective-permute-start | bytes 786440 | tf_op jit(solution)/shard_map/ppermute | solution.py:471
  3.7 1.5 %copy-start = (f32[2,128,1024]{2,1,0:T(8,128)S(1)}, f32[2,128,1024]{2,1,0:T(8,128)}, u32[]{:S(2)}) copy-start(f32[2,128,1024]{2,1,0:T(8,128)} %inv_ref.1) | copy-start | bytes 3145732
  5.1 16.8 %collective-permute-start.2 = (f32[1280,128]{1,0:T(8,128)S(1)}, f32[1280,128]{1,0:T(8,128)S(1)}, u32[]{:S(2)}, u32[]{:S(2)}) collective-permute-start(f32[1280,128]{1,0:T(8,128)S(1)} %get-tuple-element.27.own_ref), channel_id=1, source_target_pairs={{0,33},{1,32},{2,35},{3,34},{4,37},{5,36},{6,39},{7,38},{8,1},{9,0... | collective-permute-start | bytes 1966088 | tf_op jit(solution)/shard_map/ppermute | solution.py:484
  5.2 17.2 %collective-permute-start.6 = (f32[2,128,1024]{2,1,0:T(8,128)S(1)}, f32[2,128,1024]{2,1,0:T(8,128)S(1)}, u32[]{:S(2)}, u32[]{:S(2)}) collective-permute-start(f32[2,128,1024]{2,1,0:T(8,128)S(1)} %copy-done), channel_id=1, source_target_pairs={{0,1},{1,0},{2,3},{3,2},{4,5},{5,4},{6,7},{7,6},{8,9},{9,8},{10,11... | collective-permute-start | bytes 3145736 | tf_op jit(solution)/shard_map/ppermute | solution.py:471
  5.4 5.8 %collective-permute-start.1 = (f32[256,128]{1,0:T(8,128)S(1)}, f32[256,128]{1,0:T(8,128)S(1)}, u32[]{:S(2)}, u32[]{:S(2)}) collective-permute-start(f32[256,128]{1,0:T(8,128)S(1)} %get-tuple-element.24), channel_id=1, source_target_pairs={{0,9},{1,8},{2,11},{3,10},{4,13},{5,12},{6,15},{7,14},{8,41},{9,40... | collective-permute-start | bytes 393224 | tf_op jit(solution)/shard_map/ppermute | solution.py:484
  11.2 7.0 %collective-permute-start.5 = (f32[256,128]{1,0:T(8,128)S(1)}, f32[256,128]{1,0:T(8,128)S(1)}, u32[]{:S(2)}, u32[]{:S(2)}) collective-permute-start(f32[256,128]{1,0:T(8,128)S(1)} %get-tuple-element.28.a.dep_ref), channel_id=1, source_target_pairs={{0,4},{1,5},{2,6},{3,7},{4,0},{5,1},{6,2},{7,3},{8,12},{9,13},{10,... | collective-permute-start | bytes 393224 | tf_op jit(solution)/shard_map/ppermute | solution.py:471
  14.3 7.3 %collective-permute-start.4 = (f32[256,128]{1,0:T(8,128)S(1)}, f32[256,128]{1,0:T(8,128)S(1)}, u32[]{:S(2)}, u32[]{:S(2)}) collective-permute-start(f32[256,128]{1,0:T(8,128)S(1)} %get-tuple-element.28.a.dep_ref), channel_id=1, source_target_pairs={{0,3},{1,2},{2,1},{3,0},{4,7},{5,6},{6,5},{7,4},{8,11},{9,10},{10,... | collective-permute-start | bytes 393224 | tf_op jit(solution)/shard_map/ppermute | solution.py:471
  14.9 6.6 %collective-permute-start.3 = (f32[256,128]{1,0:T(8,128)S(1)}, f32[256,128]{1,0:T(8,128)S(1)}, u32[]{:S(2)}, u32[]{:S(2)}) collective-permute-start(f32[256,128]{1,0:T(8,128)S(1)} %get-tuple-element.28.a.dep_ref), channel_id=1, source_target_pairs={{0,7},{1,6},{2,5},{3,4},{4,3},{5,2},{6,1},{7,0},{8,15},{9,14},{10,... | collective-permute-start | bytes 393224 | tf_op jit(solution)/shard_map/ppermute | solution.py:471
  21.9 2.0 %collective-permute-start.7 = (f32[1024,128]{1,0:T(8,128)S(1)}, f32[1024,128]{1,0:T(8,128)S(1)}, u32[]{:S(2)}, u32[]{:S(2)}) collective-permute-start(f32[1024,128]{1,0:T(8,128)S(1)} %odd.1.tile_ref), channel_id=1, source_target_pairs={{0,1},{1,0},{2,3},{3,2},{4,5},{5,4},{6,7},{7,6},{8,9},{9,8},{10,11... | collective-permute-start | bytes 1572872 | tf_op jit(solution)/shard_map/ppermute | solution.py:471
  24.3 7.2 %collective-permute-start.10 = (f32[256,128]{1,0:T(8,128)S(1)}, f32[256,128]{1,0:T(8,128)S(1)}, u32[]{:S(2)}, u32[]{:S(2)}) collective-permute-start(f32[256,128]{1,0:T(8,128)S(1)} %rest.1.dep_ref.a), channel_id=1, source_target_pairs={{0,4},{1,5},{2,6},{3,7},{4,0},{5,1},{6,2},{7,3},{8,12},{9,13},{10,... | collective-permute-start | bytes 393224 | tf_op jit(solution)/shard_map/ppermute | solution.py:471
  27.3 6.9 %collective-permute-start.9 = (f32[256,128]{1,0:T(8,128)S(1)}, f32[256,128]{1,0:T(8,128)S(1)}, u32[]{:S(2)}, u32[]{:S(2)}) collective-permute-start(f32[256,128]{1,0:T(8,128)S(1)} %rest.1.dep_ref.a), channel_id=1, source_target_pairs={{0,3},{1,2},{2,1},{3,0},{4,7},{5,6},{6,5},{7,4},{8,11},{9,10},{10,... | collective-permute-start | bytes 393224 | tf_op jit(solution)/shard_map/ppermute | solution.py:471
  28.3 6.2 %collective-permute-start.8 = (f32[256,128]{1,0:T(8,128)S(1)}, f32[256,128]{1,0:T(8,128)S(1)}, u32[]{:S(2)}, u32[]{:S(2)}) collective-permute-start(f32[256,128]{1,0:T(8,128)S(1)} %rest.1.dep_ref.a), channel_id=1, source_target_pairs={{0,7},{1,6},{2,5},{3,4},{4,3},{5,2},{6,1},{7,0},{8,15},{9,14},{10,... | collective-permute-start | bytes 393224 | tf_op jit(solution)/shard_map/ppermute | solution.py:471
  35.0 5.0 %collective-permute-start.13 = (f32[128,128]{1,0:T(8,128)S(1)}, f32[128,128]{1,0:T(8,128)S(1)}, u32[]{:S(2)}, u32[]{:S(2)}) collective-permute-start(f32[128,128]{1,0:T(8,128)S(1)} %second.1.a), channel_id=1, source_target_pairs={{0,97},{1,96},{2,99},{3,98},{4,101},{5,100},{6,103},{7,102},{8,105... | collective-permute-start | bytes 196616 | tf_op jit(solution)/shard_map/ppermute | solution.py:484
  35.1 4.9 %collective-permute-start.12 = (f32[128,128]{1,0:T(8,128)S(1)}, f32[128,128]{1,0:T(8,128)S(1)}, u32[]{:S(2)}, u32[]{:S(2)}) collective-permute-start(f32[128,128]{1,0:T(8,128)S(1)} %second.1.a), channel_id=1, source_target_pairs={{0,65},{1,64},{2,67},{3,66},{4,69},{5,68},{6,71},{7,70},{8,73},{9,... | collective-permute-start | bytes 196616 | tf_op jit(solution)/shard_map/ppermute | solution.py:484
  35.2 5.0 %collective-permute-start.11 = (f32[128,128]{1,0:T(8,128)S(1)}, f32[128,128]{1,0:T(8,128)S(1)}, u32[]{:S(2)}, u32[]{:S(2)}) collective-permute-start(f32[128,128]{1,0:T(8,128)S(1)} %second.1.a), channel_id=1, source_target_pairs={{0,33},{1,32},{2,35},{3,34},{4,37},{5,36},{6,39},{7,38},{8,41},{9,... | collective-permute-start | bytes 196616 | tf_op jit(solution)/shard_map/ppermute | solution.py:484
  40.2 4.3 %collective-permute-start.16 = (f32[128,128]{1,0:T(8,128)S(1)}, f32[128,128]{1,0:T(8,128)S(1)}, u32[]{:S(2)}, u32[]{:S(2)}) collective-permute-start(f32[128,128]{1,0:T(8,128)S(1)} %choose.1.a), channel_id=1, source_target_pairs={{0,17},{1,16},{2,19},{3,18},{4,21},{5,20},{6,23},{7,22},{8,1},{9,0... | collective-permute-start | bytes 196616 | tf_op jit(solution)/shard_map/ppermute | solution.py:484
  40.2 5.8 %collective-permute-start.15 = (f32[128,128]{1,0:T(8,128)S(1)}, f32[128,128]{1,0:T(8,128)S(1)}, u32[]{:S(2)}, u32[]{:S(2)}) collective-permute-start(f32[128,128]{1,0:T(8,128)S(1)} %choose.1.a), channel_id=1, source_target_pairs={{0,25},{1,24},{2,27},{3,26},{4,29},{5,28},{6,31},{7,30},{8,17},{9,... | collective-permute-start | bytes 196616 | tf_op jit(solution)/shard_map/ppermute | solution.py:484
  40.3 6.2 %collective-permute-start.14 = (f32[128,128]{1,0:T(8,128)S(1)}, f32[128,128]{1,0:T(8,128)S(1)}, u32[]{:S(2)}, u32[]{:S(2)}) collective-permute-start(f32[128,128]{1,0:T(8,128)S(1)} %choose.1.a), channel_id=1, source_target_pairs={{0,9},{1,8},{2,11},{3,10},{4,13},{5,12},{6,15},{7,14},{8,25},{9,24... | collective-permute-start | bytes 196616 | tf_op jit(solution)/shard_map/ppermute | solution.py:484
  46.7 1.3 %collective-permute-start.17 = (f32[128,128]{1,0:T(8,128)S(1)}, f32[128,128]{1,0:T(8,128)S(1)}, u32[]{:S(2)}, u32[]{:S(2)}) collective-permute-start(f32[128,128]{1,0:T(8,128)S(1)} %get-tuple-element.33), channel_id=1, source_target_pairs={{0,1},{1,0},{2,3},{3,2},{4,5},{5,4},{6,7},{7,6},{8,9},{9,8},{10,11... | collective-permute-start | bytes 196616 | tf_op jit(solution)/shard_map/ppermute | solution.py:471
